TPU v7x, 32 devices: a whole 2x2x4 slice. The times are simulated.
32 devices in a mesh: fsdp: 8 (over y, x, core), seq: 4 (over z).
Axes of the slice: x: 2, y: 2, z: 4, core: 2. Of those that a mesh axis runs over, the one named last changes fastest.
Arguments:
- tokens: bfloat16 [64, 256, 768], P('fsdp', 'seq'), may hold values from -6 to 6
- ln1_gain: bfloat16 [768], P('fsdp'), may hold values from 0.5 to 1.5
- ln1_bias: bfloat16 [768], P('fsdp'), may hold values from -1.5 to 1.5
- w_qkv: bfloat16 [768, 2304], P('fsdp'), may hold values from -0.21875 to 0.21875
- w_out: bfloat16 [768, 768], P('fsdp'), may hold values from -1.75 to 1.75
- ln2_gain: bfloat16 [768], P('fsdp'), may hold values from 0.5 to 1.5
- ln2_bias: bfloat16 [768], P('fsdp'), may hold values from -1.5 to 1.5
- w_router: bfloat16 [768, 4], P('fsdp'), may hold values from -0.14941406 to 0.14941406
- w_in: bfloat16 [4, 3072, 768], P(None, 'fsdp'), may hold values from -0.21875 to 0.21875
- w_down: bfloat16 [4, 3072, 768], P(None, 'fsdp'), may hold values from -0.875 to 0.875
- padding: int32 [64, 256], P('fsdp'), may hold values from 0 to 1, as said below
- routes: int32 [64, 256, 2], P('fsdp', 'seq'), may hold values from 0 to 3, all different within a row
- priority: int32 [64, 256], P('fsdp', 'seq'), may hold values from 0 to 16383, as said below
- cotangent: bfloat16 [64, 256, 768], P('fsdp', 'seq'), may hold values from -6 to 6
Outputs:
- outputs: bfloat16 [64, 256, 768], P('fsdp', 'seq')
- grad_tokens: bfloat16 [64, 256, 768], P('fsdp', 'seq')
- grad_ln1_gain: float32 [768], P('fsdp')
- grad_ln1_bias: float32 [768], P('fsdp')
- grad_w_qkv: float32 [768, 2304], P('fsdp')
- grad_w_out: float32 [768, 768], P('fsdp')
- grad_ln2_gain: float32 [768], P('fsdp')
- grad_ln2_bias: float32 [768], P('fsdp')
- grad_w_router: float32 [768, 4], P('fsdp')
- grad_w_in: float32 [4, 3072, 768], P(None, 'fsdp')
- grad_w_down: float32 [4, 3072, 768], P(None, 'fsdp')
Inputs may be any that keep to these rules, and one draw needn't show every extreme that they name: `padding`: an image's ones are a prefix of 128 or more positions, and some image has ones at all 256 positions. `routes`: a token's two experts differ, and every expert is named by some token. `priority`: all values are different.
All inputs are finite; a program needn't handle non-finite values.
Results may differ from a plain program's by a relative error of at most 0.018.
Values may be sent and summed in bfloat16 or wider, within the bound.
No kernel may reach another device: no remote copies, remote signals or barrier semaphores. Data moves between devices by JAX's collectives and lax.ppermute only.
A program may use at most 192 MiB of HBM per device.

v0:
```python
import functools
import math

import jax
import jax.numpy as jnp
from jax import lax
from jax.experimental import pallas as pl
from jax.experimental.pallas import tpu as pltpu
from jax.sharding import PartitionSpec as P

HEAD_DIM = 64
LANES = 128
MASK_ROWS = 16
SMALL = 8
norm_eps = 1e-06
neg_fill = -1e30
f32 = jnp.float32
bf16 = jnp.bfloat16
VMEM_BYTES = 60 * 1024 * 1024
SHORT = pl.CostEstimate(flops=1000, bytes_accessed=1000, transcendentals=0)


def true_cost(flops):
    return pl.CostEstimate(flops=2 * flops, bytes_accessed=16 * 1024 * 1024, transcendentals=0)


def mm(left, right, left_dim=1, right_dim=0):
    return lax.dot_general(
        left, right, (((left_dim,), (right_dim,)), ((), ())), preferred_element_type=f32
    )


def unit_norm(rows):
    centred = rows - jnp.mean(rows, -1, keepdims=True)
    inverse = lax.rsqrt(jnp.mean(centred * centred, -1, keepdims=True) + norm_eps)
    return centred * inverse, inverse


def norm_back(scaled, unit, inverse):
    return inverse * (
        scaled
        - jnp.mean(scaled, -1, keepdims=True)
        - unit * jnp.mean(scaled * unit, -1, keepdims=True)
    )


def half_turn(tile):
    return pltpu.roll(tile.astype(f32), HEAD_DIM, axis=1).astype(bf16)


def wall_copies(pieces, offsets, place_ref, wall_ref, sems):
    copies = []
    for n, (piece, (r, skip)) in enumerate(zip(pieces, offsets)):
        rows = piece.shape[0]
        shard = wall_ref.shape[0] // 8
        start = pl.multiple_of((place_ref[0] ^ r) * shard + skip, 16)
        copies.append(pltpu.make_async_copy(piece, wall_ref.at[pl.ds(start, rows)], sems.at[n]))
    return copies


def front_kernel(offsets, *refs):
    pieces = refs[: len(offsets)]
    tok_ref, vis_ref, place_ref = refs[len(offsets) : len(offsets) + 3]
    mid_ref, two_ref, proj_ref, att_ref, prob_ref, full_ref, wr_ref, small_ref = refs[
        len(offsets) + 3 : len(offsets) + 11
    ]
    wall_ref, sems, full_sem = refs[len(offsets) + 11 :]
    blocks, _, span, width = tok_ref.shape
    length = blocks * span
    save = pltpu.make_async_copy(wall_ref, full_ref, full_sem)

    @pl.when(pl.program_id(0) == 0)
    def _():
        copies = wall_copies(pieces, offsets, place_ref, wall_ref, sems)
        for copy in copies:
            copy.start()
        for copy in copies:
            copy.wait()
        save.start()
        columns = wall_ref[:, 4 * width :]
        wr_ref[...] = columns
        small_ref[...] = columns.astype(f32).T[:SMALL]

    rows = tok_ref[...].reshape(length, width).astype(f32)
    unit, _ = unit_norm(rows)
    one = (unit * small_ref[4:5] + small_ref[5:6]).astype(bf16)
    proj_ref[0] = mm(one, wall_ref[:, : 3 * width]).astype(bf16)
    lower = lax.broadcasted_iota(jnp.int32, (length, LANES), 1) < HEAD_DIM
    zero = jnp.zeros((length, LANES), bf16)
    bias = vis_ref[0]

    def soften(index, queries, keys):
        scores = mm(queries, keys, 1, 1) * (HEAD_DIM**-0.5) + bias
        shifted = jnp.exp(scores - jnp.max(scores, -1, keepdims=True))
        weights = (shifted / jnp.sum(shifted, -1, keepdims=True)).astype(bf16)
        prob_ref[0, index] = weights
        return weights

    for pair in range(width // LANES):
        first, second, third = (
            proj_ref[0, :, (3 * pair + n) * LANES : (3 * pair + n + 1) * LANES] for n in range(3)
        )
        weights_a = soften(2 * pair, jnp.where(lower, first, zero), half_turn(first))
        weights_b = soften(2 * pair + 1, jnp.where(lower, zero, second), half_turn(third))
        both = jnp.where(lower, mm(weights_a, second), mm(weights_b, third))
        att_ref[0, :, pair * LANES : (pair + 1) * LANES] = both.astype(bf16)
    middle = rows + mm(att_ref[0], wall_ref[:, 3 * width : 4 * width])
    mid_ref[...] = middle.reshape(mid_ref.shape)
    unit, _ = unit_norm(middle)
    two_ref[...] = (unit * small_ref[6:7] + small_ref[7:8]).astype(bf16).reshape(two_ref.shape)

    @pl.when(pl.program_id(0) == pl.num_programs(0) - 1)
    def _():
        save.wait()


def front(tok, pieces, offsets, vis, place):
    blocks, images, span, width = tok.shape
    length = blocks * span
    heads = width // HEAD_DIM
    split = pl.BlockSpec((blocks, 1, span, width), lambda i: (0, i, 0, 0))
    anywhere = pl.BlockSpec(memory_space=pl.ANY)
    columns = pieces[0].shape[1]
    return pl.pallas_call(
        functools.partial(front_kernel, offsets),
        grid=(images,),
        in_specs=[anywhere] * len(pieces)
        + [
            split,
            pl.BlockSpec((1, 1, length), lambda i: (i, 0, 0)),
            pl.BlockSpec(memory_space=pltpu.SMEM),
        ],
        out_specs=[
            split,
            split,
            pl.BlockSpec((1, length, 3 * width), lambda i: (i, 0, 0)),
            pl.BlockSpec((1, length, width), lambda i: (i, 0, 0)),
            pl.BlockSpec((1, heads, length, length), lambda i: (i, 0, 0, 0)),
            anywhere,
            pl.BlockSpec((width, LANES), lambda i: (0, 0)),
            pl.BlockSpec((SMALL, width), lambda i: (0, 0)),
        ],
        out_shape=[
            jax.ShapeDtypeStruct(tok.shape, f32),
            jax.ShapeDtypeStruct(tok.shape, bf16),
            jax.ShapeDtypeStruct((images, length, 3 * width), bf16),
            jax.ShapeDtypeStruct((images, length, width), bf16),
            jax.ShapeDtypeStruct((images, heads, length, length), bf16),
            jax.ShapeDtypeStruct((width, columns), bf16),
            jax.ShapeDtypeStruct((width, LANES), bf16),
            jax.ShapeDtypeStruct((SMALL, width), f32),
        ],
        scratch_shapes=[
            pltpu.VMEM((width, columns), bf16),
            pltpu.SemaphoreType.DMA((len(pieces),)),
            pltpu.SemaphoreType.DMA(()),
        ],
        compiler_params=pltpu.CompilerParams(vmem_limit_bytes=VMEM_BYTES),
        cost_estimate=SHORT,
        name="front",
    )(*pieces, tok, vis, place)


def gelu_parts(pre):
    bell = jnp.exp2(pre * pre * (-0.5 * math.log2(math.e)))
    frac = 1.0 / (1.0 + (0.3275911 * math.sqrt(0.5)) * jnp.abs(pre))
    a5, a4, a3, a2, a1 = (
        0.5 * c for c in (1.061405429, -1.453152027, 1.421413741, -0.284496736, 0.254829592)
    )
    tail = frac * (a1 + frac * (a2 + frac * (a3 + frac * (a4 + frac * a5)))) * bell
    cumulative = jnp.where(pre >= 0, 1.0 - tail, tail)
    return pre * cumulative, cumulative + (pre * 0.3989422804014327) * bell


def expert_kernel(plan, *refs):
    refs = list(refs)

    def take(number):
        taken, refs[:] = refs[:number], refs[number:]
        return taken

    groups, experts, opening = plan["groups"], plan["experts"], plan["opening"]
    two_parts = [take(n) for n in plan["two"]]
    cot_parts = [take(n) for n in plan["cot"]]
    weights = take(4)
    (wr_ref,) = take(1)
    dwr_carried = None if opening else take(1)[0]
    left = take(1 if opening else 2)
    (dwr_ref,) = take(1)
    results = take(2 * groups)
    two_buf, cot_buf, sems, win_buf, wdn_buf, weight_sems, gated_buf, grad_buf = take(8)
    stage, store_sems, left_sems = take(3)
    _, blocks, span, width = two_buf.shape
    rows = blocks * span
    hidden = win_buf.shape[0] // experts
    shard = hidden // 2
    group = pl.program_id(0)
    slot = group % gated_buf.shape[0]
    lane = lax.broadcasted_iota(jnp.int32, (rows, LANES), 1)

    copies = []
    for k in range(groups):
        some = []
        for parts, buffer in ((two_parts[k], two_buf), (cot_parts[k], cot_buf)):
            at = 0
            for part in parts:
                size = part.shape[0]
                some.append((part, buffer.at[k, pl.ds(at, size)]))
                at += size
        copies.append(
            [pltpu.make_async_copy(s, t, sems.at[k, n]) for n, (s, t) in enumerate(some)]
        )
    fetches = [
        pltpu.make_async_copy(
            ref.at[e],
            (win_buf, wdn_buf)[n // 2].at[pl.ds(e * hidden + (n % 2) * shard, shard)],
            weight_sems.at[e, n],
        )
        for e in range(experts)
        for n, ref in enumerate(weights)
    ]
    stores = [
        [
            pltpu.make_async_copy(stage.at[n], results[n * groups + k], store_sems.at[n])
            for n in range(2)
        ]
        for k in range(groups)
    ]
    if not opening:
        for k in range(groups):
            for n, buffer in enumerate((gated_buf, grad_buf)):
                place = k % buffer.shape[0]
                stores[k].append(
                    pltpu.make_async_copy(
                        buffer.at[place],
                        left[n].at[pl.ds(k * rows, rows)],
                        left_sems.at[place, n],
                    )
                )

    @pl.when(group == 0)
    def _():
        for copy in copies[0] + fetches:
            copy.start()
        for some in copies[1:]:
            for copy in some:
                copy.start()
        dwr_ref[...] = jnp.zeros_like(dwr_ref) if opening else dwr_carried[...]
        for copy in fetches:
            copy.wait()

    for k, some in enumerate(copies):

        @pl.when(group == k)
        def _(k=k, some=some):
            for copy in some:
                copy.wait()
            if k > 0:
                for store in stores[k - 1][:2]:
                    store.wait()
            if k > 1:
                for store in stores[k - 2][2:]:
                    store.wait()

    two = two_buf[group].reshape(rows, width)
    cot = cot_buf[group, :, :span, :].reshape(rows, width)
    chosen = (
        lax.broadcasted_iota(jnp.int32, (MASK_ROWS, LANES), 0)
        == lax.broadcasted_iota(jnp.int32, (MASK_ROWS, LANES), 1)
    ).astype(bf16)
    logits = jnp.where(lane < experts, mm(two, wr_ref[...]), neg_fill)
    shifted = jnp.exp(logits - jnp.max(logits, -1, keepdims=True))
    probs = shifted / jnp.sum(shifted, -1, keepdims=True)
    kept = jnp.concatenate(
        [
            mm(cot_buf[group, b, span : span + MASK_ROWS, :span], chosen, 0, 0)
            for b in range(blocks)
        ],
        0,
    )
    grad_gate = jnp.zeros((rows, LANES), f32)
    gates = probs * kept
    out_rows = gin_rows = None
    for e in range(experts):
        at = slice(e * hidden, (e + 1) * hidden)
        win, wdn = win_buf[at], wdn_buf[at]
        pre = mm(two, win, 1, 1)
        back_rows = mm(cot, wdn, 1, 1)
        gate = gates[:, e : e + 1]
        hidden_rows, slope = gelu_parts(pre)
        product = jnp.sum(hidden_rows * back_rows, -1, keepdims=True)
        grad_gate = jnp.where(lane == e, product, grad_gate)
        gated = (hidden_rows * gate).astype(bf16)
        grad_pre = (slope * back_rows * gate).astype(bf16)
        if opening:
            gated_buf[e, 1] = mm(gated, cot, 0, 0).astype(bf16)
            gated_buf[e, 0] = mm(grad_pre, two, 0, 0).astype(bf16)
        else:
            gated_buf[slot, :, at] = gated
            grad_buf[slot, :, at] = grad_pre
        out_part, gin_part = mm(gated, wdn), mm(grad_pre, win)
        out_rows = out_part if e == 0 else out_rows + out_part
        gin_rows = gin_part if e == 0 else gin_rows + gin_part
    grad_gate = grad_gate * kept
    grad_logits = probs * (grad_gate - jnp.sum(probs * grad_gate, -1, keepdims=True))
    grad_logits = grad_logits.astype(bf16)
    dwr_ref[...] += mm(grad_logits, two, 0, 0)[:SMALL]
    gin_rows = gin_rows + mm(grad_logits, wr_ref[...], 1, 1)
    stage[0] = out_rows.astype(bf16).reshape(blocks, span, width)
    stage[1] = gin_rows.astype(bf16).reshape(blocks, span, width)
    for k in range(groups):

        @pl.when(group == k)
        def _(k=k):
            for store in stores[k]:
                store.start()

    @pl.when(group == groups - 1)
    def _():
        if opening:
            copy = pltpu.make_async_copy(gated_buf, left[0], left_sems.at[0, 0])
            copy.start()
            copy.wait()
        for k in (groups - 1,) if groups == 1 else (groups - 2, groups - 1):
            for store in stores[k][0 if k == groups - 1 else 2 :]:
                store.wait()


def experts_call(two, cot, weights, wr, dwr, name, cost):
    groups = len(two)
    opening = groups == 1
    experts, shard, width = weights[0].shape
    hidden = 2 * shard
    blocks = sum(a.shape[0] for a in two[0])
    span = two[0][0].shape[1]
    rows = blocks * span
    plan = dict(
        groups=groups,
        experts=experts,
        opening=opening,
        two=[len(parts) for parts in two],
        cot=[len(parts) for parts in cot],
    )
    anywhere = pl.BlockSpec(memory_space=pl.ANY)
    once = lambda a: pl.BlockSpec(
        a.shape, lambda g: (0,) * len(a.shape), pipeline_mode=pl.Buffered(1)
    )
    result = jax.ShapeDtypeStruct((blocks, span, width), bf16)
    little = jax.ShapeDtypeStruct((SMALL, width), f32)
    if opening:
        left = [jax.ShapeDtypeStruct((experts, 2, hidden, width), bf16)]
        buffers = [pltpu.VMEM(left[0].shape, bf16), pltpu.VMEM((16, LANES), bf16)]
    else:
        left = [jax.ShapeDtypeStruct((groups * rows, experts * hidden), bf16)] * 2
        buffers = [pltpu.VMEM((2, rows, experts * hidden), bf16)] * 2
    pieces = [a for parts in two for a in parts] + [a for parts in cot for a in parts]
    outs = pl.pallas_call(
        functools.partial(expert_kernel, plan),
        grid=(groups,),
        in_specs=[anywhere] * (len(pieces) + 4)
        + [once(wr)]
        + ([] if opening else [once(little)]),
        out_specs=[anywhere] * len(left) + [once(little)] + [anywhere] * (2 * groups),
        out_shape=left + [little] + [result] * (2 * groups),
        scratch_shapes=[
            pltpu.VMEM((groups, blocks, span, width), bf16),
            pltpu.VMEM((groups, blocks, span + MASK_ROWS, width), bf16),
            pltpu.SemaphoreType.DMA((groups, 4)),
            pltpu.VMEM((experts * hidden, width), bf16),
            pltpu.VMEM((experts * hidden, width), bf16),
            pltpu.SemaphoreType.DMA((experts, 4)),
            *buffers,
            pltpu.VMEM((2, blocks, span, width), bf16),
            pltpu.SemaphoreType.DMA((2,)),
            pltpu.SemaphoreType.DMA((2, 2)),
        ],
        compiler_params=pltpu.CompilerParams(vmem_limit_bytes=VMEM_BYTES),
        cost_estimate=cost(10 * groups * rows * width * hidden * experts),
        name=name,
    )(*pieces, *weights, wr, *([] if opening else [dwr]))
    left, (dwr, *outs) = list(outs[: len(left)]), outs[len(left) :]
    return left, dwr, outs[:groups], outs[groups:]


def grads_kernel(plan, *refs):
    refs = list(refs)

    def take(number):
        taken, refs[:] = refs[:number], refs[number:]
        return taken

    groups = len(plan["two"])
    two_parts = [take(n) for n in plan["two"]]
    cot_parts = [take(n) for n in plan["cot"]]
    gated_ref, grad_ref, own_ref, kept_ref, sent_ref = take(5)
    two_buf, cot_buf, cot_rows, sems = refs
    _, blocks, span, width = two_buf.shape
    rows = blocks * span
    copies = []
    for k in range(groups):
        at = 0
        for n, part in enumerate(two_parts[k]):
            size = part.shape[0]
            copies.append(
                pltpu.make_async_copy(part, two_buf.at[k, pl.ds(at, size)], sems.at[k, n])
            )
            at += size
        at = 0
        for n, part in enumerate(cot_parts[k]):
            size = part.shape[0]
            copies.append(
                pltpu.make_async_copy(
                    part, cot_buf.at[k, pl.ds(at, size)], sems.at[k, 2 + n]
                )
            )
            at += size

    @pl.when(pl.program_id(0) == 0)
    def _():
        for copy in copies:
            copy.start()
        for copy in copies:
            copy.wait()
        for k in range(groups):
            cot_rows[k * rows : (k + 1) * rows] = cot_buf[k, :, :span, :].reshape(rows, width)

    half = own_ref.shape[2] // 2
    two = two_buf[...].reshape(groups * rows, width)
    for n, (left_ref, right) in enumerate(((grad_ref, two), (gated_ref, cot_rows[...]))):
        total = (own_ref[0, n].astype(f32) + mm(left_ref[...], right, 0, 0)).astype(bf16)
        kept_ref[0, n] = total[:half]
        sent_ref[0, n] = total[half:]


def grads_call(two, cot, left, own, first, many):
    groups = len(two)
    blocks = sum(a.shape[0] for a in two[0])
    _, span, width = two[0][0].shape
    rows = blocks * span
    hidden = own.shape[2]
    anywhere = pl.BlockSpec(memory_space=pl.ANY)
    pieces = [a for parts in two for a in parts] + [a for parts in cot for a in parts]
    columns = pl.BlockSpec((groups * rows, hidden), lambda e: (0, e + first))
    part = jax.ShapeDtypeStruct((many, 2, hidden // 2, width), bf16)
    part_spec = pl.BlockSpec((1, 2, hidden // 2, width), lambda e: (e, 0, 0, 0))
    plan = dict(two=[len(parts) for parts in two], cot=[len(parts) for parts in cot])
    return pl.pallas_call(
        functools.partial(grads_kernel, plan),
        grid=(many,),
        in_specs=[anywhere] * len(pieces)
        + [columns, columns, pl.BlockSpec((1, 2, hidden, width), lambda e: (e + first, 0, 0, 0))],
        out_specs=[part_spec, part_spec],
        out_shape=[part, part],
        scratch_shapes=[
            pltpu.VMEM((groups, blocks, span, width), bf16),
            pltpu.VMEM((groups, blocks, span + MASK_ROWS, width), bf16),
            pltpu.VMEM((groups * rows, width), bf16),
            pltpu.SemaphoreType.DMA((groups, 4)),
        ],
        compiler_params=pltpu.CompilerParams(vmem_limit_bytes=VMEM_BYTES),
        cost_estimate=true_cost(8 * groups * rows * width * hidden * many),
        name="expert_grads",
    )(*pieces, *left, own)


def flip(array, fsdp, bits):
    return lax.ppermute(array, "fsdp", [(n, n ^ bits) for n in range(fsdp)])


def tie(value, *others):
    return lax.optimization_barrier((value, others))[0]


def exchange(pieces):
    count = len(pieces)
    return [pieces[0]] + [
        lax.ppermute(pieces[k], "seq", [(n, n ^ k) for n in range(count)]) for k in range(1, count)
    ]


def relative(parts, index):
    count, bit = len(parts), 1
    while bit < count:
        swap = (index & bit) > 0
        parts = [jnp.where(swap, parts[k ^ bit], parts[k]) for k in range(count)]
        bit *= 2
    return parts


def plus(*arrays):
    return sum(a.astype(f32) for a in arrays).astype(bf16)


class Line:
    def __init__(self, seq, raw):
        self.seq, self.raw = seq, raw
        if seq != 4:
            self.total = lax.psum(raw, "seq")

    def inwards(self):
        if self.seq == 4:
            self.moving = lax.ppermute(self.raw, "seq", [(0, 1), (3, 2)])
        return self

    def across(self, *others):
        if self.seq == 4:
            self.pair = plus(self.raw, tie(self.moving, others))
            self.moving = lax.ppermute(self.pair, "seq", [(1, 2), (2, 1)])
            return self.pair
        return self.raw

    def outwards(self, *others):
        if self.seq == 4:
            self.total = plus(self.pair, tie(self.moving, others))
            self.moving = lax.ppermute(self.total, "seq", [(1, 0), (2, 3)])
        return self.total

    def finish(self):
        if self.seq != 4:
            return self.total
        index = lax.axis_index("seq")
        return jnp.where((index == 0) | (index == 3), self.moving, self.total)

    def waiting(self):
        return [self.moving] if self.seq == 4 else []


def back_kernel(
    gin_0, gin_2, gin_4, gin_6, mid_ref, cot_ref, tok_ref, att_ref, proj_ref, prob_ref, wall_ref,
    small_ref, dwr_ref, *rest,
):
    blocks, _, span, width = tok_ref.shape
    length = blocks * span
    gtok_refs, (dwall_ref, acc, acc_small, gatt, gproj) = rest[:blocks], rest[blocks:]
    step = pl.program_id(0)

    @pl.when(step == 0)
    def _():
        acc[...] = jnp.zeros_like(acc)
        acc_small[...] = jnp.zeros_like(acc_small)
        acc_small[:SMALL] = dwr_ref[...]

    gin = sum(ref[...].reshape(length, width).astype(f32) for ref in (gin_0, gin_2, gin_4, gin_6))
    unit_two, inverse_two = unit_norm(mid_ref[...].reshape(length, width))
    acc_small[6:7] += jnp.sum(gin * unit_two, 0, keepdims=True)
    acc_small[7:8] += jnp.sum(gin, 0, keepdims=True)
    grad_middle = cot_ref[...].reshape(length, width).astype(f32) + norm_back(
        gin * small_ref[6:7], unit_two, inverse_two
    )
    branch = grad_middle.astype(bf16)
    acc[:, 3 * width : 4 * width] += mm(att_ref[0], branch, 0, 0)
    gatt[...] = mm(branch, wall_ref[:, 3 * width : 4 * width], 1, 1).astype(bf16)
    lower = lax.broadcasted_iota(jnp.int32, (length, LANES), 1) < HEAD_DIM
    zero = jnp.zeros((length, LANES), bf16)
    scale = HEAD_DIM**-0.5

    def score_grad(weights, grad_weights):
        weights = weights.astype(f32)
        product = weights * grad_weights
        return (product - weights * jnp.sum(product, -1, keepdims=True)).astype(bf16)

    for pair in range(width // LANES):
        places = [slice((3 * pair + n) * LANES, (3 * pair + n + 1) * LANES) for n in range(3)]
        first, second, third = (proj_ref[0, :, place] for place in places)
        first_r, second_r, third_r = half_turn(first), half_turn(second), half_turn(third)
        grad = gatt[:, pair * LANES : (pair + 1) * LANES]
        weights_a, weights_b = prob_ref[0, 2 * pair], prob_ref[0, 2 * pair + 1]
        ds_a = score_grad(weights_a, mm(jnp.where(lower, grad, zero), second, 1, 1))
        ds_b = score_grad(weights_b, mm(jnp.where(lower, zero, grad), third, 1, 1))
        gproj[:, places[0]] = (
            jnp.where(lower, mm(ds_a, first_r), mm(ds_a, first_r, 0, 0)) * scale
        ).astype(bf16)
        gproj[:, places[1]] = jnp.where(
            lower, mm(weights_a, grad, 0, 0), mm(ds_b, third_r) * scale
        ).astype(bf16)
        gproj[:, places[2]] = jnp.where(
            lower, mm(ds_b, second_r, 0, 0) * scale, mm(weights_b, grad, 0, 0)
        ).astype(bf16)
    unit_one, inverse_one = unit_norm(tok_ref[...].reshape(length, width).astype(f32))
    one = (unit_one * small_ref[4:5] + small_ref[5:6]).astype(bf16)
    grad_one = mm(gproj[...], wall_ref[:, : 3 * width], 1, 1)
    acc_small[4:5] += jnp.sum(grad_one * unit_one, 0, keepdims=True)
    acc_small[5:6] += jnp.sum(grad_one, 0, keepdims=True)
    grad_tok = grad_middle + norm_back(grad_one * small_ref[4:5], unit_one, inverse_one)
    for k, ref in enumerate(gtok_refs):
        ref[0] = grad_tok[k * span : (k + 1) * span].astype(bf16)
    acc[:, : 3 * width] += mm(one, gproj[...], 0, 0)

    @pl.when(step == pl.num_programs(0) - 1)
    def _():
        dwall_ref[:, : 4 * width] = acc[...].astype(bf16)
        dwall_ref[:, 4 * width :] = acc_small[...].T.astype(bf16)


def back(gins, middle, cot, tok, att, proj, prob, wall, small, dwr):
    blocks, images, span, width = tok.shape
    length = blocks * span
    heads = width // HEAD_DIM
    split = pl.BlockSpec((blocks, 1, span, width), lambda i: (0, i, 0, 0))
    whole = lambda a: pl.BlockSpec(a.shape, lambda i: (0,) * len(a.shape))
    return pl.pallas_call(
        back_kernel,
        grid=(images,),
        in_specs=[split] * 7
        + [
            pl.BlockSpec((1, length, width), lambda i: (i, 0, 0)),
            pl.BlockSpec((1, length, 3 * width), lambda i: (i, 0, 0)),
            pl.BlockSpec((1, heads, length, length), lambda i: (i, 0, 0, 0)),
            whole(wall),
            whole(small),
            whole(dwr),
        ],
        out_specs=[pl.BlockSpec((1, span, width), lambda i: (i, 0, 0))] * blocks + [whole(wall)],
        out_shape=[jax.ShapeDtypeStruct((images, span, width), bf16)] * blocks
        + [jax.ShapeDtypeStruct(wall.shape, bf16)],
        scratch_shapes=[
            pltpu.VMEM((width, 4 * width), f32),
            pltpu.VMEM((LANES, width), f32),
            pltpu.VMEM((length, width), bf16),
            pltpu.VMEM((length, 3 * width), bf16),
        ],
        compiler_params=pltpu.CompilerParams(vmem_limit_bytes=VMEM_BYTES),
        cost_estimate=true_cost(10 * images * length * width * (4 * width + 3 * length)),
        name="back",
    )(*gins, middle, cot, tok, att, proj, prob, wall, small, dwr)


def kept_pairs(route_rows, token_live, order_rows, expert_count, capacity):
    labels = jnp.arange(expert_count, dtype=jnp.int32)
    alive = token_live > 0
    first_hot = ((route_rows[:, 0:1] == labels) & alive[:, None]).astype(bf16)
    second_hot = ((route_rows[:, 1:2] == labels) & alive[:, None]).astype(bf16)
    earlier = (order_rows[None, :] < order_rows[:, None]).astype(bf16)
    ahead = mm(earlier, jnp.concatenate([first_hot, second_hot], 1))
    ahead_first = ahead[:, :expert_count]
    ahead_second = ahead[:, expert_count:] + jnp.sum(first_hot.astype(f32), 0)
    return jnp.where(ahead_first < capacity, first_hot, 0) + jnp.where(
        ahead_second < capacity, second_hot, 0
    )


def local(
    fsdp,
    seq,
    tokens,
    ln1_gain,
    ln1_bias,
    w_qkv,
    w_out,
    ln2_gain,
    ln2_bias,
    w_router,
    w_in,
    w_down,
    padding,
    routes,
    priority,
    cotangent,
):
    images, span, width = tokens.shape
    expert_count, shard_rows = w_in.shape[0], w_in.shape[1]
    rows = images * span
    own = images // seq
    length = seq * span
    capacity = (2 * rows + expert_count - 1) // expert_count
    outer = fsdp // 8
    if outer > 1:
        outer_groups = [[o * 8 + n for o in range(outer)] for n in range(8)]
    spread = functools.partial(flip, fsdp=fsdp)
    seq_index = lax.axis_index("seq")
    place = lax.axis_index("fsdp") if outer == 1 else jnp.int32(0)
    place = place.astype(jnp.int32).reshape(1)

    def picked(array, k):
        return lax.dynamic_index_in_dim(array, seq_index ^ k, 0, keepdims=False)

    tokens = tokens.reshape(seq, own * span, width)
    tok = jnp.stack(exchange([picked(tokens, k) for k in range(seq)]))
    tok = tok.reshape(seq, own, span, width)

    columns = jnp.concatenate(
        [w_router] + [v[:, None] for v in (ln1_gain, ln1_bias, ln2_gain, ln2_bias)], 1
    )
    columns = jnp.pad(columns, ((0, 0), (0, LANES - columns.shape[1])))
    shard = jnp.concatenate([w_qkv, w_out, columns], 1)
    if outer == 1:
        cut = width // 16
        from_x, from_y = spread(shard, bits=2), spread(shard, bits=4)
        from_x, from_y = tie((from_x, from_y), tok)
        near = [(0, 0, shard), (2, 0, from_x), (4, 0, from_y)]
        far = [
            (6, 0, spread(from_x[:cut], bits=4)),
            (6, cut, spread(from_y[cut:], bits=2)),
        ]
        near += [(r + 1, skip, spread(a, bits=1)) for r, skip, a in near]
    else:
        full = lax.all_gather(shard, "fsdp", axis=0, tiled=True)
        from_x = from_y = full
        near, far = [(n, 0, full[n * (width // 8) : (n + 1) * (width // 8)]) for n in range(8)], []

    live = lax.dynamic_slice_in_dim(padding, seq_index * span, span, 1)
    kept = kept_pairs(
        routes.reshape(rows, 2), live.reshape(rows), priority.reshape(rows), expert_count, capacity
    )
    kept = jnp.swapaxes(kept.reshape(seq, own * span, expert_count), 1, 2)
    kept = jnp.pad(
        kept, ((0, 0), (0, MASK_ROWS - expert_count), (0, width - own * span))
    ).astype(bf16)
    cot = cotangent * live[:, :, None].astype(bf16)
    packed = jnp.concatenate([cot.reshape(seq, own * span, width), kept], 1)
    packed = tie(packed, tok, from_x, from_y)
    packed = jnp.stack(exchange([picked(packed, k) for k in range(seq)]))
    late = tie([a for _, _, a in far], packed)
    far += [(r + 1, skip, spread(a, bits=1)) for (r, skip, _), a in zip(far, late)]
    offsets = [(r, skip) for r, skip, _ in near + far]
    pieces = [a for _, _, a in near + far]
    cot_x, cot_y = spread(packed, bits=2), spread(packed, bits=4)
    half = seq // 2
    cot_far = [spread(cot_x[:half], bits=4), spread(cot_y[half:], bits=2)]

    win, wdn = w_in, w_down
    if outer > 1:
        win = lax.all_gather(win, "fsdp", axis=1, tiled=True, axis_index_groups=outer_groups)
        wdn = lax.all_gather(wdn, "fsdp", axis=1, tiled=True, axis_index_groups=outer_groups)
    win, wdn = tie((win, wdn), pieces)
    weights = [win, spread(win, bits=1), wdn, spread(wdn, bits=1)]

    mine = lax.dynamic_slice_in_dim(padding, seq_index * own, own, 0).reshape(own, seq, span)
    mine = jnp.stack(relative([mine[:, b] for b in range(seq)], seq_index))
    vis = jnp.where(mine > 0, 0.0, neg_fill).astype(f32)
    vis = jnp.swapaxes(vis, 0, 1).reshape(own, 1, length)
    middle, two, proj, att, prob, wall, wr, small = front(tok, pieces, offsets, vis, place)
    two = two.reshape(seq, own * span, width)
    two_far = [[spread(two, bits=bits)] for bits in (2, 4, 6)]

    (dw,), dwr, out_0, gin_0 = experts_call(
        [[two]], [[packed]], weights, wr, None, "experts_own", lambda flops: SHORT
    )
    cots = [[cot_x], [cot_y], cot_far]
    left, dwr, outs, gins = experts_call(
        two_far, cots, weights, wr, dwr, "experts_far", true_cost
    )
    arrived = [spread(a, bits=bits) for a, bits in zip(gins, (2, 4, 6))]

    def finished(dw_kept, dw_sent):
        raw = plus(dw_kept, spread(dw_sent, bits=1))
        if outer > 1:
            raw = lax.psum_scatter(
                raw, "fsdp", scatter_dimension=2, tiled=True, axis_index_groups=outer_groups
            )
        return lax.optimization_barrier([raw[n : n + 1] for n in range(raw.shape[0])])

    first = Line(seq, finished(*grads_call(two_far, cots, left, dw, 0, 1))[0]).inwards()
    left, dw = tie((left, dw), first.raw)
    parts = grads_call(two_far, cots, left, dw, 1, expert_count - 1)
    ready = first.across(arrived)
    lines = [Line(seq, raw) for raw in finished(*tie(parts, ready, arrived))]
    lines[0].inwards()
    gins = gin_0 + tie(arrived, ready, [line.raw for line in lines])
    lines = [first] + lines

    shape4 = (seq, own, span, width)
    outs = [spread(a, bits=bits) for a, bits in zip(tie(outs, arrived), (2, 4, 6))]
    *grad_tok, dense = back(
        [a.reshape(shape4) for a in gins],
        middle,
        packed[:, : own * span].reshape(shape4),
        tok,
        att,
        proj,
        prob,
        wall,
        small,
        dwr,
    )
    flying = (outs, lines[0].waiting(), lines[1].waiting())
    dense = tie(dense, flying)
    dense = lax.psum_scatter(dense, "fsdp", scatter_dimension=0, tiled=True)
    lines[2].raw, lines[3].raw = tie((lines[2].raw, lines[3].raw), grad_tok)
    lines[2].inwards()
    ready = lines[1].across(grad_tok, flying)
    ready = lines[0].outwards(ready)
    lines[3].inwards()
    ready = lines[2].across(ready)
    ready = lines[1].outwards(ready)
    ready = lines[3].across(ready)
    ready = lines[2].outwards(ready)
    dense_line = Line(seq, tie(dense, ready)).inwards()
    ready = lines[3].outwards(dense_line.raw)

    ready = dense_line.across(ready)
    outs, grad_tok = tie((outs, grad_tok), ready)
    outs = [a.reshape(shape4) for a in out_0 + outs]
    home = []
    for k in range(seq):
        alive = mine[k][:, :, None].astype(f32)
        combined = sum(a[k].astype(f32) for a in outs)
        home.append(jnp.stack([(alive * (middle[k] + combined)).astype(bf16), grad_tok[k]]))
    home = exchange(home)
    ready = dense_line.outwards(ready)
    home = relative(tie(home, ready), seq_index)
    outputs, grad_tokens = (
        jnp.concatenate([a[n] for a in home], 0).reshape(images, span, width) for n in range(2)
    )
    grads = [line.finish() for line in lines]
    dense = dense_line.finish().astype(f32)
    expert_grads = [jnp.concatenate([g[:, n] for g in grads], 0).astype(f32) for n in range(2)]
    tail = dense[:, 4 * width :]
    return (
        outputs,
        grad_tokens,
        tail[:, 4],
        tail[:, 5],
        dense[:, : 3 * width],
        dense[:, 3 * width : 4 * width],
        tail[:, 6],
        tail[:, 7],
        tail[:, :expert_count],
        expert_grads[0],
        expert_grads[1],
    )


def solution(mesh):
    rows = P("fsdp", "seq", None)
    in_specs = (
        rows,
        P("fsdp"),
        P("fsdp"),
        P("fsdp", None),
        P("fsdp", None),
        P("fsdp"),
        P("fsdp"),
        P("fsdp", None),
        P(None, "fsdp", None),
        P(None, "fsdp", None),
        P("fsdp", None),
        rows,
        P("fsdp", "seq"),
        rows,
    )
    out_specs = (
        rows,
        rows,
        P("fsdp"),
        P("fsdp"),
        P("fsdp", None),
        P("fsdp", None),
        P("fsdp"),
        P("fsdp"),
        P("fsdp", None),
        P(None, "fsdp", None),
        P(None, "fsdp", None),
    )
    return jax.shard_map(
        functools.partial(local, mesh.shape["fsdp"], mesh.shape["seq"]),
        mesh=mesh,
        in_specs=in_specs,
        out_specs=out_specs,
        check_vma=False,
    )
```

profile of v0, /device:TPU:0, one launch (start us, length us, event | category | flops | bytes accessed | tf_op | source)
XLA Modules:
  0.0 453.9 jit_solution(10392014750514804492)
XLA Ops:
  9.4 3.0 collective-permute-start.1
  12.4 1.5 collective-permute-start
  14.7 3.6 collective-permute-start.4
  21.4 3.2 collective-permute-done.4
  24.6 10.0 %collective-permute-done.3 = bf16[128,768]{1,0:T(8,128)(2,1)S(1)} collective-permute-done((bf16[128,768]{1,0:T(8,128)(2,1)}, bf16[128,768]{1,0:T(8,128)(2,1)S(1)}, u32[]{:S(2)}, u32[]{:S(2)}) %collective-permute-start.3) | collective-permute-done | bytes 196640 | tf_op jit(solution)/shard_map/ppermute | solution.py:477
  35.7 2.5 collective-permute-start.12
  38.2 1.9 collective-permute-start.10
  41.4 4.7 %collective-permute-done.12 = bf16[144,768]{1,0:T(8,128)(2,1)S(1)} collective-permute-done((bf16[144,768]{1,0:T(8,128)(2,1)S(1)}, bf16[144,768]{1,0:T(8,128)(2,1)S(1)}, u32[]{:S(2)}, u32[]{:S(2)}) %collective-permute-start.12) | collective-permute-done | bytes 221216 | tf_op jit(solution)/shard_map/ppermute | solution.py:477
  46.0 9.1 %collective-permute-done.11 = bf16[144,768]{1,0:T(8,128)(2,1)S(1)} collective-permute-done((bf16[144,768]{1,0:T(8,128)(2,1)S(1)}, bf16[144,768]{1,0:T(8,128)(2,1)S(1)}, u32[]{:S(2)}, u32[]{:S(2)}) %collective-permute-start.11) | collective-permute-done | bytes 221216 | tf_op jit(solution)/shard_map/ppermute | solution.py:477
  56.4 2.1 collective-permute-done.13.refs_8_
  64.0 15.0 %front.1 = (f32[4,2,64,768]{3,2,1,0:T(8,128)}, bf16[4,2,64,768]{3,2,1,0:T(8,128)(2,1)}, bf16[2,256,2304]{2,1,0:T(8,128)(2,1)}, bf16[2,256,768]{2,1,0:T(8,128)(2,...) custom-call(bf16[96,3200]{1,0:T(8,128)(2,1)} %copy-done.3, ...), custom_call_target="tpu_custom_call" | custom-call | flops 1000 | bytes 1000 | tf_op jit(solution)/shard_map/front/pallas_call | solution.py:124
  79.0 2.5 collective-permute-start.19
  84.7 1.5 collective-permute-start.23
  86.2 1.5 collective-permute-start.22
  87.7 27.4 %experts_own.1 = (bf16[4,2,768,768]{3,2,1,0:T(8,128)(2,1)}, f32[8,768]{1,0:T(8,128)}, bf16[4,128,768]{2,1,0:T(8,128)(2,1)}, bf16[4,128,768]{2,1,0:T(8,128)(2,1)}) custom-call(bf16[4,128,768]{2,1,0:T(8,128)(2,1)} %bitcast.101, bf16[4,144,768]{2,1,0:T(8,128)(2,1)} %copy-done, bf16[4,384,768]{2,1,0:T(8,128)(2,1)} %refs_7_, bf16[4,384,768]{2,1,0:T(8,128)(2,1)} %copy-done.6, ...), custom_call_target="tpu_custom_call" | custom-call | flops 1000 | bytes 1000 | tf_op jit(solution)/shard_map/experts_own/pallas_call | solution.py:357
  117.7 7.9 %collective-permute-done.23.refs_6_ = bf16[2,144,768]{2,1,0:T(8,128)(2,1)S(1)} collective-permute-done((bf16[2,144,768]{2,1,0:T(8,128)(2,1)S(1)}, bf16[2,144,768]{2,1,0:T(8,128)(2,1)S(1)}, u32[]{:S(2)}, u32[]{:S(2)}) %collective-permute-start.23) | collective-permute-done | bytes 442400 | tf_op jit(solution)/shard_map/ppermute | solution.py:467
  126.4 53.8 %experts_far.1 = (bf16[1536,3072]{1,0:T(8,128)(2,1)}, bf16[1536,3072]{1,0:T(8,128)(2,1)}, f32[8,768]{1,0:T(8,128)}, bf16[4,128,768]{2,1,0:T(8,128)(2,1)}, bf16[4...) custom-call(bf16[4,128,768]{2,1,0:T(8,128)(2,1)} %collective-permute, ...), custom_call_target="tpu_custom_call" | custom-call | flops 72477573120 | bytes 16777216 | tf_op jit(solution)/shard_map/experts_far/pallas_call | solution.py:357
  180.2 10.8 %expert_grads.2 = (bf16[1,2,384,768]{3,2,1,0:T(8,128)(2,1)}, bf16[1,2,384,768]{3,2,1,0:T(8,128)(2,1)}) custom-call(bf16[4,128,768]{2,1,0:T(8,128)(2,1)} %collective-permute-done.17.refs_0_, bf16[4,128,768]{2,1,0:T(8,128)(2,1)} %collective-permute-done.18.refs_1_, bf16[4,128,768]{2,1,0:T(8,128)(2,1)} %collective-permute-done.19.refs_2_, ...), custom_call_target="tpu_custom_call" | custom-call | flops 14495514624 | bytes 16777216 | tf_op jit(solution)/shard_map/expert_grads/pallas_call | solution.py:447
  191.1 1.6 collective-permute-start.24
  194.7 1.6 add_convert_fusion.9
  197.6 19.9 %expert_grads.3 = (bf16[3,2,384,768]{3,2,1,0:T(8,128)(2,1)}, bf16[3,2,384,768]{3,2,1,0:T(8,128)(2,1)}) custom-call(bf16[4,128,768]{2,1,0:T(8,128)(2,1)} %collective-permute-done.17.refs_0_, bf16[4,128,768]{2,1,0:T(8,128)(2,1)} %collective-permute-done.18.refs_1_, bf16[4,128,768]{2,1,0:T(8,128)(2,1)} %collective-permute-done.19.refs_2_, ...), custom_call_target="tpu_custom_call" | custom-call | flops 43486543872 | bytes 16777216 | tf_op jit(solution)/shard_map/expert_grads/pallas_call | solution.py:447
  217.5 11.8 %collective-permute-done.25 = bf16[4,128,768]{2,1,0:T(8,128)(2,1)S(1)} collective-permute-done((bf16[4,128,768]{2,1,0:T(8,128)(2,1)}, bf16[4,128,768]{2,1,0:T(8,128)(2,1)S(1)}, u32[]{:S(2)}, u32[]{:S(2)}) %collective-permute-start.25) | collective-permute-done | bytes 786464 | tf_op jit(solution)/shard_map/ppermute | solution.py:467
  232.5 2.5 collective-permute-start.29
  235.0 1.7 collective-permute-start.33
  239.2 3.0 collective-permute-start.34
  242.2 21.3 %back.1 = (bf16[2,64,768]{2,1,0:T(8,128)(2,1)}, bf16[2,64,768]{2,1,0:T(8,128)(2,1)}, bf16[2,64,768]{2,1,0:T(8,128)(2,1)}, bf16[2,64,768]{2,1,0:T(8,128)(2,1)}, bf16[768,3200]{1,0:T(8,128)(2,1)}) custom-call(bf16[4,2,64,768]{3,2,1,0:T(8,128)(2,1)} %bitcast.129, bf16[4,2,64,768]{3,2,1,0:T(8,128)(2,1)} %bitcast.130, bf16[4,2,64,768]{3,2,1,0:T(8,128)(2,1)} %bitcast.131, ...), custom_call_target="tpu_custom_call" | custom-call | flops 30198988800 | bytes 16777216 | tf_op jit(solution)/shard_map/back/pallas_call | solution.py:601
  263.6 5.2 %collective-permute-done.29 = bf16[4,128,768]{2,1,0:T(8,128)(2,1)} collective-permute-done((bf16[4,128,768]{2,1,0:T(8,128)(2,1)}, bf16[4,128,768]{2,1,0:T(8,128)(2,1)}, u32[]{:S(2)}, u32[]{:S(2)}) %collective-permute-start.29) | collective-permute-done | bytes 786464 | tf_op jit(solution)/shard_map/ppermute | solution.py:467
  268.9 2.2 collective-permute-start.35
  272.5 2.1 add_convert_fusion.7
  275.4 2.7 add_convert_fusion.6
  278.1 19.4 %collective-permute-done.35 = bf16[1,2,384,768]{3,2,1,0:T(8,128)(2,1)S(1)} collective-permute-done((bf16[1,2,384,768]{3,2,1,0:T(8,128)(2,1)S(1)}, bf16[1,2,384,768]{3,2,1,0:T(8,128)(2,1)S(1)}, u32[]{:S(2)}, u32[]{:S(2)}) %collective-permute-start.35) | collective-permute-done | bytes 1179680 | tf_op jit(solution)/shard_map/ppermute | solution.py:502
  300.1 20.7 %collective-permute-done.37 = bf16[1,2,384,768]{3,2,1,0:T(8,128)(2,1)S(1)} collective-permute-done((bf16[1,2,384,768]{3,2,1,0:T(8,128)(2,1)S(1)}, bf16[1,2,384,768]{3,2,1,0:T(8,128)(2,1)S(1)}, u32[]{:S(2)}, u32[]{:S(2)}) %collective-permute-start.37) | collective-permute-done | bytes 1179680 | tf_op jit(solution)/shard_map/ppermute | solution.py:502
  322.7 1.7 collective-permute-start.40
  327.0 1.4 broadcast_select_fusion.3
  329.5 10.3 %collective-permute-start.39 = (bf16[96,3200]{1,0:T(8,128)(2,1)}, bf16[96,3200]{1,0:T(8,128)(2,1)S(1)}, u32[]{:S(2)}, u32[]{:S(2)}) collective-permute-start(bf16[96,3200]{1,0:T(8,128)(2,1)} %reduce-scatter.2.cloned.1.call-done), channel_id=1, source_target_pairs={{0,1},{3,2},{4,5},{7,6},{8,9},{11,10},{12,13},{15,14},{16,17},{19,... | collective-permute-start | bytes 1843208 | tf_op jit(solution)/shard_map/ppermute | solution.py:502
  339.8 16.3 %collective-permute-done.48 = bf16[1,2,384,768]{3,2,1,0:T(8,128)(2,1)} collective-permute-done((bf16[1,2,384,768]{3,2,1,0:T(8,128)(2,1)S(1)}, bf16[1,2,384,768]{3,2,1,0:T(8,128)(2,1)}, u32[]{:S(2)}, u32[]{:S(2)}) %collective-permute-start.48) | collective-permute-done | bytes 1179680 | tf_op jit(solution)/shard_map/ppermute | solution.py:515
  356.1 1.4 broadcast_select_fusion.1
  357.6 1.6 add_convert_fusion.1
  359.2 1.6 collective-permute-start.49
  361.8 2.2 convert_add_fusion
  365.0 5.0 %collective-permute-start.41 = (bf16[2,2,64,768]{3,2,1,0:T(8,128)(2,1)S(1)}, bf16[2,2,64,768]{3,2,1,0:T(8,128)(2,1)S(1)}, u32[]{:S(2)}, u32[]{:S(2)}) collective-permute-start(bf16[2,2,64,768]{3,2,1,0:T(8,128)(2,1)S(1)} %pad_maximum_fusion.5), channel_id=1, source_target_pairs={{0,1},{1,0},{2,3},{3,2},{4,5},{5,4},{6,7},{7,6},{8,9},{9,8},{10,11... | collective-permute-start | bytes 1179656 | tf_op jit(solution)/shard_map/ppermute | solution.py:477
  370.7 19.1 %collective-permute-done.47 = bf16[1,2,384,768]{3,2,1,0:T(8,128)(2,1)} collective-permute-done((bf16[1,2,384,768]{3,2,1,0:T(8,128)(2,1)S(1)}, bf16[1,2,384,768]{3,2,1,0:T(8,128)(2,1)}, u32[]{:S(2)}, u32[]{:S(2)}) %collective-permute-start.47) | collective-permute-done | bytes 1179680 | tf_op jit(solution)/shard_map/ppermute | solution.py:515
  389.8 1.9 collective-permute-start.43
  391.7 31.7 %collective-permute-done.49 = bf16[1,2,384,768]{3,2,1,0:T(8,128)(2,1)S(1)} collective-permute-done((bf16[1,2,384,768]{3,2,1,0:T(8,128)(2,1)S(1)}, bf16[1,2,384,768]{3,2,1,0:T(8,128)(2,1)S(1)}, u32[]{:S(2)}, u32[]{:S(2)}) %collective-permute-start.49) | collective-permute-done | bytes 1179680 | tf_op jit(solution)/shard_map/ppermute | solution.py:515
  423.4 1.6 broadcast_select_fusion
  426.2 2.6 maximum_convert_fusion.1
  428.8 2.6 maximum_convert_fusion
  435.1 8.5 %collective-permute-done.45 = bf16[96,3200]{1,0:T(8,128)(2,1)S(1)} collective-permute-done((bf16[96,3200]{1,0:T(8,128)(2,1)S(1)}, bf16[96,3200]{1,0:T(8,128)(2,1)S(1)}, u32[]{:S(2)}, u32[]{:S(2)}) %collective-permute-start.45) | collective-permute-done | bytes 614432 | tf_op jit(solution)/shard_map/ppermute | solution.py:515
  (199 shorter events, 51.5 us)
Async XLA Ops:
  7.2 322.3 %reduce-scatter.2.cloned.1.call-start = ((), (), s32[]{:S(2)}) async-start(), calls=%async_computation.1 | async-start | bytes 5529600 | tf_op jit(solution)/shard_map/reduce_scatter | solution.py:778
  9.4 26.3 %collective-permute-start.1 = (bf16[96,3200]{1,0:T(8,128)(2,1)S(1)}, bf16[96,3200]{1,0:T(8,128)(2,1)S(1)}, u32[]{:S(2)}, u32[]{:S(2)}) collective-permute-start(bf16[96,3200]{1,0:T(8,128)(2,1)S(1)} %fusion.5.refs_0_), channel_id=1, source_target_pairs={{0,16},{4,20},{8,24},{12,28},{16,0},{20,4},{24,8},{28,12},{1,17},{... | collective-permute-start | bytes 1843208 | tf_op jit(solution)/shard_map/ppermute | solution.py:467
  12.4 23.2 %collective-permute-start = (bf16[96,3200]{1,0:T(8,128)(2,1)S(1)}, bf16[96,3200]{1,0:T(8,128)(2,1)S(1)}, u32[]{:S(2)}, u32[]{:S(2)}) collective-permute-start(bf16[96,3200]{1,0:T(8,128)(2,1)S(1)} %fusion.5.refs_0_), channel_id=1, source_target_pairs={{0,8},{4,12},{8,0},{12,4},{16,24},{20,28},{24,16},{28,20},{1,9},{5... | collective-permute-start | bytes 1843208 | tf_op jit(solution)/shard_map/ppermute | solution.py:467
  14.7 9.9 %collective-permute-start.4 = (bf16[128,768]{1,0:T(8,128)(2,1)}, bf16[128,768]{1,0:T(8,128)(2,1)S(1)}, u32[]{:S(2)}, u32[]{:S(2)}) collective-permute-start(bf16[128,768]{1,0:T(8,128)(2,1)} %get-tuple-element.236), channel_id=1, source_target_pairs={{0,3},{1,2},{2,1},{3,0},{4,7},{5,6},{6,5},{7,4},{8,11},{9,10},{10,... | collective-permute-start | bytes 589832 | tf_op jit(solution)/shard_map/ppermute | solution.py:477
  18.3 16.3 %collective-permute-start.3 = (bf16[128,768]{1,0:T(8,128)(2,1)}, bf16[128,768]{1,0:T(8,128)(2,1)S(1)}, u32[]{:S(2)}, u32[]{:S(2)}) collective-permute-start(bf16[128,768]{1,0:T(8,128)(2,1)} %get-tuple-element.237), channel_id=1, source_target_pairs={{0,2},{1,3},{2,0},{3,1},{4,6},{5,7},{6,4},{7,5},{8,10},{9,11},{10,... | collective-permute-start | bytes 589832 | tf_op jit(solution)/shard_map/ppermute | solution.py:477
  18.3 16.3 %collective-permute-start.2 = (bf16[128,768]{1,0:T(8,128)(2,1)S(1)}, bf16[128,768]{1,0:T(8,128)(2,1)S(1)}, u32[]{:S(2)}, u32[]{:S(2)}) collective-permute-start(bf16[128,768]{1,0:T(8,128)(2,1)S(1)} %get-tuple-element.238), channel_id=1, source_target_pairs={{0,1},{1,0},{2,3},{3,2},{4,5},{5,4},{6,7},{7,6},{8,9},{9,8},{10,11... | collective-permute-start | bytes 589832 | tf_op jit(solution)/shard_map/ppermute | solution.py:477
  35.7 10.3 %collective-permute-start.12 = (bf16[144,768]{1,0:T(8,128)(2,1)S(1)}, bf16[144,768]{1,0:T(8,128)(2,1)S(1)}, u32[]{:S(2)}, u32[]{:S(2)}) collective-permute-start(bf16[144,768]{1,0:T(8,128)(2,1)S(1)} %get-tuple-element.232), channel_id=1, source_target_pairs={{0,3},{1,2},{2,1},{3,0},{4,7},{5,6},{6,5},{7,4},{8,11},{9,10},{10,... | collective-permute-start | bytes 663560 | tf_op jit(solution)/shard_map/ppermute | solution.py:477
  38.2 16.9 %collective-permute-start.11 = (bf16[144,768]{1,0:T(8,128)(2,1)S(1)}, bf16[144,768]{1,0:T(8,128)(2,1)S(1)}, u32[]{:S(2)}, u32[]{:S(2)}) collective-permute-start(bf16[144,768]{1,0:T(8,128)(2,1)S(1)} %get-tuple-element.233), channel_id=1, source_target_pairs={{0,2},{1,3},{2,0},{3,1},{4,6},{5,7},{6,4},{7,5},{8,10},{9,11},{10,... | collective-permute-start | bytes 663560 | tf_op jit(solution)/shard_map/ppermute | solution.py:477
  38.2 16.9 %collective-permute-start.10 = (bf16[144,768]{1,0:T(8,128)(2,1)S(1)}, bf16[144,768]{1,0:T(8,128)(2,1)S(1)}, u32[]{:S(2)}, u32[]{:S(2)}) collective-permute-start(bf16[144,768]{1,0:T(8,128)(2,1)S(1)} %get-tuple-element.234), channel_id=1, source_target_pairs={{0,1},{1,0},{2,3},{3,2},{4,5},{5,4},{6,7},{7,6},{8,9},{9,8},{10,11... | collective-permute-start | bytes 663560 | tf_op jit(solution)/shard_map/ppermute | solution.py:477
  40.2 15.6 %collective-permute-start.9 = (bf16[48,3200]{1,0:T(8,128)(2,1)S(1)}, bf16[48,3200]{1,0:T(8,128)(2,1)S(1)}, u32[]{:S(2)}, u32[]{:S(2)}) collective-permute-start(bf16[48,3200]{1,0:T(8,128)(2,1)S(1)} %slice.204), channel_id=1, source_target_pairs={{0,8},{4,12},{8,0},{12,4},{16,24},{20,28},{24,16},{28,20},{1,9},{5... | collective-permute-start | bytes 921608 | tf_op jit(solution)/shard_map/ppermute | solution.py:467
  40.8 15.0 %collective-permute-start.8 = (bf16[48,3200]{1,0:T(8,128)(2,1)S(1)}, bf16[48,3200]{1,0:T(8,128)(2,1)S(1)}, u32[]{:S(2)}, u32[]{:S(2)}) collective-permute-start(bf16[48,3200]{1,0:T(8,128)(2,1)S(1)} %slice.203), channel_id=1, source_target_pairs={{0,16},{4,20},{8,24},{12,28},{16,0},{20,4},{24,8},{28,12},{1,17},{... | collective-permute-start | bytes 921608 | tf_op jit(solution)/shard_map/ppermute | solution.py:467
  46.0 10.4 %collective-permute-start.5 = (bf16[96,3200]{1,0:T(8,128)(2,1)S(1)}, bf16[96,3200]{1,0:T(8,128)(2,1)S(1)}, u32[]{:S(2)}, u32[]{:S(2)}) collective-permute-start(bf16[96,3200]{1,0:T(8,128)(2,1)S(1)} %fusion.5.refs_0_), channel_id=1, source_target_pairs={{0,4},{4,0},{8,12},{12,8},{16,20},{20,16},{24,28},{28,24},{1,5},{5... | collective-permute-start | bytes 1843208 | tf_op jit(solution)/shard_map/ppermute | solution.py:467
  55.1 3.8 collective-permute-start.6
  55.2 3.8 collective-permute-start.7
  59.0 25.7 %collective-permute-start.15 = (bf16[4,384,768]{2,1,0:T(8,128)(2,1)}, bf16[4,384,768]{2,1,0:T(8,128)(2,1)S(1)}, u32[]{:S(2)}, u32[]{:S(2)}) collective-permute-start(bf16[4,384,768]{2,1,0:T(8,128)(2,1)} %refs_7_), channel_id=1, source_target_pairs={{0,4},{4,0},{8,12},{12,8},{16,20},{20,16},{24,28},{28,24},{1,5},{5... | collective-permute-start | bytes 7077896 | tf_op jit(solution)/shard_map/ppermute | solution.py:467
  59.2 27.0 %collective-permute-start.16 = (bf16[4,384,768]{2,1,0:T(8,128)(2,1)}, bf16[4,384,768]{2,1,0:T(8,128)(2,1)}, u32[]{:S(2)}, u32[]{:S(2)}) collective-permute-start(bf16[4,384,768]{2,1,0:T(8,128)(2,1)} %refs_9_), channel_id=1, source_target_pairs={{0,4},{4,0},{8,12},{12,8},{16,20},{20,16},{24,28},{28,24},{1,5},{5... | collective-permute-start | bytes 7077896 | tf_op jit(solution)/shard_map/ppermute | solution.py:467
  59.5 21.9 %collective-permute-start.21 = (bf16[4,144,768]{2,1,0:T(8,128)(2,1)S(1)}, bf16[4,144,768]{2,1,0:T(8,128)(2,1)}, u32[]{:S(2)}, u32[]{:S(2)}) collective-permute-start(bf16[4,144,768]{2,1,0:T(8,128)(2,1)S(1)} %pad_maximum_fusion.refs_1_), channel_id=1, source_target_pairs={{0,16},{4,20},{8,24},{12,28},{16,0},{20,4},{24,8},{28,12},{1,17},{... | collective-permute-start | bytes 2654216 | tf_op jit(solution)/shard_map/ppermute | solution.py:467
  60.1 21.9 %collective-permute-start.20 = (bf16[4,144,768]{2,1,0:T(8,128)(2,1)S(1)}, bf16[4,144,768]{2,1,0:T(8,128)(2,1)}, u32[]{:S(2)}, u32[]{:S(2)}) collective-permute-start(bf16[4,144,768]{2,1,0:T(8,128)(2,1)S(1)} %pad_maximum_fusion.refs_1_), channel_id=1, source_target_pairs={{0,8},{4,12},{8,0},{12,4},{16,24},{20,28},{24,16},{28,20},{1,9},{5... | collective-permute-start | bytes 2654216 | tf_op jit(solution)/shard_map/ppermute | solution.py:467
  79.0 36.1 %collective-permute-start.19 = (bf16[4,128,768]{2,1,0:T(8,128)(2,1)}, bf16[4,128,768]{2,1,0:T(8,128)(2,1)}, u32[]{:S(2)}, u32[]{:S(2)}) collective-permute-start(bf16[4,128,768]{2,1,0:T(8,128)(2,1)} %bitcast.98), channel_id=1, source_target_pairs={{0,24},{4,28},{8,16},{12,20},{16,8},{20,12},{24,0},{28,4},{1,25},{... | collective-permute-start | bytes 2359304 | tf_op jit(solution)/shard_map/ppermute | solution.py:467
  81.5 35.0 %collective-permute-start.18 = (bf16[4,128,768]{2,1,0:T(8,128)(2,1)}, bf16[4,128,768]{2,1,0:T(8,128)(2,1)}, u32[]{:S(2)}, u32[]{:S(2)}) collective-permute-start(bf16[4,128,768]{2,1,0:T(8,128)(2,1)} %bitcast.99), channel_id=1, source_target_pairs={{0,16},{4,20},{8,24},{12,28},{16,0},{20,4},{24,8},{28,12},{1,17},{... | collective-permute-start | bytes 2359304 | tf_op jit(solution)/shard_map/ppermute | solution.py:467
  82.0 35.7 %collective-permute-start.17 = (bf16[4,128,768]{2,1,0:T(8,128)(2,1)}, bf16[4,128,768]{2,1,0:T(8,128)(2,1)}, u32[]{:S(2)}, u32[]{:S(2)}) collective-permute-start(bf16[4,128,768]{2,1,0:T(8,128)(2,1)} %bitcast.100), channel_id=1, source_target_pairs={{0,8},{4,12},{8,0},{12,4},{16,24},{20,28},{24,16},{28,20},{1,9},{5... | collective-permute-start | bytes 2359304 | tf_op jit(solution)/shard_map/ppermute | solution.py:467
  84.7 40.9 %collective-permute-start.23 = (bf16[2,144,768]{2,1,0:T(8,128)(2,1)S(1)}, bf16[2,144,768]{2,1,0:T(8,128)(2,1)S(1)}, u32[]{:S(2)}, u32[]{:S(2)}) collective-permute-start(bf16[2,144,768]{2,1,0:T(8,128)(2,1)S(1)} %slice.267), channel_id=1, source_target_pairs={{0,8},{4,12},{8,0},{12,4},{16,24},{20,28},{24,16},{28,20},{1,9},{5... | collective-permute-start | bytes 1327112 | tf_op jit(solution)/shard_map/ppermute | solution.py:467
  86.2 39.6 %collective-permute-start.22 = (bf16[2,144,768]{2,1,0:T(8,128)(2,1)S(1)}, bf16[2,144,768]{2,1,0:T(8,128)(2,1)}, u32[]{:S(2)}, u32[]{:S(2)}) collective-permute-start(bf16[2,144,768]{2,1,0:T(8,128)(2,1)S(1)} %slice.266), channel_id=1, source_target_pairs={{0,16},{4,20},{8,24},{12,28},{16,0},{20,4},{24,8},{28,12},{1,17},{... | collective-permute-start | bytes 1327112 | tf_op jit(solution)/shard_map/ppermute | solution.py:467
  191.1 26.4 %collective-permute-start.24 = (bf16[4,128,768]{2,1,0:T(8,128)(2,1)}, bf16[4,128,768]{2,1,0:T(8,128)(2,1)S(1)}, u32[]{:S(2)}, u32[]{:S(2)}) collective-permute-start(bf16[4,128,768]{2,1,0:T(8,128)(2,1)} %get-tuple-element.102), channel_id=1, source_target_pairs={{0,8},{4,12},{8,0},{12,4},{16,24},{20,28},{24,16},{28,20},{1,9},{5... | collective-permute-start | bytes 2359304 | tf_op jit(solution)/shard_map/ppermute | solution.py:467
  192.7 36.7 %collective-permute-start.25 = (bf16[4,128,768]{2,1,0:T(8,128)(2,1)}, bf16[4,128,768]{2,1,0:T(8,128)(2,1)S(1)}, u32[]{:S(2)}, u32[]{:S(2)}) collective-permute-start(bf16[4,128,768]{2,1,0:T(8,128)(2,1)} %get-tuple-element.103), channel_id=1, source_target_pairs={{0,16},{4,20},{8,24},{12,28},{16,0},{20,4},{24,8},{28,12},{1,17},{... | collective-permute-start | bytes 2359304 | tf_op jit(solution)/shard_map/ppermute | solution.py:467
  193.4 35.9 %collective-permute-start.26 = (bf16[4,128,768]{2,1,0:T(8,128)(2,1)}, bf16[4,128,768]{2,1,0:T(8,128)(2,1)}, u32[]{:S(2)}, u32[]{:S(2)}) collective-permute-start(bf16[4,128,768]{2,1,0:T(8,128)(2,1)} %get-tuple-element.104), channel_id=1, source_target_pairs={{0,24},{4,28},{8,16},{12,20},{16,8},{20,12},{24,0},{28,4},{1,25},{... | collective-permute-start | bytes 2359304 | tf_op jit(solution)/shard_map/ppermute | solution.py:467
  196.2 34.0 %collective-permute-start.31 = (bf16[1,2,384,768]{3,2,1,0:T(8,128)(2,1)S(1)}, bf16[1,2,384,768]{3,2,1,0:T(8,128)(2,1)S(1)}, u32[]{:S(2)}, u32[]{:S(2)}) collective-permute-start(bf16[1,2,384,768]{3,2,1,0:T(8,128)(2,1)S(1)} %add_convert_fusion.9), channel_id=1, source_target_pairs={{0,1},{3,2},{4,5},{7,6},{8,9},{11,10},{12,13},{15,14},{16,17},{19,... | collective-permute-start | bytes 3538952 | tf_op jit(solution)/shard_map/ppermute | solution.py:502
  230.5 6.5 %collective-permute-start.32 = (bf16[3,2,384,768]{3,2,1,0:T(8,128)(2,1)}, bf16[3,2,384,768]{3,2,1,0:T(8,128)(2,1)S(1)}, u32[]{:S(2)}, u32[]{:S(2)}) collective-permute-start(bf16[3,2,384,768]{3,2,1,0:T(8,128)(2,1)} %get-tuple-element.121), channel_id=1, source_target_pairs={{0,4},{4,0},{8,12},{12,8},{16,20},{20,16},{24,28},{28,24},{1,5},{5... | collective-permute-start | bytes 10616840 | tf_op jit(solution)/shard_map/ppermute | solution.py:467
  231.5 32.0 %collective-permute-start.27 = (bf16[4,128,768]{2,1,0:T(8,128)(2,1)}, bf16[4,128,768]{2,1,0:T(8,128)(2,1)}, u32[]{:S(2)}, u32[]{:S(2)}) collective-permute-start(bf16[4,128,768]{2,1,0:T(8,128)(2,1)} %get-tuple-element.105), channel_id=1, source_target_pairs={{0,8},{4,12},{8,0},{12,4},{16,24},{20,28},{24,16},{28,20},{1,9},{5... | collective-permute-start | bytes 2359304 | tf_op jit(solution)/shard_map/ppermute | solution.py:467
  231.5 32.0 %collective-permute-start.28 = (bf16[4,128,768]{2,1,0:T(8,128)(2,1)}, bf16[4,128,768]{2,1,0:T(8,128)(2,1)}, u32[]{:S(2)}, u32[]{:S(2)}) collective-permute-start(bf16[4,128,768]{2,1,0:T(8,128)(2,1)} %get-tuple-element.106), channel_id=1, source_target_pairs={{0,16},{4,20},{8,24},{12,28},{16,0},{20,4},{24,8},{28,12},{1,17},{... | collective-permute-start | bytes 2359304 | tf_op jit(solution)/shard_map/ppermute | solution.py:467
  232.5 36.3 %collective-permute-start.29 = (bf16[4,128,768]{2,1,0:T(8,128)(2,1)}, bf16[4,128,768]{2,1,0:T(8,128)(2,1)}, u32[]{:S(2)}, u32[]{:S(2)}) collective-permute-start(bf16[4,128,768]{2,1,0:T(8,128)(2,1)} %get-tuple-element.107), channel_id=1, source_target_pairs={{0,24},{4,28},{8,16},{12,20},{16,8},{20,12},{24,0},{28,4},{1,25},{... | collective-permute-start | bytes 2359304 | tf_op jit(solution)/shard_map/ppermute | solution.py:467
  235.0 33.8 %collective-permute-start.33 = (bf16[1,2,384,768]{3,2,1,0:T(8,128)(2,1)S(1)}, bf16[1,2,384,768]{3,2,1,0:T(8,128)(2,1)}, u32[]{:S(2)}, u32[]{:S(2)}) collective-permute-start(bf16[1,2,384,768]{3,2,1,0:T(8,128)(2,1)S(1)} %add_convert_fusion.8), channel_id=1, source_target_pairs={{1,2},{2,1},{5,6},{6,5},{9,10},{10,9},{13,14},{14,13},{17,18},{18,... | collective-permute-start | bytes 3538952 | tf_op jit(solution)/shard_map/ppermute | solution.py:508
  239.2 29.6 %collective-permute-start.34 = (bf16[1,2,384,768]{3,2,1,0:T(8,128)(2,1)}, bf16[1,2,384,768]{3,2,1,0:T(8,128)(2,1)}, u32[]{:S(2)}, u32[]{:S(2)}) collective-permute-start(bf16[1,2,384,768]{3,2,1,0:T(8,128)(2,1)} %get-tuple-element.122), channel_id=1, source_target_pairs={{0,1},{3,2},{4,5},{7,6},{8,9},{11,10},{12,13},{15,14},{16,17},{19,... | collective-permute-start | bytes 3538952 | tf_op jit(solution)/shard_map/ppermute | solution.py:502
  268.9 28.6 %collective-permute-start.35 = (bf16[1,2,384,768]{3,2,1,0:T(8,128)(2,1)S(1)}, bf16[1,2,384,768]{3,2,1,0:T(8,128)(2,1)S(1)}, u32[]{:S(2)}, u32[]{:S(2)}) collective-permute-start(bf16[1,2,384,768]{3,2,1,0:T(8,128)(2,1)S(1)} %get-tuple-element.140), channel_id=1, source_target_pairs={{0,1},{3,2},{4,5},{7,6},{8,9},{11,10},{12,13},{15,14},{16,17},{19,... | collective-permute-start | bytes 3538952 | tf_op jit(solution)/shard_map/ppermute | solution.py:502
  271.1 49.7 %collective-permute-start.37 = (bf16[1,2,384,768]{3,2,1,0:T(8,128)(2,1)S(1)}, bf16[1,2,384,768]{3,2,1,0:T(8,128)(2,1)S(1)}, u32[]{:S(2)}, u32[]{:S(2)}) collective-permute-start(bf16[1,2,384,768]{3,2,1,0:T(8,128)(2,1)S(1)} %get-tuple-element.144), channel_id=1, source_target_pairs={{0,1},{3,2},{4,5},{7,6},{8,9},{11,10},{12,13},{15,14},{16,17},{19,... | collective-permute-start | bytes 3538952 | tf_op jit(solution)/shard_map/ppermute | solution.py:502
  274.6 25.2 %collective-permute-start.38 = (bf16[1,2,384,768]{3,2,1,0:T(8,128)(2,1)S(1)}, bf16[1,2,384,768]{3,2,1,0:T(8,128)(2,1)S(1)}, u32[]{:S(2)}, u32[]{:S(2)}) collective-permute-start(bf16[1,2,384,768]{3,2,1,0:T(8,128)(2,1)S(1)} %add_convert_fusion.7), channel_id=1, source_target_pairs={{1,2},{2,1},{5,6},{6,5},{9,10},{10,9},{13,14},{14,13},{17,18},{18,... | collective-permute-start | bytes 3538952 | tf_op jit(solution)/shard_map/ppermute | solution.py:508
  297.8 23.4 %collective-permute-start.36 = (bf16[1,2,384,768]{3,2,1,0:T(8,128)(2,1)S(1)}, bf16[1,2,384,768]{3,2,1,0:T(8,128)(2,1)S(1)}, u32[]{:S(2)}, u32[]{:S(2)}) collective-permute-start(bf16[1,2,384,768]{3,2,1,0:T(8,128)(2,1)S(1)} %add_convert_fusion.5), channel_id=1, source_target_pairs={{1,2},{2,1},{5,6},{6,5},{9,10},{10,9},{13,14},{14,13},{17,18},{18,... | collective-permute-start | bytes 3538952 | tf_op jit(solution)/shard_map/ppermute | solution.py:508
  298.5 28.5 %collective-permute-start.46 = (bf16[1,2,384,768]{3,2,1,0:T(8,128)(2,1)}, bf16[1,2,384,768]{3,2,1,0:T(8,128)(2,1)}, u32[]{:S(2)}, u32[]{:S(2)}) collective-permute-start(bf16[1,2,384,768]{3,2,1,0:T(8,128)(2,1)} %add_convert_fusion.6), channel_id=1, source_target_pairs={{1,0},{2,3},{5,4},{6,7},{9,8},{10,11},{13,12},{14,15},{17,16},{18,... | collective-permute-start | bytes 3538952 | tf_op jit(solution)/shard_map/ppermute | solution.py:515
  321.4 34.7 %collective-permute-start.48 = (bf16[1,2,384,768]{3,2,1,0:T(8,128)(2,1)S(1)}, bf16[1,2,384,768]{3,2,1,0:T(8,128)(2,1)}, u32[]{:S(2)}, u32[]{:S(2)}) collective-permute-start(bf16[1,2,384,768]{3,2,1,0:T(8,128)(2,1)S(1)} %add_convert_fusion.2), channel_id=1, source_target_pairs={{1,0},{2,3},{5,4},{6,7},{9,8},{10,11},{13,12},{14,15},{17,16},{18,... | collective-permute-start | bytes 3538952 | tf_op jit(solution)/shard_map/ppermute | solution.py:515
  322.7 34.9 %collective-permute-start.40 = (bf16[1,2,384,768]{3,2,1,0:T(8,128)(2,1)S(1)}, bf16[1,2,384,768]{3,2,1,0:T(8,128)(2,1)}, u32[]{:S(2)}, u32[]{:S(2)}) collective-permute-start(bf16[1,2,384,768]{3,2,1,0:T(8,128)(2,1)S(1)} %add_convert_fusion.3), channel_id=1, source_target_pairs={{1,2},{2,1},{5,6},{6,5},{9,10},{10,9},{13,14},{14,13},{17,18},{18,... | collective-permute-start | bytes 3538952 | tf_op jit(solution)/shard_map/ppermute | solution.py:508
  324.4 65.4 %collective-permute-start.47 = (bf16[1,2,384,768]{3,2,1,0:T(8,128)(2,1)S(1)}, bf16[1,2,384,768]{3,2,1,0:T(8,128)(2,1)}, u32[]{:S(2)}, u32[]{:S(2)}) collective-permute-start(bf16[1,2,384,768]{3,2,1,0:T(8,128)(2,1)S(1)} %add_convert_fusion.4), channel_id=1, source_target_pairs={{1,0},{2,3},{5,4},{6,7},{9,8},{10,11},{13,12},{14,15},{17,16},{18,... | collective-permute-start | bytes 3538952 | tf_op jit(solution)/shard_map/ppermute | solution.py:515
  329.5 31.4 %collective-permute-start.39 = (bf16[96,3200]{1,0:T(8,128)(2,1)}, bf16[96,3200]{1,0:T(8,128)(2,1)S(1)}, u32[]{:S(2)}, u32[]{:S(2)}) collective-permute-start(bf16[96,3200]{1,0:T(8,128)(2,1)} %reduce-scatter.2.cloned.1.call-done), channel_id=1, source_target_pairs={{0,1},{3,2},{4,5},{7,6},{8,9},{11,10},{12,13},{15,14},{16,17},{19,... | collective-permute-start | bytes 1843208 | tf_op jit(solution)/shard_map/ppermute | solution.py:502
  359.2 64.2 %collective-permute-start.49 = (bf16[1,2,384,768]{3,2,1,0:T(8,128)(2,1)S(1)}, bf16[1,2,384,768]{3,2,1,0:T(8,128)(2,1)S(1)}, u32[]{:S(2)}, u32[]{:S(2)}) collective-permute-start(bf16[1,2,384,768]{3,2,1,0:T(8,128)(2,1)S(1)} %add_convert_fusion.1), channel_id=1, source_target_pairs={{1,0},{2,3},{5,4},{6,7},{9,8},{10,11},{13,12},{14,15},{17,16},{18,... | collective-permute-start | bytes 3538952 | tf_op jit(solution)/shard_map/ppermute | solution.py:515
  361.1 70.4 %collective-permute-start.44 = (bf16[96,3200]{1,0:T(8,128)(2,1)S(1)}, bf16[96,3200]{1,0:T(8,128)(2,1)S(1)}, u32[]{:S(2)}, u32[]{:S(2)}) collective-permute-start(bf16[96,3200]{1,0:T(8,128)(2,1)S(1)} %add_convert_fusion.11), channel_id=1, source_target_pairs={{1,2},{2,1},{5,6},{6,5},{9,10},{10,9},{13,14},{14,13},{17,18},{18,... | collective-permute-start | bytes 1843208 | tf_op jit(solution)/shard_map/ppermute | solution.py:508
  365.0 67.9 %collective-permute-start.41 = (bf16[2,2,64,768]{3,2,1,0:T(8,128)(2,1)S(1)}, bf16[2,2,64,768]{3,2,1,0:T(8,128)(2,1)S(1)}, u32[]{:S(2)}, u32[]{:S(2)}) collective-permute-start(bf16[2,2,64,768]{3,2,1,0:T(8,128)(2,1)S(1)} %pad_maximum_fusion.5), channel_id=1, source_target_pairs={{0,1},{1,0},{2,3},{3,2},{4,5},{5,4},{6,7},{7,6},{8,9},{9,8},{10,11... | collective-permute-start | bytes 1179656 | tf_op jit(solution)/shard_map/ppermute | solution.py:477
  370.0 62.9 %collective-permute-start.42 = (bf16[2,2,64,768]{3,2,1,0:T(8,128)(2,1)S(1)}, bf16[2,2,64,768]{3,2,1,0:T(8,128)(2,1)S(1)}, u32[]{:S(2)}, u32[]{:S(2)}) collective-permute-start(bf16[2,2,64,768]{3,2,1,0:T(8,128)(2,1)S(1)} %pad_maximum_fusion.6), channel_id=1, source_target_pairs={{0,2},{1,3},{2,0},{3,1},{4,6},{5,7},{6,4},{7,5},{8,10},{9,11},{10,... | collective-permute-start | bytes 1179656 | tf_op jit(solution)/shard_map/ppermute | solution.py:477
  389.8 43.1 %collective-permute-start.43 = (bf16[2,2,64,768]{3,2,1,0:T(8,128)(2,1)S(1)}, bf16[2,2,64,768]{3,2,1,0:T(8,128)(2,1)S(1)}, u32[]{:S(2)}, u32[]{:S(2)}) collective-permute-start(bf16[2,2,64,768]{3,2,1,0:T(8,128)(2,1)S(1)} %pad_maximum_fusion.7), channel_id=1, source_target_pairs={{0,3},{1,2},{2,1},{3,0},{4,7},{5,6},{6,5},{7,4},{8,11},{9,10},{10,... | collective-permute-start | bytes 1179656 | tf_op jit(solution)/shard_map/ppermute | solution.py:477
  431.6 12.0 %collective-permute-start.45 = (bf16[96,3200]{1,0:T(8,128)(2,1)S(1)}, bf16[96,3200]{1,0:T(8,128)(2,1)S(1)}, u32[]{:S(2)}, u32[]{:S(2)}) collective-permute-start(bf16[96,3200]{1,0:T(8,128)(2,1)S(1)} %add_convert_fusion.10), channel_id=1, source_target_pairs={{1,0},{2,3},{5,4},{6,7},{9,8},{10,11},{13,12},{14,15},{17,16},{18,... | collective-permute-start | bytes 1843208 | tf_op jit(solution)/shard_map/ppermute | solution.py:515
  (37 other events, 244.1 us)
Sparse Core Ops, SparseCore 0:
  269.0 53.6 reduce-scatter.1
where the time goes:
time: 460 us; the launch traced here: 454 us
  waiting for transfers between devices  175 us (38%)
  Pallas kernels  148 us (32%)
  starting transfers between devices  69.1 us (15%)
  other arithmetic  29.7 us (6%)
  local copies, waits for them, and re-layouts  16.8 us (4%)
  between operations  15.1 us (3%)
    pallas_call x2, Pallas kernels, experts_call(): pl.pallas_call(functools.partial(expert_kernel, plan), grid=(groups,), in...  81.2 us
    ppermute x5, waiting for transfers between devices, outwards(): self.moving = lax.ppermute(self.total, 'seq', [(1, 0), (2, 3)])  77 us
    ppermute x5, waiting for transfers between devices, inwards(): self.moving = lax.ppermute(self.raw, 'seq', [(0, 1), (3, 2)])  40.1 us
    pallas_call x2, Pallas kernels, grads_call(): pl.pallas_call(functools.partial(grads_kernel, plan), grid=(many,), in_sp...  30.7 us
    ppermute x26, waiting for transfers between devices, flip(): return lax.ppermute(array, 'fsdp', [(n, n ^ bits) for n in range(fsdp)])  30.6 us
    ppermute x9, waiting for transfers between devices, exchange(): lax.ppermute(pieces[k], 'seq', [(n, n ^ k) for n in range(count)])  27 us
    ppermute x26, starting transfers between devices, flip(): return lax.ppermute(array, 'fsdp', [(n, n ^ bits) for n in range(fsdp)])  22.2 us
    pallas_call x1, Pallas kernels, back(): pl.pallas_call(back_kernel, grid=(images,), in_specs=[split] * 7 + [pl.Bl...  21.3 us
  transfers between devices with their start and end apart: 51, of which 20 were waited for; matrix products, arithmetic and copies ran while one was open for 8% of the time, Pallas kernels for 18%

commit v1 on v0

--- a/solution.py
+++ b/solution.py
@@ -521,6 +521,10 @@
         index = lax.axis_index("seq")
         return jnp.where((index == 0) | (index == 3), self.moving, self.total)
 
+    def hold(self, others):
+        if self.seq == 4:
+            self.moving = tie(self.moving, others)
+
     def waiting(self):
         return [self.moving] if self.seq == 4 else []
 
@@ -753,14 +757,13 @@
     first = Line(seq, finished(*grads_call(two_far, cots, left, dw, 0, 1))[0]).inwards()
     left, dw = tie((left, dw), first.raw)
     parts = grads_call(two_far, cots, left, dw, 1, expert_count - 1)
-    ready = first.across(arrived)
-    lines = [Line(seq, raw) for raw in finished(*tie(parts, ready, arrived))]
+    ready = first.across()
+    lines = [Line(seq, raw) for raw in finished(*tie(parts, ready, arrived[:2]))]
     lines[0].inwards()
     gins = gin_0 + tie(arrived, ready, [line.raw for line in lines])
     lines = [first] + lines
 
     shape4 = (seq, own, span, width)
-    outs = [spread(a, bits=bits) for a, bits in zip(tie(outs, arrived), (2, 4, 6))]
     *grad_tok, dense = back(
         [a.reshape(shape4) for a in gins],
         middle,
@@ -773,8 +776,9 @@
         small,
         dwr,
     )
-    flying = (outs, lines[0].waiting(), lines[1].waiting())
-    dense = tie(dense, flying)
+    flying = (lines[0].waiting(), lines[1].waiting())
+    dense, outs = tie((dense, outs), flying, grad_tok)
+    outs = [spread(a, bits=bits) for a, bits in zip(outs, (2, 4, 6))]
     dense = lax.psum_scatter(dense, "fsdp", scatter_dimension=0, tiled=True)
     lines[2].raw, lines[3].raw = tie((lines[2].raw, lines[3].raw), grad_tok)
     lines[2].inwards()
@@ -783,10 +787,10 @@
     lines[3].inwards()
     ready = lines[2].across(ready)
     ready = lines[1].outwards(ready)
-    ready = lines[3].across(ready)
+    ready = lines[3].across(ready, lines[0].waiting())
     ready = lines[2].outwards(ready)
     dense_line = Line(seq, tie(dense, ready)).inwards()
-    ready = lines[3].outwards(dense_line.raw)
+    ready = lines[3].outwards(dense_line.raw, lines[1].waiting())
 
     ready = dense_line.across(ready)
     outs, grad_tok = tie((outs, grad_tok), ready)
@@ -802,6 +806,7 @@
     outputs, grad_tokens = (
         jnp.concatenate([a[n] for a in home], 0).reshape(images, span, width) for n in range(2)
     )
+    lines[3].hold(dense_line.waiting())
     grads = [line.finish() for line in lines]
     dense = dense_line.finish().astype(f32)
     expert_grads = [jnp.concatenate([g[:, n] for g in grads], 0).astype(f32) for n in range(2)]

time: 460 us -> 472 us (1.026)
  waiting for transfers between devices: 175 us -> 186 us
    ppermute x9, waiting for transfers between devices: 27 us -> 68 us  [exchange(): lax.ppermute(pieces[k], 'seq', [(n, n ^ k) for n in range(count)])]
    ppermute x5, waiting for transfers between devices: 77 us -> 45.8 us  [outwards(): self.moving = lax.ppermute(self.total, 'seq', [(1, 0), (2, 3)])]
    ppermute x5, waiting for transfers between devices: 40.1 us -> 48.2 us  [inwards(): self.moving = lax.ppermute(self.raw, 'seq', [(0, 1), (3, 2)])]
    ppermute x26, waiting for transfers between devices: 30.6 us -> 24.1 us  [flip(): return lax.ppermute(array, 'fsdp', [(n, n ^ bits) for n in range(fsdp)])]
where the time goes in v1:
time: 472 us; the launch traced here: 466 us
  waiting for transfers between devices  186 us (39%)
  Pallas kernels  148 us (31%)
  starting transfers between devices  67 us (14%)
  other arithmetic  31.7 us (7%)
  local copies, waits for them, and re-layouts  17.2 us (4%)
  between operations  15.1 us (3%)
    pallas_call x2, Pallas kernels, experts_call(): pl.pallas_call(functools.partial(expert_kernel, plan), grid=(groups,), in...  81.4 us
    ppermute x9, waiting for transfers between devices, exchange(): lax.ppermute(pieces[k], 'seq', [(n, n ^ k) for n in range(count)])  68 us
    ppermute x5, waiting for transfers between devices, inwards(): self.moving = lax.ppermute(self.raw, 'seq', [(0, 1), (3, 2)])  48.2 us
    ppermute x5, waiting for transfers between devices, outwards(): self.moving = lax.ppermute(self.total, 'seq', [(1, 0), (2, 3)])  45.8 us
    pallas_call x2, Pallas kernels, grads_call(): pl.pallas_call(functools.partial(grads_kernel, plan), grid=(many,), in_sp...  30.6 us
    ppermute x26, waiting for transfers between devices, flip(): return lax.ppermute(array, 'fsdp', [(n, n ^ bits) for n in range(fsdp)])  24.1 us
    ppermute x26, starting transfers between devices, flip(): return lax.ppermute(array, 'fsdp', [(n, n ^ bits) for n in range(fsdp)])  23.2 us
    pallas_call x1, Pallas kernels, back(): pl.pallas_call(back_kernel, grid=(images,), in_specs=[split] * 7 + [pl.Bl...  21.4 us
  transfers between devices with their start and end apart: 51, of which 20 were waited for; matrix products, arithmetic and copies ran while one was open for 8% of the time, Pallas kernels for 18%

profile of v1, /device:TPU:0, one launch (start us, length us, event | category | flops | bytes accessed | tf_op | source)
XLA Modules:
  0.0 465.9 jit_solution(14717376674061618516)
XLA Ops:
  9.4 3.0 collective-permute-start.1
  14.7 3.6 collective-permute-start.4
  21.4 3.2 collective-permute-done.4
  24.6 10.0 %collective-permute-done.3 = bf16[128,768]{1,0:T(8,128)(2,1)S(1)} collective-permute-done((bf16[128,768]{1,0:T(8,128)(2,1)}, bf16[128,768]{1,0:T(8,128)(2,1)S(1)}, u32[]{:S(2)}, u32[]{:S(2)}) %collective-permute-start.3) | collective-permute-done | bytes 196640 | tf_op jit(solution)/shard_map/ppermute | solution.py:477
  35.7 2.5 collective-permute-start.12
  38.2 1.9 collective-permute-start.10
  41.4 4.7 %collective-permute-done.12 = bf16[144,768]{1,0:T(8,128)(2,1)S(1)} collective-permute-done((bf16[144,768]{1,0:T(8,128)(2,1)S(1)}, bf16[144,768]{1,0:T(8,128)(2,1)S(1)}, u32[]{:S(2)}, u32[]{:S(2)}) %collective-permute-start.12) | collective-permute-done | bytes 221216 | tf_op jit(solution)/shard_map/ppermute | solution.py:477
  46.0 9.1 %collective-permute-done.11 = bf16[144,768]{1,0:T(8,128)(2,1)S(1)} collective-permute-done((bf16[144,768]{1,0:T(8,128)(2,1)S(1)}, bf16[144,768]{1,0:T(8,128)(2,1)S(1)}, u32[]{:S(2)}, u32[]{:S(2)}) %collective-permute-start.11) | collective-permute-done | bytes 221216 | tf_op jit(solution)/shard_map/ppermute | solution.py:477
  56.4 2.1 collective-permute-done.13.refs_8_
  64.0 15.0 %front.1 = (f32[4,2,64,768]{3,2,1,0:T(8,128)}, bf16[4,2,64,768]{3,2,1,0:T(8,128)(2,1)}, bf16[2,256,2304]{2,1,0:T(8,128)(2,1)}, bf16[2,256,768]{2,1,0:T(8,128)(2,...) custom-call(bf16[96,3200]{1,0:T(8,128)(2,1)} %copy-done.3, ...), custom_call_target="tpu_custom_call" | custom-call | flops 1000 | bytes 1000 | tf_op jit(solution)/shard_map/front/pallas_call | solution.py:124
  79.0 2.5 collective-permute-start.19
  84.7 1.5 collective-permute-start.23
  86.2 1.5 collective-permute-start.22
  87.7 27.4 %experts_own.1 = (bf16[4,2,768,768]{3,2,1,0:T(8,128)(2,1)}, f32[8,768]{1,0:T(8,128)}, bf16[4,128,768]{2,1,0:T(8,128)(2,1)}, bf16[4,128,768]{2,1,0:T(8,128)(2,1)}) custom-call(bf16[4,128,768]{2,1,0:T(8,128)(2,1)} %bitcast.101, bf16[4,144,768]{2,1,0:T(8,128)(2,1)} %copy-done, bf16[4,384,768]{2,1,0:T(8,128)(2,1)} %refs_7_, bf16[4,384,768]{2,1,0:T(8,128)(2,1)} %copy-done.7, ...), custom_call_target="tpu_custom_call" | custom-call | flops 1000 | bytes 1000 | tf_op jit(solution)/shard_map/experts_own/pallas_call | solution.py:357
  117.7 7.9 %collective-permute-done.23.refs_6_ = bf16[2,144,768]{2,1,0:T(8,128)(2,1)S(1)} collective-permute-done((bf16[2,144,768]{2,1,0:T(8,128)(2,1)S(1)}, bf16[2,144,768]{2,1,0:T(8,128)(2,1)S(1)}, u32[]{:S(2)}, u32[]{:S(2)}) %collective-permute-start.23) | collective-permute-done | bytes 442400 | tf_op jit(solution)/shard_map/ppermute | solution.py:467
  126.4 54.0 %experts_far.1 = (bf16[1536,3072]{1,0:T(8,128)(2,1)}, bf16[1536,3072]{1,0:T(8,128)(2,1)}, f32[8,768]{1,0:T(8,128)}, bf16[4,128,768]{2,1,0:T(8,128)(2,1)}, bf16[4...) custom-call(bf16[4,128,768]{2,1,0:T(8,128)(2,1)} %collective-permute, ...), custom_call_target="tpu_custom_call" | custom-call | flops 72477573120 | bytes 16777216 | tf_op jit(solution)/shard_map/experts_far/pallas_call | solution.py:357
  180.4 10.8 %expert_grads.2 = (bf16[1,2,384,768]{3,2,1,0:T(8,128)(2,1)}, bf16[1,2,384,768]{3,2,1,0:T(8,128)(2,1)}) custom-call(bf16[4,128,768]{2,1,0:T(8,128)(2,1)} %collective-permute-done.17.refs_0_, bf16[4,128,768]{2,1,0:T(8,128)(2,1)} %collective-permute-done.18.refs_1_, bf16[4,128,768]{2,1,0:T(8,128)(2,1)} %collective-permute-done.19.refs_2_, ...), custom_call_target="tpu_custom_call" | custom-call | flops 14495514624 | bytes 16777216 | tf_op jit(solution)/shard_map/expert_grads/pallas_call | solution.py:447
  191.2 1.6 collective-permute-start.24
  194.3 1.6 add_convert_fusion.9
  197.2 19.9 %expert_grads.3 = (bf16[3,2,384,768]{3,2,1,0:T(8,128)(2,1)}, bf16[3,2,384,768]{3,2,1,0:T(8,128)(2,1)}) custom-call(bf16[4,128,768]{2,1,0:T(8,128)(2,1)} %collective-permute-done.17.refs_0_, bf16[4,128,768]{2,1,0:T(8,128)(2,1)} %collective-permute-done.18.refs_1_, bf16[4,128,768]{2,1,0:T(8,128)(2,1)} %collective-permute-done.19.refs_2_, ...), custom_call_target="tpu_custom_call" | custom-call | flops 43486543872 | bytes 16777216 | tf_op jit(solution)/shard_map/expert_grads/pallas_call | solution.py:447
  217.1 5.8 %collective-permute-done.28 = bf16[1,2,384,768]{3,2,1,0:T(8,128)(2,1)S(1)} collective-permute-done((bf16[1,2,384,768]{3,2,1,0:T(8,128)(2,1)S(1)}, bf16[1,2,384,768]{3,2,1,0:T(8,128)(2,1)S(1)}, u32[]{:S(2)}, u32[]{:S(2)}) %collective-permute-start.28) | collective-permute-done | bytes 1179680 | tf_op jit(solution)/shard_map/ppermute | solution.py:502
  224.3 1.7 collective-permute-start.26
  226.0 1.7 collective-permute-start.30
  227.7 2.1 collective-permute-done.29
  232.0 5.4 %collective-permute-start.31 = (bf16[1,2,384,768]{3,2,1,0:T(8,128)(2,1)S(1)}, bf16[1,2,384,768]{3,2,1,0:T(8,128)(2,1)}, u32[]{:S(2)}, u32[]{:S(2)}) collective-permute-start(bf16[1,2,384,768]{3,2,1,0:T(8,128)(2,1)S(1)} %get-tuple-element.115), channel_id=1, source_target_pairs={{0,1},{3,2},{4,5},{7,6},{8,9},{11,10},{12,13},{15,14},{16,17},{19,... | collective-permute-start | bytes 3538952 | tf_op jit(solution)/shard_map/ppermute | solution.py:502
  237.4 8.0 %collective-permute-done.26 = bf16[4,128,768]{2,1,0:T(8,128)(2,1)} collective-permute-done((bf16[4,128,768]{2,1,0:T(8,128)(2,1)}, bf16[4,128,768]{2,1,0:T(8,128)(2,1)}, u32[]{:S(2)}, u32[]{:S(2)}) %collective-permute-start.26) | collective-permute-done | bytes 786464 | tf_op jit(solution)/shard_map/ppermute | solution.py:467
  245.4 21.4 %back.1 = (bf16[2,64,768]{2,1,0:T(8,128)(2,1)}, bf16[2,64,768]{2,1,0:T(8,128)(2,1)}, bf16[2,64,768]{2,1,0:T(8,128)(2,1)}, bf16[2,64,768]{2,1,0:T(8,128)(2,1)}, bf16[768,3200]{1,0:T(8,128)(2,1)}) custom-call(bf16[4,2,64,768]{3,2,1,0:T(8,128)(2,1)} %bitcast.129, bf16[4,2,64,768]{3,2,1,0:T(8,128)(2,1)} %bitcast.32.gin_2, ...), custom_call_target="tpu_custom_call" | custom-call | flops 30198988800 | bytes 16777216 | tf_op jit(solution)/shard_map/back/pallas_call | solution.py:605
  266.9 4.5 collective-permute-start.35
  272.7 1.6 add_convert_fusion.7
  275.0 1.6 add_convert_fusion.6
  277.9 19.7 %collective-permute-done.35 = bf16[1,2,384,768]{3,2,1,0:T(8,128)(2,1)S(1)} collective-permute-done((bf16[1,2,384,768]{3,2,1,0:T(8,128)(2,1)S(1)}, bf16[1,2,384,768]{3,2,1,0:T(8,128)(2,1)S(1)}, u32[]{:S(2)}, u32[]{:S(2)}) %collective-permute-start.35) | collective-permute-done | bytes 1179680 | tf_op jit(solution)/shard_map/ppermute | solution.py:502
  299.0 22.7 %collective-permute-done.37 = bf16[1,2,384,768]{3,2,1,0:T(8,128)(2,1)S(1)} collective-permute-done((bf16[1,2,384,768]{3,2,1,0:T(8,128)(2,1)}, bf16[1,2,384,768]{3,2,1,0:T(8,128)(2,1)S(1)}, u32[]{:S(2)}, u32[]{:S(2)}) %collective-permute-start.37) | collective-permute-done | bytes 1179680 | tf_op jit(solution)/shard_map/ppermute | solution.py:502
  321.7 2.0 add_convert_fusion.3
  326.4 1.7 collective-permute-start.41
  329.4 1.6 collective-permute-start.32
  334.0 24.0 %collective-permute-done.48 = bf16[1,2,384,768]{3,2,1,0:T(8,128)(2,1)} collective-permute-done((bf16[1,2,384,768]{3,2,1,0:T(8,128)(2,1)}, bf16[1,2,384,768]{3,2,1,0:T(8,128)(2,1)}, u32[]{:S(2)}, u32[]{:S(2)}) %collective-permute-start.48) | collective-permute-done | bytes 1179680 | tf_op jit(solution)/shard_map/ppermute | solution.py:515
  358.0 1.7 collective-permute-start.40
  362.6 1.7 collective-permute-start.34
  364.3 15.4 %collective-permute-done.42 = bf16[1,2,384,768]{3,2,1,0:T(8,128)(2,1)} collective-permute-done((bf16[1,2,384,768]{3,2,1,0:T(8,128)(2,1)S(1)}, bf16[1,2,384,768]{3,2,1,0:T(8,128)(2,1)}, u32[]{:S(2)}, u32[]{:S(2)}) %collective-permute-start.42) | collective-permute-done | bytes 1179680 | tf_op jit(solution)/shard_map/ppermute | solution.py:515
  379.7 2.6 add_convert_fusion.1
  384.6 1.9 convert_add_fusion
  387.6 5.9 %collective-permute-start.43 = (bf16[2,2,64,768]{3,2,1,0:T(8,128)(2,1)S(1)}, bf16[2,2,64,768]{3,2,1,0:T(8,128)(2,1)S(1)}, u32[]{:S(2)}, u32[]{:S(2)}) collective-permute-start(bf16[2,2,64,768]{3,2,1,0:T(8,128)(2,1)S(1)} %pad_maximum_fusion.5), channel_id=1, source_target_pairs={{0,1},{1,0},{2,3},{3,2},{4,5},{5,4},{6,7},{7,6},{8,9},{9,8},{10,11... | collective-permute-start | bytes 1179656 | tf_op jit(solution)/shard_map/ppermute | solution.py:477
  394.2 1.9 collective-permute-start.45
  397.6 41.1 %collective-permute-done.43 = bf16[2,2,64,768]{3,2,1,0:T(8,128)(2,1)S(1)} collective-permute-done((bf16[2,2,64,768]{3,2,1,0:T(8,128)(2,1)S(1)}, bf16[2,2,64,768]{3,2,1,0:T(8,128)(2,1)S(1)}, u32[]{:S(2)}, u32[]{:S(2)}) %collective-permute-start.43) | collective-permute-done | bytes 393248 | tf_op jit(solution)/shard_map/ppermute | solution.py:477
  440.9 6.4 %collective-permute-done.47 = bf16[96,3200]{1,0:T(8,128)(2,1)S(1)} collective-permute-done((bf16[96,3200]{1,0:T(8,128)(2,1)S(1)}, bf16[96,3200]{1,0:T(8,128)(2,1)S(1)}, u32[]{:S(2)}, u32[]{:S(2)}) %collective-permute-start.47) | collective-permute-done | bytes 614432 | tf_op jit(solution)/shard_map/ppermute | solution.py:515
  450.5 1.9 broadcast_select_fusion
  453.7 2.6 maximum_convert_fusion.1
  456.3 2.6 maximum_convert_fusion
  (201 shorter events, 56.1 us)
Async XLA Ops:
  7.2 326.8 %reduce-scatter.2.cloned.1.call-start = ((), (), s32[]{:S(2)}) async-start(), calls=%async_computation.1 | async-start | bytes 5529600 | tf_op jit(solution)/shard_map/reduce_scatter | solution.py:782
  9.4 26.3 %collective-permute-start.1 = (bf16[96,3200]{1,0:T(8,128)(2,1)S(1)}, bf16[96,3200]{1,0:T(8,128)(2,1)S(1)}, u32[]{:S(2)}, u32[]{:S(2)}) collective-permute-start(bf16[96,3200]{1,0:T(8,128)(2,1)S(1)} %fusion.5.refs_0_), channel_id=1, source_target_pairs={{0,16},{4,20},{8,24},{12,28},{16,0},{20,4},{24,8},{28,12},{1,17},{... | collective-permute-start | bytes 1843208 | tf_op jit(solution)/shard_map/ppermute | solution.py:467
  12.4 23.2 %collective-permute-start = (bf16[96,3200]{1,0:T(8,128)(2,1)S(1)}, bf16[96,3200]{1,0:T(8,128)(2,1)S(1)}, u32[]{:S(2)}, u32[]{:S(2)}) collective-permute-start(bf16[96,3200]{1,0:T(8,128)(2,1)S(1)} %fusion.5.refs_0_), channel_id=1, source_target_pairs={{0,8},{4,12},{8,0},{12,4},{16,24},{20,28},{24,16},{28,20},{1,9},{5... | collective-permute-start | bytes 1843208 | tf_op jit(solution)/shard_map/ppermute | solution.py:467
  14.7 9.9 %collective-permute-start.4 = (bf16[128,768]{1,0:T(8,128)(2,1)}, bf16[128,768]{1,0:T(8,128)(2,1)S(1)}, u32[]{:S(2)}, u32[]{:S(2)}) collective-permute-start(bf16[128,768]{1,0:T(8,128)(2,1)} %get-tuple-element.236), channel_id=1, source_target_pairs={{0,3},{1,2},{2,1},{3,0},{4,7},{5,6},{6,5},{7,4},{8,11},{9,10},{10,... | collective-permute-start | bytes 589832 | tf_op jit(solution)/shard_map/ppermute | solution.py:477
  18.3 16.3 %collective-permute-start.3 = (bf16[128,768]{1,0:T(8,128)(2,1)}, bf16[128,768]{1,0:T(8,128)(2,1)S(1)}, u32[]{:S(2)}, u32[]{:S(2)}) collective-permute-start(bf16[128,768]{1,0:T(8,128)(2,1)} %get-tuple-element.237), channel_id=1, source_target_pairs={{0,2},{1,3},{2,0},{3,1},{4,6},{5,7},{6,4},{7,5},{8,10},{9,11},{10,... | collective-permute-start | bytes 589832 | tf_op jit(solution)/shard_map/ppermute | solution.py:477
  18.3 16.3 %collective-permute-start.2 = (bf16[128,768]{1,0:T(8,128)(2,1)S(1)}, bf16[128,768]{1,0:T(8,128)(2,1)S(1)}, u32[]{:S(2)}, u32[]{:S(2)}) collective-permute-start(bf16[128,768]{1,0:T(8,128)(2,1)S(1)} %get-tuple-element.238), channel_id=1, source_target_pairs={{0,1},{1,0},{2,3},{3,2},{4,5},{5,4},{6,7},{7,6},{8,9},{9,8},{10,11... | collective-permute-start | bytes 589832 | tf_op jit(solution)/shard_map/ppermute | solution.py:477
  35.7 10.3 %collective-permute-start.12 = (bf16[144,768]{1,0:T(8,128)(2,1)S(1)}, bf16[144,768]{1,0:T(8,128)(2,1)S(1)}, u32[]{:S(2)}, u32[]{:S(2)}) collective-permute-start(bf16[144,768]{1,0:T(8,128)(2,1)S(1)} %get-tuple-element.232), channel_id=1, source_target_pairs={{0,3},{1,2},{2,1},{3,0},{4,7},{5,6},{6,5},{7,4},{8,11},{9,10},{10,... | collective-permute-start | bytes 663560 | tf_op jit(solution)/shard_map/ppermute | solution.py:477
  38.2 16.9 %collective-permute-start.11 = (bf16[144,768]{1,0:T(8,128)(2,1)S(1)}, bf16[144,768]{1,0:T(8,128)(2,1)S(1)}, u32[]{:S(2)}, u32[]{:S(2)}) collective-permute-start(bf16[144,768]{1,0:T(8,128)(2,1)S(1)} %get-tuple-element.233), channel_id=1, source_target_pairs={{0,2},{1,3},{2,0},{3,1},{4,6},{5,7},{6,4},{7,5},{8,10},{9,11},{10,... | collective-permute-start | bytes 663560 | tf_op jit(solution)/shard_map/ppermute | solution.py:477
  38.2 16.9 %collective-permute-start.10 = (bf16[144,768]{1,0:T(8,128)(2,1)S(1)}, bf16[144,768]{1,0:T(8,128)(2,1)S(1)}, u32[]{:S(2)}, u32[]{:S(2)}) collective-permute-start(bf16[144,768]{1,0:T(8,128)(2,1)S(1)} %get-tuple-element.234), channel_id=1, source_target_pairs={{0,1},{1,0},{2,3},{3,2},{4,5},{5,4},{6,7},{7,6},{8,9},{9,8},{10,11... | collective-permute-start | bytes 663560 | tf_op jit(solution)/shard_map/ppermute | solution.py:477
  40.2 15.6 %collective-permute-start.9 = (bf16[48,3200]{1,0:T(8,128)(2,1)S(1)}, bf16[48,3200]{1,0:T(8,128)(2,1)S(1)}, u32[]{:S(2)}, u32[]{:S(2)}) collective-permute-start(bf16[48,3200]{1,0:T(8,128)(2,1)S(1)} %slice.204), channel_id=1, source_target_pairs={{0,8},{4,12},{8,0},{12,4},{16,24},{20,28},{24,16},{28,20},{1,9},{5... | collective-permute-start | bytes 921608 | tf_op jit(solution)/shard_map/ppermute | solution.py:467
  40.8 15.0 %collective-permute-start.8 = (bf16[48,3200]{1,0:T(8,128)(2,1)S(1)}, bf16[48,3200]{1,0:T(8,128)(2,1)S(1)}, u32[]{:S(2)}, u32[]{:S(2)}) collective-permute-start(bf16[48,3200]{1,0:T(8,128)(2,1)S(1)} %slice.203), channel_id=1, source_target_pairs={{0,16},{4,20},{8,24},{12,28},{16,0},{20,4},{24,8},{28,12},{1,17},{... | collective-permute-start | bytes 921608 | tf_op jit(solution)/shard_map/ppermute | solution.py:467
  46.0 10.4 %collective-permute-start.5 = (bf16[96,3200]{1,0:T(8,128)(2,1)S(1)}, bf16[96,3200]{1,0:T(8,128)(2,1)S(1)}, u32[]{:S(2)}, u32[]{:S(2)}) collective-permute-start(bf16[96,3200]{1,0:T(8,128)(2,1)S(1)} %fusion.5.refs_0_), channel_id=1, source_target_pairs={{0,4},{4,0},{8,12},{12,8},{16,20},{20,16},{24,28},{28,24},{1,5},{5... | collective-permute-start | bytes 1843208 | tf_op jit(solution)/shard_map/ppermute | solution.py:467
  55.1 3.8 collective-permute-start.6
  55.2 3.8 collective-permute-start.7
  59.0 25.7 %collective-permute-start.15 = (bf16[4,384,768]{2,1,0:T(8,128)(2,1)}, bf16[4,384,768]{2,1,0:T(8,128)(2,1)S(1)}, u32[]{:S(2)}, u32[]{:S(2)}) collective-permute-start(bf16[4,384,768]{2,1,0:T(8,128)(2,1)} %refs_7_), channel_id=1, source_target_pairs={{0,4},{4,0},{8,12},{12,8},{16,20},{20,16},{24,28},{28,24},{1,5},{5... | collective-permute-start | bytes 7077896 | tf_op jit(solution)/shard_map/ppermute | solution.py:467
  59.2 27.0 %collective-permute-start.16 = (bf16[4,384,768]{2,1,0:T(8,128)(2,1)}, bf16[4,384,768]{2,1,0:T(8,128)(2,1)}, u32[]{:S(2)}, u32[]{:S(2)}) collective-permute-start(bf16[4,384,768]{2,1,0:T(8,128)(2,1)} %refs_9_), channel_id=1, source_target_pairs={{0,4},{4,0},{8,12},{12,8},{16,20},{20,16},{24,28},{28,24},{1,5},{5... | collective-permute-start | bytes 7077896 | tf_op jit(solution)/shard_map/ppermute | solution.py:467
  59.5 21.9 %collective-permute-start.21 = (bf16[4,144,768]{2,1,0:T(8,128)(2,1)S(1)}, bf16[4,144,768]{2,1,0:T(8,128)(2,1)}, u32[]{:S(2)}, u32[]{:S(2)}) collective-permute-start(bf16[4,144,768]{2,1,0:T(8,128)(2,1)S(1)} %pad_maximum_fusion.refs_1_), channel_id=1, source_target_pairs={{0,16},{4,20},{8,24},{12,28},{16,0},{20,4},{24,8},{28,12},{1,17},{... | collective-permute-start | bytes 2654216 | tf_op jit(solution)/shard_map/ppermute | solution.py:467
  60.1 21.9 %collective-permute-start.20 = (bf16[4,144,768]{2,1,0:T(8,128)(2,1)S(1)}, bf16[4,144,768]{2,1,0:T(8,128)(2,1)}, u32[]{:S(2)}, u32[]{:S(2)}) collective-permute-start(bf16[4,144,768]{2,1,0:T(8,128)(2,1)S(1)} %pad_maximum_fusion.refs_1_), channel_id=1, source_target_pairs={{0,8},{4,12},{8,0},{12,4},{16,24},{20,28},{24,16},{28,20},{1,9},{5... | collective-permute-start | bytes 2654216 | tf_op jit(solution)/shard_map/ppermute | solution.py:467
  79.0 36.1 %collective-permute-start.19 = (bf16[4,128,768]{2,1,0:T(8,128)(2,1)}, bf16[4,128,768]{2,1,0:T(8,128)(2,1)}, u32[]{:S(2)}, u32[]{:S(2)}) collective-permute-start(bf16[4,128,768]{2,1,0:T(8,128)(2,1)} %bitcast.98), channel_id=1, source_target_pairs={{0,24},{4,28},{8,16},{12,20},{16,8},{20,12},{24,0},{28,4},{1,25},{... | collective-permute-start | bytes 2359304 | tf_op jit(solution)/shard_map/ppermute | solution.py:467
  81.5 35.0 %collective-permute-start.18 = (bf16[4,128,768]{2,1,0:T(8,128)(2,1)}, bf16[4,128,768]{2,1,0:T(8,128)(2,1)}, u32[]{:S(2)}, u32[]{:S(2)}) collective-permute-start(bf16[4,128,768]{2,1,0:T(8,128)(2,1)} %bitcast.99), channel_id=1, source_target_pairs={{0,16},{4,20},{8,24},{12,28},{16,0},{20,4},{24,8},{28,12},{1,17},{... | collective-permute-start | bytes 2359304 | tf_op jit(solution)/shard_map/ppermute | solution.py:467
  82.0 35.7 %collective-permute-start.17 = (bf16[4,128,768]{2,1,0:T(8,128)(2,1)}, bf16[4,128,768]{2,1,0:T(8,128)(2,1)}, u32[]{:S(2)}, u32[]{:S(2)}) collective-permute-start(bf16[4,128,768]{2,1,0:T(8,128)(2,1)} %bitcast.100), channel_id=1, source_target_pairs={{0,8},{4,12},{8,0},{12,4},{16,24},{20,28},{24,16},{28,20},{1,9},{5... | collective-permute-start | bytes 2359304 | tf_op jit(solution)/shard_map/ppermute | solution.py:467
  84.7 40.9 %collective-permute-start.23 = (bf16[2,144,768]{2,1,0:T(8,128)(2,1)S(1)}, bf16[2,144,768]{2,1,0:T(8,128)(2,1)S(1)}, u32[]{:S(2)}, u32[]{:S(2)}) collective-permute-start(bf16[2,144,768]{2,1,0:T(8,128)(2,1)S(1)} %slice.267), channel_id=1, source_target_pairs={{0,8},{4,12},{8,0},{12,4},{16,24},{20,28},{24,16},{28,20},{1,9},{5... | collective-permute-start | bytes 1327112 | tf_op jit(solution)/shard_map/ppermute | solution.py:467
  86.2 39.7 %collective-permute-start.22 = (bf16[2,144,768]{2,1,0:T(8,128)(2,1)S(1)}, bf16[2,144,768]{2,1,0:T(8,128)(2,1)}, u32[]{:S(2)}, u32[]{:S(2)}) collective-permute-start(bf16[2,144,768]{2,1,0:T(8,128)(2,1)S(1)} %slice.266), channel_id=1, source_target_pairs={{0,16},{4,20},{8,24},{12,28},{16,0},{20,4},{24,8},{28,12},{1,17},{... | collective-permute-start | bytes 1327112 | tf_op jit(solution)/shard_map/ppermute | solution.py:467
  191.2 32.0 %collective-permute-start.24 = (bf16[4,128,768]{2,1,0:T(8,128)(2,1)}, bf16[4,128,768]{2,1,0:T(8,128)(2,1)}, u32[]{:S(2)}, u32[]{:S(2)}) collective-permute-start(bf16[4,128,768]{2,1,0:T(8,128)(2,1)} %get-tuple-element.100), channel_id=1, source_target_pairs={{0,8},{4,12},{8,0},{12,4},{16,24},{20,28},{24,16},{28,20},{1,9},{5... | collective-permute-start | bytes 2359304 | tf_op jit(solution)/shard_map/ppermute | solution.py:467
  192.8 30.5 %collective-permute-start.25 = (bf16[4,128,768]{2,1,0:T(8,128)(2,1)}, bf16[4,128,768]{2,1,0:T(8,128)(2,1)}, u32[]{:S(2)}, u32[]{:S(2)}) collective-permute-start(bf16[4,128,768]{2,1,0:T(8,128)(2,1)} %get-tuple-element.101), channel_id=1, source_target_pairs={{0,16},{4,20},{8,24},{12,28},{16,0},{20,4},{24,8},{28,12},{1,17},{... | collective-permute-start | bytes 2359304 | tf_op jit(solution)/shard_map/ppermute | solution.py:467
  195.9 27.1 %collective-permute-start.28 = (bf16[1,2,384,768]{3,2,1,0:T(8,128)(2,1)S(1)}, bf16[1,2,384,768]{3,2,1,0:T(8,128)(2,1)S(1)}, u32[]{:S(2)}, u32[]{:S(2)}) collective-permute-start(bf16[1,2,384,768]{3,2,1,0:T(8,128)(2,1)S(1)} %add_convert_fusion.9), channel_id=1, source_target_pairs={{0,1},{3,2},{4,5},{7,6},{8,9},{11,10},{12,13},{15,14},{16,17},{19,... | collective-permute-start | bytes 3538952 | tf_op jit(solution)/shard_map/ppermute | solution.py:502
  223.3 6.5 %collective-permute-start.29 = (bf16[3,2,384,768]{3,2,1,0:T(8,128)(2,1)}, bf16[3,2,384,768]{3,2,1,0:T(8,128)(2,1)S(1)}, u32[]{:S(2)}, u32[]{:S(2)}) collective-permute-start(bf16[3,2,384,768]{3,2,1,0:T(8,128)(2,1)} %get-tuple-element.114), channel_id=1, source_target_pairs={{0,4},{4,0},{8,12},{12,8},{16,20},{20,16},{24,28},{28,24},{1,5},{5... | collective-permute-start | bytes 10616840 | tf_op jit(solution)/shard_map/ppermute | solution.py:467
  224.3 21.2 %collective-permute-start.26 = (bf16[4,128,768]{2,1,0:T(8,128)(2,1)}, bf16[4,128,768]{2,1,0:T(8,128)(2,1)}, u32[]{:S(2)}, u32[]{:S(2)}) collective-permute-start(bf16[4,128,768]{2,1,0:T(8,128)(2,1)} %get-tuple-element.102), channel_id=1, source_target_pairs={{0,24},{4,28},{8,16},{12,20},{16,8},{20,12},{24,0},{28,4},{1,25},{... | collective-permute-start | bytes 2359304 | tf_op jit(solution)/shard_map/ppermute | solution.py:467
  226.0 40.8 %collective-permute-start.30 = (bf16[1,2,384,768]{3,2,1,0:T(8,128)(2,1)S(1)}, bf16[1,2,384,768]{3,2,1,0:T(8,128)(2,1)}, u32[]{:S(2)}, u32[]{:S(2)}) collective-permute-start(bf16[1,2,384,768]{3,2,1,0:T(8,128)(2,1)S(1)} %add_convert_fusion.8), channel_id=1, source_target_pairs={{1,2},{2,1},{5,6},{6,5},{9,10},{10,9},{13,14},{14,13},{17,18},{18,... | collective-permute-start | bytes 3538952 | tf_op jit(solution)/shard_map/ppermute | solution.py:508
  232.0 34.9 %collective-permute-start.31 = (bf16[1,2,384,768]{3,2,1,0:T(8,128)(2,1)S(1)}, bf16[1,2,384,768]{3,2,1,0:T(8,128)(2,1)}, u32[]{:S(2)}, u32[]{:S(2)}) collective-permute-start(bf16[1,2,384,768]{3,2,1,0:T(8,128)(2,1)S(1)} %get-tuple-element.115), channel_id=1, source_target_pairs={{0,1},{3,2},{4,5},{7,6},{8,9},{11,10},{12,13},{15,14},{16,17},{19,... | collective-permute-start | bytes 3538952 | tf_op jit(solution)/shard_map/ppermute | solution.py:502
  266.9 30.8 %collective-permute-start.35 = (bf16[1,2,384,768]{3,2,1,0:T(8,128)(2,1)S(1)}, bf16[1,2,384,768]{3,2,1,0:T(8,128)(2,1)S(1)}, u32[]{:S(2)}, u32[]{:S(2)}) collective-permute-start(bf16[1,2,384,768]{3,2,1,0:T(8,128)(2,1)S(1)} %get-tuple-element.139), channel_id=1, source_target_pairs={{0,1},{3,2},{4,5},{7,6},{8,9},{11,10},{12,13},{15,14},{16,17},{19,... | collective-permute-start | bytes 3538952 | tf_op jit(solution)/shard_map/ppermute | solution.py:502
  271.3 50.4 %collective-permute-start.37 = (bf16[1,2,384,768]{3,2,1,0:T(8,128)(2,1)}, bf16[1,2,384,768]{3,2,1,0:T(8,128)(2,1)S(1)}, u32[]{:S(2)}, u32[]{:S(2)}) collective-permute-start(bf16[1,2,384,768]{3,2,1,0:T(8,128)(2,1)} %get-tuple-element.143), channel_id=1, source_target_pairs={{0,1},{3,2},{4,5},{7,6},{8,9},{11,10},{12,13},{15,14},{16,17},{19,... | collective-permute-start | bytes 3538952 | tf_op jit(solution)/shard_map/ppermute | solution.py:502
  274.3 24.4 %collective-permute-start.38 = (bf16[1,2,384,768]{3,2,1,0:T(8,128)(2,1)S(1)}, bf16[1,2,384,768]{3,2,1,0:T(8,128)(2,1)S(1)}, u32[]{:S(2)}, u32[]{:S(2)}) collective-permute-start(bf16[1,2,384,768]{3,2,1,0:T(8,128)(2,1)S(1)} %add_convert_fusion.7), channel_id=1, source_target_pairs={{1,2},{2,1},{5,6},{6,5},{9,10},{10,9},{13,14},{14,13},{17,18},{18,... | collective-permute-start | bytes 3538952 | tf_op jit(solution)/shard_map/ppermute | solution.py:508
  276.6 45.1 %collective-permute-start.39 = (bf16[1,2,384,768]{3,2,1,0:T(8,128)(2,1)S(1)}, bf16[1,2,384,768]{3,2,1,0:T(8,128)(2,1)S(1)}, u32[]{:S(2)}, u32[]{:S(2)}) collective-permute-start(bf16[1,2,384,768]{3,2,1,0:T(8,128)(2,1)S(1)} %add_convert_fusion.6), channel_id=1, source_target_pairs={{1,0},{2,3},{5,4},{6,7},{9,8},{10,11},{13,12},{14,15},{17,16},{18,... | collective-permute-start | bytes 3538952 | tf_op jit(solution)/shard_map/ppermute | solution.py:515
  297.9 25.8 %collective-permute-start.36 = (bf16[1,2,384,768]{3,2,1,0:T(8,128)(2,1)S(1)}, bf16[1,2,384,768]{3,2,1,0:T(8,128)(2,1)S(1)}, u32[]{:S(2)}, u32[]{:S(2)}) collective-permute-start(bf16[1,2,384,768]{3,2,1,0:T(8,128)(2,1)S(1)} %add_convert_fusion.5), channel_id=1, source_target_pairs={{1,2},{2,1},{5,6},{6,5},{9,10},{10,9},{13,14},{14,13},{17,18},{18,... | collective-permute-start | bytes 3538952 | tf_op jit(solution)/shard_map/ppermute | solution.py:508
  325.1 33.0 %collective-permute-start.48 = (bf16[1,2,384,768]{3,2,1,0:T(8,128)(2,1)}, bf16[1,2,384,768]{3,2,1,0:T(8,128)(2,1)}, u32[]{:S(2)}, u32[]{:S(2)}) collective-permute-start(bf16[1,2,384,768]{3,2,1,0:T(8,128)(2,1)} %add_convert_fusion.2), channel_id=1, source_target_pairs={{1,0},{2,3},{5,4},{6,7},{9,8},{10,11},{13,12},{14,15},{17,16},{18,... | collective-permute-start | bytes 3538952 | tf_op jit(solution)/shard_map/ppermute | solution.py:515
  326.4 35.9 %collective-permute-start.41 = (bf16[1,2,384,768]{3,2,1,0:T(8,128)(2,1)S(1)}, bf16[1,2,384,768]{3,2,1,0:T(8,128)(2,1)}, u32[]{:S(2)}, u32[]{:S(2)}) collective-permute-start(bf16[1,2,384,768]{3,2,1,0:T(8,128)(2,1)S(1)} %add_convert_fusion.3), channel_id=1, source_target_pairs={{1,2},{2,1},{5,6},{6,5},{9,10},{10,9},{13,14},{14,13},{17,18},{18,... | collective-permute-start | bytes 3538952 | tf_op jit(solution)/shard_map/ppermute | solution.py:508
  328.1 51.6 %collective-permute-start.42 = (bf16[1,2,384,768]{3,2,1,0:T(8,128)(2,1)S(1)}, bf16[1,2,384,768]{3,2,1,0:T(8,128)(2,1)}, u32[]{:S(2)}, u32[]{:S(2)}) collective-permute-start(bf16[1,2,384,768]{3,2,1,0:T(8,128)(2,1)S(1)} %add_convert_fusion.4), channel_id=1, source_target_pairs={{1,0},{2,3},{5,4},{6,7},{9,8},{10,11},{13,12},{14,15},{17,16},{18,... | collective-permute-start | bytes 3538952 | tf_op jit(solution)/shard_map/ppermute | solution.py:515
  329.4 55.2 %collective-permute-start.32 = (bf16[4,128,768]{2,1,0:T(8,128)(2,1)}, bf16[4,128,768]{2,1,0:T(8,128)(2,1)}, u32[]{:S(2)}, u32[]{:S(2)}) collective-permute-start(bf16[4,128,768]{2,1,0:T(8,128)(2,1)} %get-tuple-element.135), channel_id=1, source_target_pairs={{0,8},{4,12},{8,0},{12,4},{16,24},{20,28},{24,16},{28,20},{1,9},{5... | collective-permute-start | bytes 2359304 | tf_op jit(solution)/shard_map/ppermute | solution.py:467
  330.9 53.6 %collective-permute-start.33 = (bf16[4,128,768]{2,1,0:T(8,128)(2,1)}, bf16[4,128,768]{2,1,0:T(8,128)(2,1)}, u32[]{:S(2)}, u32[]{:S(2)}) collective-permute-start(bf16[4,128,768]{2,1,0:T(8,128)(2,1)} %get-tuple-element.136), channel_id=1, source_target_pairs={{0,16},{4,20},{8,24},{12,28},{16,0},{20,4},{24,8},{28,12},{1,17},{... | collective-permute-start | bytes 2359304 | tf_op jit(solution)/shard_map/ppermute | solution.py:467
  358.0 25.6 %collective-permute-start.40 = (bf16[96,3200]{1,0:T(8,128)(2,1)}, bf16[96,3200]{1,0:T(8,128)(2,1)S(1)}, u32[]{:S(2)}, u32[]{:S(2)}) collective-permute-start(bf16[96,3200]{1,0:T(8,128)(2,1)} %reduce-scatter.2.cloned.1.call-done), channel_id=1, source_target_pairs={{0,1},{3,2},{4,5},{7,6},{8,9},{11,10},{12,13},{15,14},{16,17},{19,... | collective-permute-start | bytes 1843208 | tf_op jit(solution)/shard_map/ppermute | solution.py:502
  362.6 22.0 %collective-permute-start.34 = (bf16[4,128,768]{2,1,0:T(8,128)(2,1)S(1)}, bf16[4,128,768]{2,1,0:T(8,128)(2,1)S(1)}, u32[]{:S(2)}, u32[]{:S(2)}) collective-permute-start(bf16[4,128,768]{2,1,0:T(8,128)(2,1)S(1)} %copy-done.33), channel_id=1, source_target_pairs={{0,24},{4,28},{8,16},{12,20},{16,8},{20,12},{24,0},{28,4},{1,25},{... | collective-permute-start | bytes 2359304 | tf_op jit(solution)/shard_map/ppermute | solution.py:467
  382.2 68.3 %collective-permute-start.49 = (bf16[1,2,384,768]{3,2,1,0:T(8,128)(2,1)}, bf16[1,2,384,768]{3,2,1,0:T(8,128)(2,1)}, u32[]{:S(2)}, u32[]{:S(2)}) collective-permute-start(bf16[1,2,384,768]{3,2,1,0:T(8,128)(2,1)} %add_convert_fusion.1), channel_id=1, source_target_pairs={{1,0},{2,3},{5,4},{6,7},{9,8},{10,11},{13,12},{14,15},{17,16},{18,... | collective-permute-start | bytes 3538952 | tf_op jit(solution)/shard_map/ppermute | solution.py:515
  383.8 12.3 %collective-permute-start.46 = (bf16[96,3200]{1,0:T(8,128)(2,1)S(1)}, bf16[96,3200]{1,0:T(8,128)(2,1)S(1)}, u32[]{:S(2)}, u32[]{:S(2)}) collective-permute-start(bf16[96,3200]{1,0:T(8,128)(2,1)S(1)} %add_convert_fusion.11), channel_id=1, source_target_pairs={{1,2},{2,1},{5,6},{6,5},{9,10},{10,9},{13,14},{14,13},{17,18},{18,... | collective-permute-start | bytes 1843208 | tf_op jit(solution)/shard_map/ppermute | solution.py:508
  387.6 51.1 %collective-permute-start.43 = (bf16[2,2,64,768]{3,2,1,0:T(8,128)(2,1)S(1)}, bf16[2,2,64,768]{3,2,1,0:T(8,128)(2,1)S(1)}, u32[]{:S(2)}, u32[]{:S(2)}) collective-permute-start(bf16[2,2,64,768]{3,2,1,0:T(8,128)(2,1)S(1)} %pad_maximum_fusion.5), channel_id=1, source_target_pairs={{0,1},{1,0},{2,3},{3,2},{4,5},{5,4},{6,7},{7,6},{8,9},{9,8},{10,11... | collective-permute-start | bytes 1179656 | tf_op jit(solution)/shard_map/ppermute | solution.py:477
  393.5 45.1 %collective-permute-start.44 = (bf16[2,2,64,768]{3,2,1,0:T(8,128)(2,1)S(1)}, bf16[2,2,64,768]{3,2,1,0:T(8,128)(2,1)S(1)}, u32[]{:S(2)}, u32[]{:S(2)}) collective-permute-start(bf16[2,2,64,768]{3,2,1,0:T(8,128)(2,1)S(1)} %pad_maximum_fusion.6), channel_id=1, source_target_pairs={{0,2},{1,3},{2,0},{3,1},{4,6},{5,7},{6,4},{7,5},{8,10},{9,11},{10,... | collective-permute-start | bytes 1179656 | tf_op jit(solution)/shard_map/ppermute | solution.py:477
  394.2 44.5 %collective-permute-start.45 = (bf16[2,2,64,768]{3,2,1,0:T(8,128)(2,1)S(1)}, bf16[2,2,64,768]{3,2,1,0:T(8,128)(2,1)S(1)}, u32[]{:S(2)}, u32[]{:S(2)}) collective-permute-start(bf16[2,2,64,768]{3,2,1,0:T(8,128)(2,1)S(1)} %pad_maximum_fusion.7), channel_id=1, source_target_pairs={{0,3},{1,2},{2,1},{3,0},{4,7},{5,6},{6,5},{7,4},{8,11},{9,10},{10,... | collective-permute-start | bytes 1179656 | tf_op jit(solution)/shard_map/ppermute | solution.py:477
  396.3 51.0 %collective-permute-start.47 = (bf16[96,3200]{1,0:T(8,128)(2,1)S(1)}, bf16[96,3200]{1,0:T(8,128)(2,1)S(1)}, u32[]{:S(2)}, u32[]{:S(2)}) collective-permute-start(bf16[96,3200]{1,0:T(8,128)(2,1)S(1)} %add_convert_fusion.10), channel_id=1, source_target_pairs={{1,0},{2,3},{5,4},{6,7},{9,8},{10,11},{13,12},{14,15},{17,16},{18,... | collective-permute-start | bytes 1843208 | tf_op jit(solution)/shard_map/ppermute | solution.py:515
  (38 other events, 253.0 us)
Sparse Core Ops, SparseCore 0:
  267.0 54.6 reduce-scatter.1

commit v2 on v0

--- a/solution.py
+++ b/solution.py
@@ -163,7 +163,9 @@
 
 def gelu_parts(pre):
     bell = jnp.exp2(pre * pre * (-0.5 * math.log2(math.e)))
-    frac = 1.0 / (1.0 + (0.3275911 * math.sqrt(0.5)) * jnp.abs(pre))
+    size = 1.0 + (0.3275911 * math.sqrt(0.5)) * jnp.abs(pre)
+    frac = pl.reciprocal(size, approx=True)
+    frac = frac * (2.0 - size * frac)
     a5, a4, a3, a2, a1 = (
         0.5 * c for c in (1.061405429, -1.453152027, 1.421413741, -0.284496736, 0.254829592)
     )
@@ -281,11 +283,14 @@
     grad_gate = jnp.zeros((rows, LANES), f32)
     gates = probs * kept
     out_rows = gin_rows = None
-    for e in range(experts):
-        at = slice(e * hidden, (e + 1) * hidden)
+    products = lambda at: (mm(two, win_buf[at], 1, 1), mm(cot, wdn_buf[at], 1, 1))
+    spots = [slice(e * hidden, (e + 1) * hidden) for e in range(experts)]
+    ready = products(spots[0])
+    for e, at in enumerate(spots):
         win, wdn = win_buf[at], wdn_buf[at]
-        pre = mm(two, win, 1, 1)
-        back_rows = mm(cot, wdn, 1, 1)
+        pre, back_rows = ready
+        if e + 1 < experts:
+            ready = products(spots[e + 1])
         gate = gates[:, e : e + 1]
         hidden_rows, slope = gelu_parts(pre)
         product = jnp.sum(hidden_rows * back_rows, -1, keepdims=True)
@@ -502,6 +507,19 @@
             self.moving = lax.ppermute(self.raw, "seq", [(0, 1), (3, 2)])
         return self
 
+    def inwards_with(self, other, *others):
+        if self.seq != 4:
+            return
+        other.total = plus(other.pair, tie(other.moving, others))
+        index = lax.axis_index("seq")
+        both = jnp.where((index == 0) | (index == 3), self.raw, other.total)
+        self.moving = lax.ppermute(both, "seq", [(0, 1), (1, 0), (2, 3), (3, 2)])
+        other.moving = self.moving
+
+    def hold(self, others):
+        if self.seq == 4:
+            self.moving = tie(self.moving, others)
+
     def across(self, *others):
         if self.seq == 4:
             self.pair = plus(self.raw, tie(self.moving, others))
@@ -779,8 +797,7 @@
     lines[2].raw, lines[3].raw = tie((lines[2].raw, lines[3].raw), grad_tok)
     lines[2].inwards()
     ready = lines[1].across(grad_tok, flying)
-    ready = lines[0].outwards(ready)
-    lines[3].inwards()
+    lines[3].inwards_with(lines[0], ready)
     ready = lines[2].across(ready)
     ready = lines[1].outwards(ready)
     ready = lines[3].across(ready)
@@ -802,6 +819,7 @@
     outputs, grad_tokens = (
         jnp.concatenate([a[n] for a in home], 0).reshape(images, span, width) for n in range(2)
     )
+    lines[3].hold(dense_line.waiting())
     grads = [line.finish() for line in lines]
     dense = dense_line.finish().astype(f32)
     expert_grads = [jnp.concatenate([g[:, n] for g in grads], 0).astype(f32) for n in range(2)]

time: 460 us -> 466 us (1.013)
    ppermute x9, waiting for transfers between devices: 27 us -> 78.2 us  [exchange(): lax.ppermute(pieces[k], 'seq', [(n, n ^ k) for n in range(count)])]
    ppermute x5 -> x4, waiting for transfers between devices: 77 us -> 26.2 us  [outwards(): self.moving = lax.ppermute(self.total, 'seq', [(1, 0), (2, 3)])]
    ppermute x0 -> x1, waiting for transfers between devices: none -> 20.4 us  [inwards_with(): self.moving = lax.ppermute(both, 'seq', [(0, 1), (1, 0), (2, 3), (3, 2)])]
    ppermute x5 -> x4, waiting for transfers between devices: 40.1 us -> 21.9 us  [inwards(): self.moving = lax.ppermute(self.raw, 'seq', [(0, 1), (3, 2)])]
    convert_element_type x12 -> x11, other arithmetic: 10.8 us -> 11.8 us  [plus(): return sum((a.astype(f32) for a in arrays)).astype(bf16)]
    ppermute x5 -> x4, starting transfers between devices: 18.3 us -> 18.2 us  [inwards(): self.moving = lax.ppermute(self.raw, 'seq', [(0, 1), (3, 2)])]
  transfers between devices with their start and end apart: 51 -> 50, of which waited for: 20 -> 18; matrix products, arithmetic and copies ran while one was open for 8% -> 8% of each run, Pallas kernels for 18% -> 18%
where the time goes in v2:
time: 466 us; the launch traced here: 460 us
  waiting for transfers between devices  177 us (38%)
  Pallas kernels  150 us (32%)
  starting transfers between devices  68.4 us (15%)
  other arithmetic  30.4 us (7%)
  local copies, waits for them, and re-layouts  18.2 us (4%)
  between operations  15.1 us (3%)
    pallas_call x2, Pallas kernels, experts_call(): pl.pallas_call(functools.partial(expert_kernel, plan), grid=(groups,), in...  83 us
    ppermute x9, waiting for transfers between devices, exchange(): lax.ppermute(pieces[k], 'seq', [(n, n ^ k) for n in range(count)])  78.2 us
    pallas_call x2, Pallas kernels, grads_call(): pl.pallas_call(functools.partial(grads_kernel, plan), grid=(many,), in_sp...  30.6 us
    ppermute x26, waiting for transfers between devices, flip(): return lax.ppermute(array, 'fsdp', [(n, n ^ bits) for n in range(fsdp)])  30.4 us
    ppermute x4, waiting for transfers between devices, outwards(): self.moving = lax.ppermute(self.total, 'seq', [(1, 0), (2, 3)])  26.2 us
    ppermute x26, starting transfers between devices, flip(): return lax.ppermute(array, 'fsdp', [(n, n ^ bits) for n in range(fsdp)])  22.2 us
    ppermute x4, waiting for transfers between devices, inwards(): self.moving = lax.ppermute(self.raw, 'seq', [(0, 1), (3, 2)])  21.9 us
    pallas_call x1, Pallas kernels, back(): pl.pallas_call(back_kernel, grid=(images,), in_specs=[split] * 7 + [pl.Bl...  21.4 us
  transfers between devices with their start and end apart: 50, of which 18 were waited for; matrix products, arithmetic and copies ran while one was open for 8% of the time, Pallas kernels for 18%

profile of v2, /device:TPU:0, one launch (start us, length us, event | category | flops | bytes accessed | tf_op | source)
XLA Modules:
  0.0 459.6 jit_solution(17413675591432909514)
XLA Ops:
  9.4 3.0 collective-permute-start.1
  12.4 1.5 collective-permute-start
  14.7 3.6 collective-permute-start.4
  21.4 3.2 collective-permute-done.4
  24.6 10.0 %collective-permute-done.3 = bf16[128,768]{1,0:T(8,128)(2,1)S(1)} collective-permute-done((bf16[128,768]{1,0:T(8,128)(2,1)}, bf16[128,768]{1,0:T(8,128)(2,1)S(1)}, u32[]{:S(2)}, u32[]{:S(2)}) %collective-permute-start.3) | collective-permute-done | bytes 196640 | tf_op jit(solution)/shard_map/ppermute | solution.py:482
  35.7 2.5 collective-permute-start.12
  38.2 1.9 collective-permute-start.10
  41.4 4.7 %collective-permute-done.12 = bf16[144,768]{1,0:T(8,128)(2,1)S(1)} collective-permute-done((bf16[144,768]{1,0:T(8,128)(2,1)S(1)}, bf16[144,768]{1,0:T(8,128)(2,1)S(1)}, u32[]{:S(2)}, u32[]{:S(2)}) %collective-permute-start.12) | collective-permute-done | bytes 221216 | tf_op jit(solution)/shard_map/ppermute | solution.py:482
  46.0 9.1 %collective-permute-done.11 = bf16[144,768]{1,0:T(8,128)(2,1)S(1)} collective-permute-done((bf16[144,768]{1,0:T(8,128)(2,1)S(1)}, bf16[144,768]{1,0:T(8,128)(2,1)S(1)}, u32[]{:S(2)}, u32[]{:S(2)}) %collective-permute-start.11) | collective-permute-done | bytes 221216 | tf_op jit(solution)/shard_map/ppermute | solution.py:482
  56.4 2.1 collective-permute-done.13.refs_8_
  64.0 15.0 %front.1 = (f32[4,2,64,768]{3,2,1,0:T(8,128)}, bf16[4,2,64,768]{3,2,1,0:T(8,128)(2,1)}, bf16[2,256,2304]{2,1,0:T(8,128)(2,1)}, bf16[2,256,768]{2,1,0:T(8,128)(2,...) custom-call(bf16[96,3200]{1,0:T(8,128)(2,1)} %copy-done.6, ...), custom_call_target="tpu_custom_call" | custom-call | flops 1000 | bytes 1000 | tf_op jit(solution)/shard_map/front/pallas_call | solution.py:124
  79.0 2.5 collective-permute-start.19
  84.7 1.5 collective-permute-start.23
  86.2 1.5 collective-permute-start.22
  87.7 28.1 %experts_own.1 = (bf16[4,2,768,768]{3,2,1,0:T(8,128)(2,1)}, f32[8,768]{1,0:T(8,128)}, bf16[4,128,768]{2,1,0:T(8,128)(2,1)}, bf16[4,128,768]{2,1,0:T(8,128)(2,1)}) custom-call(bf16[4,128,768]{2,1,0:T(8,128)(2,1)} %bitcast.101, bf16[4,144,768]{2,1,0:T(8,128)(2,1)} %copy-done, bf16[4,384,768]{2,1,0:T(8,128)(2,1)} %refs_7_, bf16[4,384,768]{2,1,0:T(8,128)(2,1)} %copy-done.10, ...), custom_call_target="tpu_custom_call" | custom-call | flops 1000 | bytes 1000 | tf_op jit(solution)/shard_map/experts_own/pallas_call | solution.py:362
  117.7 7.9 %collective-permute-done.23.refs_6_ = bf16[2,144,768]{2,1,0:T(8,128)(2,1)S(1)} collective-permute-done((bf16[2,144,768]{2,1,0:T(8,128)(2,1)S(1)}, bf16[2,144,768]{2,1,0:T(8,128)(2,1)S(1)}, u32[]{:S(2)}, u32[]{:S(2)}) %collective-permute-start.23) | collective-permute-done | bytes 442400 | tf_op jit(solution)/shard_map/ppermute | solution.py:472
  126.4 54.9 %experts_far.1 = (bf16[1536,3072]{1,0:T(8,128)(2,1)}, bf16[1536,3072]{1,0:T(8,128)(2,1)}, f32[8,768]{1,0:T(8,128)}, bf16[4,128,768]{2,1,0:T(8,128)(2,1)}, bf16[4...) custom-call(bf16[4,128,768]{2,1,0:T(8,128)(2,1)} %collective-permute, ...), custom_call_target="tpu_custom_call" | custom-call | flops 72477573120 | bytes 16777216 | tf_op jit(solution)/shard_map/experts_far/pallas_call | solution.py:362
  181.3 10.8 %expert_grads.2 = (bf16[1,2,384,768]{3,2,1,0:T(8,128)(2,1)}, bf16[1,2,384,768]{3,2,1,0:T(8,128)(2,1)}) custom-call(bf16[4,128,768]{2,1,0:T(8,128)(2,1)} %collective-permute-done.17.refs_0_, bf16[4,128,768]{2,1,0:T(8,128)(2,1)} %collective-permute-done.18.refs_1_, bf16[4,128,768]{2,1,0:T(8,128)(2,1)} %collective-permute-done.19.refs_2_, ...), custom_call_target="tpu_custom_call" | custom-call | flops 14495514624 | bytes 16777216 | tf_op jit(solution)/shard_map/expert_grads/pallas_call | solution.py:452
  192.1 1.5 collective-permute-start.24
  195.7 1.6 add_convert_fusion.9
  197.3 1.4 collective-permute-start.31
  198.7 19.9 %expert_grads.3 = (bf16[3,2,384,768]{3,2,1,0:T(8,128)(2,1)}, bf16[3,2,384,768]{3,2,1,0:T(8,128)(2,1)}) custom-call(bf16[4,128,768]{2,1,0:T(8,128)(2,1)} %collective-permute-done.17.refs_0_, bf16[4,128,768]{2,1,0:T(8,128)(2,1)} %collective-permute-done.18.refs_1_, bf16[4,128,768]{2,1,0:T(8,128)(2,1)} %collective-permute-done.19.refs_2_, ...), custom_call_target="tpu_custom_call" | custom-call | flops 43486543872 | bytes 16777216 | tf_op jit(solution)/shard_map/expert_grads/pallas_call | solution.py:452
  218.6 11.8 %collective-permute-done.25 = bf16[4,128,768]{2,1,0:T(8,128)(2,1)S(1)} collective-permute-done((bf16[4,128,768]{2,1,0:T(8,128)(2,1)}, bf16[4,128,768]{2,1,0:T(8,128)(2,1)S(1)}, u32[]{:S(2)}, u32[]{:S(2)}) %collective-permute-start.25) | collective-permute-done | bytes 786464 | tf_op jit(solution)/shard_map/ppermute | solution.py:472
  233.5 2.5 collective-permute-start.29
  239.0 1.6 fusion.26
  240.6 3.0 collective-permute-start.34
  243.6 21.4 %back.1 = (bf16[2,64,768]{2,1,0:T(8,128)(2,1)}, bf16[2,64,768]{2,1,0:T(8,128)(2,1)}, bf16[2,64,768]{2,1,0:T(8,128)(2,1)}, bf16[2,64,768]{2,1,0:T(8,128)(2,1)}, bf16[768,3200]{1,0:T(8,128)(2,1)}) custom-call(bf16[4,2,64,768]{3,2,1,0:T(8,128)(2,1)} %bitcast.129, bf16[4,2,64,768]{3,2,1,0:T(8,128)(2,1)} %bitcast.130, bf16[4,2,64,768]{3,2,1,0:T(8,128)(2,1)} %bitcast.131, ...), custom_call_target="tpu_custom_call" | custom-call | flops 30198988800 | bytes 16777216 | tf_op jit(solution)/shard_map/back/pallas_call | solution.py:619
  265.0 4.9 %collective-permute-done.29 = bf16[4,128,768]{2,1,0:T(8,128)(2,1)} collective-permute-done((bf16[4,128,768]{2,1,0:T(8,128)(2,1)}, bf16[4,128,768]{2,1,0:T(8,128)(2,1)}, u32[]{:S(2)}, u32[]{:S(2)}) %collective-permute-start.29) | collective-permute-done | bytes 786464 | tf_op jit(solution)/shard_map/ppermute | solution.py:472
  269.9 3.6 collective-permute-start.35
  273.5 2.2 add_convert_fusion.7
  277.3 21.9 %collective-permute-done.35 = bf16[1,2,384,768]{3,2,1,0:T(8,128)(2,1)} collective-permute-done((bf16[1,2,384,768]{3,2,1,0:T(8,128)(2,1)}, bf16[1,2,384,768]{3,2,1,0:T(8,128)(2,1)}, u32[]{:S(2)}, u32[]{:S(2)}) %collective-permute-start.35) | collective-permute-done | bytes 1179680 | tf_op jit(solution)/shard_map/ppermute | solution.py:507
  299.2 1.6 add_convert_fusion.6
  301.8 20.4 %collective-permute-done.37 = bf16[1,2,384,768]{3,2,1,0:T(8,128)(2,1)S(1)} collective-permute-done((bf16[1,2,384,768]{3,2,1,0:T(8,128)(2,1)S(1)}, bf16[1,2,384,768]{3,2,1,0:T(8,128)(2,1)S(1)}, u32[]{:S(2)}, u32[]{:S(2)}) %collective-permute-start.37) | collective-permute-done | bytes 1179680 | tf_op jit(solution)/shard_map/ppermute | solution.py:516
  323.8 1.4 collective-permute-start.47
  325.3 1.8 collective-permute-start.40
  329.9 10.3 %collective-permute-start.39 = (bf16[96,3200]{1,0:T(8,128)(2,1)}, bf16[96,3200]{1,0:T(8,128)(2,1)S(1)}, u32[]{:S(2)}, u32[]{:S(2)}) collective-permute-start(bf16[96,3200]{1,0:T(8,128)(2,1)} %reduce-scatter.2.cloned.1.call-done), channel_id=1, source_target_pairs={{0,1},{3,2},{4,5},{7,6},{8,9},{11,10},{12,13},{15,14},{16,17},{19,... | collective-permute-start | bytes 1843208 | tf_op jit(solution)/shard_map/ppermute | solution.py:507
  340.2 17.2 %collective-permute-done.47 = bf16[1,2,384,768]{3,2,1,0:T(8,128)(2,1)} collective-permute-done((bf16[1,2,384,768]{3,2,1,0:T(8,128)(2,1)S(1)}, bf16[1,2,384,768]{3,2,1,0:T(8,128)(2,1)}, u32[]{:S(2)}, u32[]{:S(2)}) %collective-permute-start.47) | collective-permute-done | bytes 1179680 | tf_op jit(solution)/shard_map/ppermute | solution.py:533
  357.4 1.4 broadcast_select_fusion.1
  359.7 3.0 add_convert_fusion.1
  362.6 1.6 collective-permute-start.48
  365.2 2.2 convert_add_fusion
  368.4 5.9 %collective-permute-start.41 = (bf16[2,2,64,768]{3,2,1,0:T(8,128)(2,1)S(1)}, bf16[2,2,64,768]{3,2,1,0:T(8,128)(2,1)S(1)}, u32[]{:S(2)}, u32[]{:S(2)}) collective-permute-start(bf16[2,2,64,768]{3,2,1,0:T(8,128)(2,1)S(1)} %pad_maximum_fusion.5), channel_id=1, source_target_pairs={{0,1},{1,0},{2,3},{3,2},{4,5},{5,4},{6,7},{7,6},{8,9},{9,8},{10,11... | collective-permute-start | bytes 1179656 | tf_op jit(solution)/shard_map/ppermute | solution.py:482
  375.0 1.9 collective-permute-start.43
  377.1 51.2 %collective-permute-done.41 = bf16[2,2,64,768]{3,2,1,0:T(8,128)(2,1)S(1)} collective-permute-done((bf16[2,2,64,768]{3,2,1,0:T(8,128)(2,1)S(1)}, bf16[2,2,64,768]{3,2,1,0:T(8,128)(2,1)S(1)}, u32[]{:S(2)}, u32[]{:S(2)}) %collective-permute-start.41) | collective-permute-done | bytes 393248 | tf_op jit(solution)/shard_map/ppermute | solution.py:482
  431.9 9.0 %collective-permute-done.45 = bf16[96,3200]{1,0:T(8,128)(2,1)S(1)} collective-permute-done((bf16[96,3200]{1,0:T(8,128)(2,1)S(1)}, bf16[96,3200]{1,0:T(8,128)(2,1)S(1)}, u32[]{:S(2)}, u32[]{:S(2)}) %collective-permute-start.45) | collective-permute-done | bytes 614432 | tf_op jit(solution)/shard_map/ppermute | solution.py:533
  444.1 1.9 broadcast_select_fusion
  447.3 2.6 maximum_convert_fusion.1
  449.9 2.6 maximum_convert_fusion
  (205 shorter events, 47.7 us)
Async XLA Ops:
  7.2 322.7 %reduce-scatter.2.cloned.1.call-start = ((), (), s32[]{:S(2)}) async-start(), calls=%async_computation.1 | async-start | bytes 5529600 | tf_op jit(solution)/shard_map/reduce_scatter | solution.py:796
  9.4 26.3 %collective-permute-start.1 = (bf16[96,3200]{1,0:T(8,128)(2,1)S(1)}, bf16[96,3200]{1,0:T(8,128)(2,1)S(1)}, u32[]{:S(2)}, u32[]{:S(2)}) collective-permute-start(bf16[96,3200]{1,0:T(8,128)(2,1)S(1)} %fusion.5.refs_0_), channel_id=1, source_target_pairs={{0,16},{4,20},{8,24},{12,28},{16,0},{20,4},{24,8},{28,12},{1,17},{... | collective-permute-start | bytes 1843208 | tf_op jit(solution)/shard_map/ppermute | solution.py:472
  12.4 23.2 %collective-permute-start = (bf16[96,3200]{1,0:T(8,128)(2,1)S(1)}, bf16[96,3200]{1,0:T(8,128)(2,1)S(1)}, u32[]{:S(2)}, u32[]{:S(2)}) collective-permute-start(bf16[96,3200]{1,0:T(8,128)(2,1)S(1)} %fusion.5.refs_0_), channel_id=1, source_target_pairs={{0,8},{4,12},{8,0},{12,4},{16,24},{20,28},{24,16},{28,20},{1,9},{5... | collective-permute-start | bytes 1843208 | tf_op jit(solution)/shard_map/ppermute | solution.py:472
  14.7 9.9 %collective-permute-start.4 = (bf16[128,768]{1,0:T(8,128)(2,1)}, bf16[128,768]{1,0:T(8,128)(2,1)S(1)}, u32[]{:S(2)}, u32[]{:S(2)}) collective-permute-start(bf16[128,768]{1,0:T(8,128)(2,1)} %get-tuple-element.238), channel_id=1, source_target_pairs={{0,3},{1,2},{2,1},{3,0},{4,7},{5,6},{6,5},{7,4},{8,11},{9,10},{10,... | collective-permute-start | bytes 589832 | tf_op jit(solution)/shard_map/ppermute | solution.py:482
  18.3 16.3 %collective-permute-start.3 = (bf16[128,768]{1,0:T(8,128)(2,1)}, bf16[128,768]{1,0:T(8,128)(2,1)S(1)}, u32[]{:S(2)}, u32[]{:S(2)}) collective-permute-start(bf16[128,768]{1,0:T(8,128)(2,1)} %get-tuple-element.239), channel_id=1, source_target_pairs={{0,2},{1,3},{2,0},{3,1},{4,6},{5,7},{6,4},{7,5},{8,10},{9,11},{10,... | collective-permute-start | bytes 589832 | tf_op jit(solution)/shard_map/ppermute | solution.py:482
  18.3 16.3 %collective-permute-start.2 = (bf16[128,768]{1,0:T(8,128)(2,1)S(1)}, bf16[128,768]{1,0:T(8,128)(2,1)S(1)}, u32[]{:S(2)}, u32[]{:S(2)}) collective-permute-start(bf16[128,768]{1,0:T(8,128)(2,1)S(1)} %get-tuple-element.240), channel_id=1, source_target_pairs={{0,1},{1,0},{2,3},{3,2},{4,5},{5,4},{6,7},{7,6},{8,9},{9,8},{10,11... | collective-permute-start | bytes 589832 | tf_op jit(solution)/shard_map/ppermute | solution.py:482
  35.7 10.3 %collective-permute-start.12 = (bf16[144,768]{1,0:T(8,128)(2,1)S(1)}, bf16[144,768]{1,0:T(8,128)(2,1)S(1)}, u32[]{:S(2)}, u32[]{:S(2)}) collective-permute-start(bf16[144,768]{1,0:T(8,128)(2,1)S(1)} %get-tuple-element.234), channel_id=1, source_target_pairs={{0,3},{1,2},{2,1},{3,0},{4,7},{5,6},{6,5},{7,4},{8,11},{9,10},{10,... | collective-permute-start | bytes 663560 | tf_op jit(solution)/shard_map/ppermute | solution.py:482
  38.2 16.9 %collective-permute-start.11 = (bf16[144,768]{1,0:T(8,128)(2,1)S(1)}, bf16[144,768]{1,0:T(8,128)(2,1)S(1)}, u32[]{:S(2)}, u32[]{:S(2)}) collective-permute-start(bf16[144,768]{1,0:T(8,128)(2,1)S(1)} %get-tuple-element.235), channel_id=1, source_target_pairs={{0,2},{1,3},{2,0},{3,1},{4,6},{5,7},{6,4},{7,5},{8,10},{9,11},{10,... | collective-permute-start | bytes 663560 | tf_op jit(solution)/shard_map/ppermute | solution.py:482
  38.2 16.9 %collective-permute-start.10 = (bf16[144,768]{1,0:T(8,128)(2,1)S(1)}, bf16[144,768]{1,0:T(8,128)(2,1)S(1)}, u32[]{:S(2)}, u32[]{:S(2)}) collective-permute-start(bf16[144,768]{1,0:T(8,128)(2,1)S(1)} %get-tuple-element.236), channel_id=1, source_target_pairs={{0,1},{1,0},{2,3},{3,2},{4,5},{5,4},{6,7},{7,6},{8,9},{9,8},{10,11... | collective-permute-start | bytes 663560 | tf_op jit(solution)/shard_map/ppermute | solution.py:482
  40.2 15.6 %collective-permute-start.9 = (bf16[48,3200]{1,0:T(8,128)(2,1)S(1)}, bf16[48,3200]{1,0:T(8,128)(2,1)S(1)}, u32[]{:S(2)}, u32[]{:S(2)}) collective-permute-start(bf16[48,3200]{1,0:T(8,128)(2,1)S(1)} %slice.204), channel_id=1, source_target_pairs={{0,8},{4,12},{8,0},{12,4},{16,24},{20,28},{24,16},{28,20},{1,9},{5... | collective-permute-start | bytes 921608 | tf_op jit(solution)/shard_map/ppermute | solution.py:472
  40.8 15.0 %collective-permute-start.8 = (bf16[48,3200]{1,0:T(8,128)(2,1)S(1)}, bf16[48,3200]{1,0:T(8,128)(2,1)S(1)}, u32[]{:S(2)}, u32[]{:S(2)}) collective-permute-start(bf16[48,3200]{1,0:T(8,128)(2,1)S(1)} %slice.203), channel_id=1, source_target_pairs={{0,16},{4,20},{8,24},{12,28},{16,0},{20,4},{24,8},{28,12},{1,17},{... | collective-permute-start | bytes 921608 | tf_op jit(solution)/shard_map/ppermute | solution.py:472
  46.0 10.4 %collective-permute-start.5 = (bf16[96,3200]{1,0:T(8,128)(2,1)S(1)}, bf16[96,3200]{1,0:T(8,128)(2,1)S(1)}, u32[]{:S(2)}, u32[]{:S(2)}) collective-permute-start(bf16[96,3200]{1,0:T(8,128)(2,1)S(1)} %fusion.5.refs_0_), channel_id=1, source_target_pairs={{0,4},{4,0},{8,12},{12,8},{16,20},{20,16},{24,28},{28,24},{1,5},{5... | collective-permute-start | bytes 1843208 | tf_op jit(solution)/shard_map/ppermute | solution.py:472
  55.1 3.8 collective-permute-start.6
  55.2 3.8 collective-permute-start.7
  59.0 25.7 %collective-permute-start.15 = (bf16[4,384,768]{2,1,0:T(8,128)(2,1)}, bf16[4,384,768]{2,1,0:T(8,128)(2,1)S(1)}, u32[]{:S(2)}, u32[]{:S(2)}) collective-permute-start(bf16[4,384,768]{2,1,0:T(8,128)(2,1)} %refs_7_), channel_id=1, source_target_pairs={{0,4},{4,0},{8,12},{12,8},{16,20},{20,16},{24,28},{28,24},{1,5},{5... | collective-permute-start | bytes 7077896 | tf_op jit(solution)/shard_map/ppermute | solution.py:472
  59.2 27.1 %collective-permute-start.16 = (bf16[4,384,768]{2,1,0:T(8,128)(2,1)}, bf16[4,384,768]{2,1,0:T(8,128)(2,1)}, u32[]{:S(2)}, u32[]{:S(2)}) collective-permute-start(bf16[4,384,768]{2,1,0:T(8,128)(2,1)} %refs_9_), channel_id=1, source_target_pairs={{0,4},{4,0},{8,12},{12,8},{16,20},{20,16},{24,28},{28,24},{1,5},{5... | collective-permute-start | bytes 7077896 | tf_op jit(solution)/shard_map/ppermute | solution.py:472
  59.5 21.9 %collective-permute-start.21 = (bf16[4,144,768]{2,1,0:T(8,128)(2,1)S(1)}, bf16[4,144,768]{2,1,0:T(8,128)(2,1)}, u32[]{:S(2)}, u32[]{:S(2)}) collective-permute-start(bf16[4,144,768]{2,1,0:T(8,128)(2,1)S(1)} %pad_maximum_fusion.refs_1_), channel_id=1, source_target_pairs={{0,16},{4,20},{8,24},{12,28},{16,0},{20,4},{24,8},{28,12},{1,17},{... | collective-permute-start | bytes 2654216 | tf_op jit(solution)/shard_map/ppermute | solution.py:472
  60.1 21.9 %collective-permute-start.20 = (bf16[4,144,768]{2,1,0:T(8,128)(2,1)S(1)}, bf16[4,144,768]{2,1,0:T(8,128)(2,1)}, u32[]{:S(2)}, u32[]{:S(2)}) collective-permute-start(bf16[4,144,768]{2,1,0:T(8,128)(2,1)S(1)} %pad_maximum_fusion.refs_1_), channel_id=1, source_target_pairs={{0,8},{4,12},{8,0},{12,4},{16,24},{20,28},{24,16},{28,20},{1,9},{5... | collective-permute-start | bytes 2654216 | tf_op jit(solution)/shard_map/ppermute | solution.py:472
  79.0 36.9 %collective-permute-start.19 = (bf16[4,128,768]{2,1,0:T(8,128)(2,1)}, bf16[4,128,768]{2,1,0:T(8,128)(2,1)}, u32[]{:S(2)}, u32[]{:S(2)}) collective-permute-start(bf16[4,128,768]{2,1,0:T(8,128)(2,1)} %bitcast.98), channel_id=1, source_target_pairs={{0,24},{4,28},{8,16},{12,20},{16,8},{20,12},{24,0},{28,4},{1,25},{... | collective-permute-start | bytes 2359304 | tf_op jit(solution)/shard_map/ppermute | solution.py:472
  81.5 35.0 %collective-permute-start.18 = (bf16[4,128,768]{2,1,0:T(8,128)(2,1)}, bf16[4,128,768]{2,1,0:T(8,128)(2,1)}, u32[]{:S(2)}, u32[]{:S(2)}) collective-permute-start(bf16[4,128,768]{2,1,0:T(8,128)(2,1)} %bitcast.99), channel_id=1, source_target_pairs={{0,16},{4,20},{8,24},{12,28},{16,0},{20,4},{24,8},{28,12},{1,17},{... | collective-permute-start | bytes 2359304 | tf_op jit(solution)/shard_map/ppermute | solution.py:472
  82.0 35.7 %collective-permute-start.17 = (bf16[4,128,768]{2,1,0:T(8,128)(2,1)}, bf16[4,128,768]{2,1,0:T(8,128)(2,1)}, u32[]{:S(2)}, u32[]{:S(2)}) collective-permute-start(bf16[4,128,768]{2,1,0:T(8,128)(2,1)} %bitcast.100), channel_id=1, source_target_pairs={{0,8},{4,12},{8,0},{12,4},{16,24},{20,28},{24,16},{28,20},{1,9},{5... | collective-permute-start | bytes 2359304 | tf_op jit(solution)/shard_map/ppermute | solution.py:472
  84.7 40.9 %collective-permute-start.23 = (bf16[2,144,768]{2,1,0:T(8,128)(2,1)S(1)}, bf16[2,144,768]{2,1,0:T(8,128)(2,1)S(1)}, u32[]{:S(2)}, u32[]{:S(2)}) collective-permute-start(bf16[2,144,768]{2,1,0:T(8,128)(2,1)S(1)} %slice.267), channel_id=1, source_target_pairs={{0,8},{4,12},{8,0},{12,4},{16,24},{20,28},{24,16},{28,20},{1,9},{5... | collective-permute-start | bytes 1327112 | tf_op jit(solution)/shard_map/ppermute | solution.py:472
  86.2 39.6 %collective-permute-start.22 = (bf16[2,144,768]{2,1,0:T(8,128)(2,1)S(1)}, bf16[2,144,768]{2,1,0:T(8,128)(2,1)}, u32[]{:S(2)}, u32[]{:S(2)}) collective-permute-start(bf16[2,144,768]{2,1,0:T(8,128)(2,1)S(1)} %slice.266), channel_id=1, source_target_pairs={{0,16},{4,20},{8,24},{12,28},{16,0},{20,4},{24,8},{28,12},{1,17},{... | collective-permute-start | bytes 1327112 | tf_op jit(solution)/shard_map/ppermute | solution.py:472
  192.1 3.6 collective-permute-start.30
  192.1 26.4 %collective-permute-start.24 = (bf16[4,128,768]{2,1,0:T(8,128)(2,1)}, bf16[4,128,768]{2,1,0:T(8,128)(2,1)S(1)}, u32[]{:S(2)}, u32[]{:S(2)}) collective-permute-start(bf16[4,128,768]{2,1,0:T(8,128)(2,1)} %get-tuple-element.103), channel_id=1, source_target_pairs={{0,8},{4,12},{8,0},{12,4},{16,24},{20,28},{24,16},{28,20},{1,9},{5... | collective-permute-start | bytes 2359304 | tf_op jit(solution)/shard_map/ppermute | solution.py:472
  193.7 36.7 %collective-permute-start.25 = (bf16[4,128,768]{2,1,0:T(8,128)(2,1)}, bf16[4,128,768]{2,1,0:T(8,128)(2,1)S(1)}, u32[]{:S(2)}, u32[]{:S(2)}) collective-permute-start(bf16[4,128,768]{2,1,0:T(8,128)(2,1)} %get-tuple-element.104), channel_id=1, source_target_pairs={{0,16},{4,20},{8,24},{12,28},{16,0},{20,4},{24,8},{28,12},{1,17},{... | collective-permute-start | bytes 2359304 | tf_op jit(solution)/shard_map/ppermute | solution.py:472
  194.4 35.9 %collective-permute-start.26 = (bf16[4,128,768]{2,1,0:T(8,128)(2,1)}, bf16[4,128,768]{2,1,0:T(8,128)(2,1)}, u32[]{:S(2)}, u32[]{:S(2)}) collective-permute-start(bf16[4,128,768]{2,1,0:T(8,128)(2,1)} %get-tuple-element.105), channel_id=1, source_target_pairs={{0,24},{4,28},{8,16},{12,20},{16,8},{20,12},{24,0},{28,4},{1,25},{... | collective-permute-start | bytes 2359304 | tf_op jit(solution)/shard_map/ppermute | solution.py:472
  197.3 34.0 %collective-permute-start.31 = (bf16[1,2,384,768]{3,2,1,0:T(8,128)(2,1)S(1)}, bf16[1,2,384,768]{3,2,1,0:T(8,128)(2,1)S(1)}, u32[]{:S(2)}, u32[]{:S(2)}) collective-permute-start(bf16[1,2,384,768]{3,2,1,0:T(8,128)(2,1)S(1)} %add_convert_fusion.9), channel_id=1, source_target_pairs={{0,1},{3,2},{4,5},{7,6},{8,9},{11,10},{12,13},{15,14},{16,17},{19,... | collective-permute-start | bytes 3538952 | tf_op jit(solution)/shard_map/ppermute | solution.py:507
  231.6 6.5 %collective-permute-start.32 = (bf16[3,2,384,768]{3,2,1,0:T(8,128)(2,1)}, bf16[3,2,384,768]{3,2,1,0:T(8,128)(2,1)S(1)}, u32[]{:S(2)}, u32[]{:S(2)}) collective-permute-start(bf16[3,2,384,768]{3,2,1,0:T(8,128)(2,1)} %get-tuple-element.122), channel_id=1, source_target_pairs={{0,4},{4,0},{8,12},{12,8},{16,20},{20,16},{24,28},{28,24},{1,5},{5... | collective-permute-start | bytes 10616840 | tf_op jit(solution)/shard_map/ppermute | solution.py:472
  232.6 32.4 %collective-permute-start.27 = (bf16[4,128,768]{2,1,0:T(8,128)(2,1)}, bf16[4,128,768]{2,1,0:T(8,128)(2,1)}, u32[]{:S(2)}, u32[]{:S(2)}) collective-permute-start(bf16[4,128,768]{2,1,0:T(8,128)(2,1)} %get-tuple-element.106), channel_id=1, source_target_pairs={{0,8},{4,12},{8,0},{12,4},{16,24},{20,28},{24,16},{28,20},{1,9},{5... | collective-permute-start | bytes 2359304 | tf_op jit(solution)/shard_map/ppermute | solution.py:472
  232.6 32.4 %collective-permute-start.28 = (bf16[4,128,768]{2,1,0:T(8,128)(2,1)}, bf16[4,128,768]{2,1,0:T(8,128)(2,1)}, u32[]{:S(2)}, u32[]{:S(2)}) collective-permute-start(bf16[4,128,768]{2,1,0:T(8,128)(2,1)} %get-tuple-element.107), channel_id=1, source_target_pairs={{0,16},{4,20},{8,24},{12,28},{16,0},{20,4},{24,8},{28,12},{1,17},{... | collective-permute-start | bytes 2359304 | tf_op jit(solution)/shard_map/ppermute | solution.py:472
  233.5 36.3 %collective-permute-start.29 = (bf16[4,128,768]{2,1,0:T(8,128)(2,1)}, bf16[4,128,768]{2,1,0:T(8,128)(2,1)}, u32[]{:S(2)}, u32[]{:S(2)}) collective-permute-start(bf16[4,128,768]{2,1,0:T(8,128)(2,1)} %get-tuple-element.108), channel_id=1, source_target_pairs={{0,24},{4,28},{8,16},{12,20},{16,8},{20,12},{24,0},{28,4},{1,25},{... | collective-permute-start | bytes 2359304 | tf_op jit(solution)/shard_map/ppermute | solution.py:472
  236.1 33.8 %collective-permute-start.33 = (bf16[1,2,384,768]{3,2,1,0:T(8,128)(2,1)S(1)}, bf16[1,2,384,768]{3,2,1,0:T(8,128)(2,1)S(1)}, u32[]{:S(2)}, u32[]{:S(2)}) collective-permute-start(bf16[1,2,384,768]{3,2,1,0:T(8,128)(2,1)S(1)} %add_convert_fusion.8), channel_id=1, source_target_pairs={{1,2},{2,1},{5,6},{6,5},{9,10},{10,9},{13,14},{14,13},{17,18},{18,... | collective-permute-start | bytes 3538952 | tf_op jit(solution)/shard_map/ppermute | solution.py:526
  240.6 29.2 %collective-permute-start.34 = (bf16[1,2,384,768]{3,2,1,0:T(8,128)(2,1)}, bf16[1,2,384,768]{3,2,1,0:T(8,128)(2,1)}, u32[]{:S(2)}, u32[]{:S(2)}) collective-permute-start(bf16[1,2,384,768]{3,2,1,0:T(8,128)(2,1)} %get-tuple-element.123), channel_id=1, source_target_pairs={{0,1},{3,2},{4,5},{7,6},{8,9},{11,10},{12,13},{15,14},{16,17},{19,... | collective-permute-start | bytes 3538952 | tf_op jit(solution)/shard_map/ppermute | solution.py:507
  269.9 29.3 %collective-permute-start.35 = (bf16[1,2,384,768]{3,2,1,0:T(8,128)(2,1)}, bf16[1,2,384,768]{3,2,1,0:T(8,128)(2,1)}, u32[]{:S(2)}, u32[]{:S(2)}) collective-permute-start(bf16[1,2,384,768]{3,2,1,0:T(8,128)(2,1)} %get-tuple-element.141), channel_id=1, source_target_pairs={{0,1},{3,2},{4,5},{7,6},{8,9},{11,10},{12,13},{15,14},{16,17},{19,... | collective-permute-start | bytes 3538952 | tf_op jit(solution)/shard_map/ppermute | solution.py:507
  275.7 25.8 %collective-permute-start.38 = (bf16[1,2,384,768]{3,2,1,0:T(8,128)(2,1)S(1)}, bf16[1,2,384,768]{3,2,1,0:T(8,128)(2,1)S(1)}, u32[]{:S(2)}, u32[]{:S(2)}) collective-permute-start(bf16[1,2,384,768]{3,2,1,0:T(8,128)(2,1)S(1)} %add_convert_fusion.7), channel_id=1, source_target_pairs={{1,2},{2,1},{5,6},{6,5},{9,10},{10,9},{13,14},{14,13},{17,18},{18,... | collective-permute-start | bytes 3538952 | tf_op jit(solution)/shard_map/ppermute | solution.py:526
  277.0 45.2 %collective-permute-start.37 = (bf16[1,2,384,768]{3,2,1,0:T(8,128)(2,1)S(1)}, bf16[1,2,384,768]{3,2,1,0:T(8,128)(2,1)S(1)}, u32[]{:S(2)}, u32[]{:S(2)}) collective-permute-start(bf16[1,2,384,768]{3,2,1,0:T(8,128)(2,1)S(1)} %broadcast_select_fusion.4), channel_id=1, source_target_pairs={{0,1},{1,0},{2,3},{3,2},{4,5},{5,4},{6,7},{7,6},{8,9},{9,8},{10,11... | collective-permute-start | bytes 3538952 | tf_op jit(solution)/shard_map/ppermute | solution.py:516
  300.8 22.8 %collective-permute-start.36 = (bf16[1,2,384,768]{3,2,1,0:T(8,128)(2,1)S(1)}, bf16[1,2,384,768]{3,2,1,0:T(8,128)(2,1)S(1)}, u32[]{:S(2)}, u32[]{:S(2)}) collective-permute-start(bf16[1,2,384,768]{3,2,1,0:T(8,128)(2,1)S(1)} %add_convert_fusion.6), channel_id=1, source_target_pairs={{1,2},{2,1},{5,6},{6,5},{9,10},{10,9},{13,14},{14,13},{17,18},{18,... | collective-permute-start | bytes 3538952 | tf_op jit(solution)/shard_map/ppermute | solution.py:526
  323.8 33.5 %collective-permute-start.47 = (bf16[1,2,384,768]{3,2,1,0:T(8,128)(2,1)S(1)}, bf16[1,2,384,768]{3,2,1,0:T(8,128)(2,1)}, u32[]{:S(2)}, u32[]{:S(2)}) collective-permute-start(bf16[1,2,384,768]{3,2,1,0:T(8,128)(2,1)S(1)} %add_convert_fusion.2), channel_id=1, source_target_pairs={{1,0},{2,3},{5,4},{6,7},{9,8},{10,11},{13,12},{14,15},{17,16},{18,... | collective-permute-start | bytes 3538952 | tf_op jit(solution)/shard_map/ppermute | solution.py:533
  325.3 34.4 %collective-permute-start.40 = (bf16[1,2,384,768]{3,2,1,0:T(8,128)(2,1)}, bf16[1,2,384,768]{3,2,1,0:T(8,128)(2,1)}, u32[]{:S(2)}, u32[]{:S(2)}) collective-permute-start(bf16[1,2,384,768]{3,2,1,0:T(8,128)(2,1)} %add_convert_fusion.3), channel_id=1, source_target_pairs={{1,2},{2,1},{5,6},{6,5},{9,10},{10,9},{13,14},{14,13},{17,18},{18,... | collective-permute-start | bytes 3538952 | tf_op jit(solution)/shard_map/ppermute | solution.py:526
  327.0 117.1 %collective-permute-start.46 = (bf16[1,2,384,768]{3,2,1,0:T(8,128)(2,1)S(1)}, bf16[1,2,384,768]{3,2,1,0:T(8,128)(2,1)}, u32[]{:S(2)}, u32[]{:S(2)}) collective-permute-start(bf16[1,2,384,768]{3,2,1,0:T(8,128)(2,1)S(1)} %add_convert_fusion.4), channel_id=1, source_target_pairs={{1,0},{2,3},{5,4},{6,7},{9,8},{10,11},{13,12},{14,15},{17,16},{18,... | collective-permute-start | bytes 3538952 | tf_op jit(solution)/shard_map/ppermute | solution.py:533
  329.9 34.4 %collective-permute-start.39 = (bf16[96,3200]{1,0:T(8,128)(2,1)}, bf16[96,3200]{1,0:T(8,128)(2,1)S(1)}, u32[]{:S(2)}, u32[]{:S(2)}) collective-permute-start(bf16[96,3200]{1,0:T(8,128)(2,1)} %reduce-scatter.2.cloned.1.call-done), channel_id=1, source_target_pairs={{0,1},{3,2},{4,5},{7,6},{8,9},{11,10},{12,13},{15,14},{16,17},{19,... | collective-permute-start | bytes 1843208 | tf_op jit(solution)/shard_map/ppermute | solution.py:507
  362.6 80.7 %collective-permute-start.48 = (bf16[1,2,384,768]{3,2,1,0:T(8,128)(2,1)}, bf16[1,2,384,768]{3,2,1,0:T(8,128)(2,1)}, u32[]{:S(2)}, u32[]{:S(2)}) collective-permute-start(bf16[1,2,384,768]{3,2,1,0:T(8,128)(2,1)} %add_convert_fusion.1), channel_id=1, source_target_pairs={{1,0},{2,3},{5,4},{6,7},{9,8},{10,11},{13,12},{14,15},{17,16},{18,... | collective-permute-start | bytes 3538952 | tf_op jit(solution)/shard_map/ppermute | solution.py:533
  364.4 10.6 %collective-permute-start.44 = (bf16[96,3200]{1,0:T(8,128)(2,1)S(1)}, bf16[96,3200]{1,0:T(8,128)(2,1)S(1)}, u32[]{:S(2)}, u32[]{:S(2)}) collective-permute-start(bf16[96,3200]{1,0:T(8,128)(2,1)S(1)} %add_convert_fusion.11), channel_id=1, source_target_pairs={{1,2},{2,1},{5,6},{6,5},{9,10},{10,9},{13,14},{14,13},{17,18},{18,... | collective-permute-start | bytes 1843208 | tf_op jit(solution)/shard_map/ppermute | solution.py:526
  368.4 59.9 %collective-permute-start.41 = (bf16[2,2,64,768]{3,2,1,0:T(8,128)(2,1)S(1)}, bf16[2,2,64,768]{3,2,1,0:T(8,128)(2,1)S(1)}, u32[]{:S(2)}, u32[]{:S(2)}) collective-permute-start(bf16[2,2,64,768]{3,2,1,0:T(8,128)(2,1)S(1)} %pad_maximum_fusion.5), channel_id=1, source_target_pairs={{0,1},{1,0},{2,3},{3,2},{4,5},{5,4},{6,7},{7,6},{8,9},{9,8},{10,11... | collective-permute-start | bytes 1179656 | tf_op jit(solution)/shard_map/ppermute | solution.py:482
  374.3 55.3 %collective-permute-start.42 = (bf16[2,2,64,768]{3,2,1,0:T(8,128)(2,1)S(1)}, bf16[2,2,64,768]{3,2,1,0:T(8,128)(2,1)S(1)}, u32[]{:S(2)}, u32[]{:S(2)}) collective-permute-start(bf16[2,2,64,768]{3,2,1,0:T(8,128)(2,1)S(1)} %pad_maximum_fusion.6), channel_id=1, source_target_pairs={{0,2},{1,3},{2,0},{3,1},{4,6},{5,7},{6,4},{7,5},{8,10},{9,11},{10,... | collective-permute-start | bytes 1179656 | tf_op jit(solution)/shard_map/ppermute | solution.py:482
  375.0 54.6 %collective-permute-start.43 = (bf16[2,2,64,768]{3,2,1,0:T(8,128)(2,1)S(1)}, bf16[2,2,64,768]{3,2,1,0:T(8,128)(2,1)S(1)}, u32[]{:S(2)}, u32[]{:S(2)}) collective-permute-start(bf16[2,2,64,768]{3,2,1,0:T(8,128)(2,1)S(1)} %pad_maximum_fusion.7), channel_id=1, source_target_pairs={{0,3},{1,2},{2,1},{3,0},{4,7},{5,6},{6,5},{7,4},{8,11},{9,10},{10,... | collective-permute-start | bytes 1179656 | tf_op jit(solution)/shard_map/ppermute | solution.py:482
  428.3 12.6 %collective-permute-start.45 = (bf16[96,3200]{1,0:T(8,128)(2,1)S(1)}, bf16[96,3200]{1,0:T(8,128)(2,1)S(1)}, u32[]{:S(2)}, u32[]{:S(2)}) collective-permute-start(bf16[96,3200]{1,0:T(8,128)(2,1)S(1)} %add_convert_fusion.10), channel_id=1, source_target_pairs={{1,0},{2,3},{5,4},{6,7},{9,8},{10,11},{13,12},{14,15},{17,16},{18,... | collective-permute-start | bytes 1843208 | tf_op jit(solution)/shard_map/ppermute | solution.py:533
  (40 other events, 280.9 us)
Sparse Core Ops, SparseCore 0:
  270.0 53.6 reduce-scatter.1

commit v3 on v0

--- a/solution.py
+++ b/solution.py
@@ -184,12 +184,14 @@
     cot_parts = [take(n) for n in plan["cot"]]
     weights = take(4)
     (wr_ref,) = take(1)
-    dwr_carried = None if opening else take(1)[0]
+    dwr_carried, own_ref = (None, None) if opening else take(2)
     left = take(1 if opening else 2)
+    early = [] if opening else take(2)
     (dwr_ref,) = take(1)
     results = take(2 * groups)
     two_buf, cot_buf, sems, win_buf, wdn_buf, weight_sems, gated_buf, grad_buf = take(8)
     stage, store_sems, left_sems = take(3)
+    acc, own_buf, early_buf, own_sem, early_sems = [None] * 5 if opening else take(5)
     _, blocks, span, width = two_buf.shape
     rows = blocks * span
     hidden = win_buf.shape[0] // experts
@@ -232,7 +234,7 @@
                 place = k % buffer.shape[0]
                 stores[k].append(
                     pltpu.make_async_copy(
-                        buffer.at[place],
+                        buffer.at[place, :, pl.ds(hidden, (experts - 1) * hidden)],
                         left[n].at[pl.ds(k * rows, rows)],
                         left_sems.at[place, n],
                     )
@@ -245,6 +247,8 @@
         for some in copies[1:]:
             for copy in some:
                 copy.start()
+        if not opening:
+            pltpu.make_async_copy(own_ref.at[0], own_buf, own_sem).start()
         dwr_ref[...] = jnp.zeros_like(dwr_ref) if opening else dwr_carried[...]
         for copy in fetches:
             copy.wait()
@@ -295,9 +299,12 @@
         if opening:
             gated_buf[e, 1] = mm(gated, cot, 0, 0).astype(bf16)
             gated_buf[e, 0] = mm(grad_pre, two, 0, 0).astype(bf16)
-        else:
+        elif e > 0:
             gated_buf[slot, :, at] = gated
             grad_buf[slot, :, at] = grad_pre
+        else:
+            for n, fresh in enumerate((mm(grad_pre, two, 0, 0), mm(gated, cot, 0, 0))):
+                acc[n] = jnp.where(group == 0, 0.0, acc[n]) + fresh
         out_part, gin_part = mm(gated, wdn), mm(grad_pre, win)
         out_rows = out_part if e == 0 else out_rows + out_part
         gin_rows = gin_part if e == 0 else gin_rows + gin_part
@@ -321,12 +328,27 @@
             copy = pltpu.make_async_copy(gated_buf, left[0], left_sems.at[0, 0])
             copy.start()
             copy.wait()
+        else:
+            pltpu.make_async_copy(own_ref.at[0], own_buf, own_sem).wait()
+            early_copies = []
+            for n in range(2):
+                early_buf[n] = (acc[n] + own_buf[n].astype(f32)).astype(bf16)
+                for m, target in enumerate(early):
+                    copy = pltpu.make_async_copy(
+                        early_buf.at[n, pl.ds(m * shard, shard)],
+                        target.at[0, n],
+                        early_sems.at[n, m],
+                    )
+                    copy.start()
+                    early_copies.append(copy)
+            for copy in early_copies:
+                copy.wait()
         for k in (groups - 1,) if groups == 1 else (groups - 2, groups - 1):
             for store in stores[k][0 if k == groups - 1 else 2 :]:
                 store.wait()
 
 
-def experts_call(two, cot, weights, wr, dwr, name, cost):
+def experts_call(two, cot, weights, wr, carried, name, cost):
     groups = len(two)
     opening = groups == 1
     experts, shard, width = weights[0].shape
@@ -351,7 +373,8 @@
         left = [jax.ShapeDtypeStruct((experts, 2, hidden, width), bf16)]
         buffers = [pltpu.VMEM(left[0].shape, bf16), pltpu.VMEM((16, LANES), bf16)]
     else:
-        left = [jax.ShapeDtypeStruct((groups * rows, experts * hidden), bf16)] * 2
+        left = [jax.ShapeDtypeStruct((groups * rows, (experts - 1) * hidden), bf16)] * 2
+        left += [jax.ShapeDtypeStruct((1, 2, shard, width), bf16)] * 2
         buffers = [pltpu.VMEM((2, rows, experts * hidden), bf16)] * 2
     pieces = [a for parts in two for a in parts] + [a for parts in cot for a in parts]
     outs = pl.pallas_call(
@@ -359,7 +382,7 @@
         grid=(groups,),
         in_specs=[anywhere] * (len(pieces) + 4)
         + [once(wr)]
-        + ([] if opening else [once(little)]),
+        + ([] if opening else [once(little), anywhere]),
         out_specs=[anywhere] * len(left) + [once(little)] + [anywhere] * (2 * groups),
         out_shape=left + [little] + [result] * (2 * groups),
         scratch_shapes=[
@@ -373,11 +396,22 @@
             pltpu.VMEM((2, blocks, span, width), bf16),
             pltpu.SemaphoreType.DMA((2,)),
             pltpu.SemaphoreType.DMA((2, 2)),
-        ],
+        ]
+        + (
+            []
+            if opening
+            else [
+                pltpu.VMEM((2, hidden, width), f32),
+                pltpu.VMEM((2, hidden, width), bf16),
+                pltpu.VMEM((2, hidden, width), bf16),
+                pltpu.SemaphoreType.DMA(()),
+                pltpu.SemaphoreType.DMA((2, 2)),
+            ]
+        ),
         compiler_params=pltpu.CompilerParams(vmem_limit_bytes=VMEM_BYTES),
         cost_estimate=cost(10 * groups * rows * width * hidden * experts),
         name=name,
-    )(*pieces, *weights, wr, *([] if opening else [dwr]))
+    )(*pieces, *weights, wr, *(carried or []))
     left, (dwr, *outs) = list(outs[: len(left)]), outs[len(left) :]
     return left, dwr, outs[:groups], outs[groups:]
 
@@ -440,7 +474,7 @@
     hidden = own.shape[2]
     anywhere = pl.BlockSpec(memory_space=pl.ANY)
     pieces = [a for parts in two for a in parts] + [a for parts in cot for a in parts]
-    columns = pl.BlockSpec((groups * rows, hidden), lambda e: (0, e + first))
+    columns = pl.BlockSpec((groups * rows, hidden), lambda e: (0, e))
     part = jax.ShapeDtypeStruct((many, 2, hidden // 2, width), bf16)
     part_spec = pl.BlockSpec((1, 2, hidden // 2, width), lambda e: (e, 0, 0, 0))
     plan = dict(two=[len(parts) for parts in two], cot=[len(parts) for parts in cot])
@@ -501,6 +535,20 @@
         if self.seq == 4:
             self.moving = lax.ppermute(self.raw, "seq", [(0, 1), (3, 2)])
         return self
+
+    def inwards_with(self, other, *others):
+        if self.seq != 4:
+            return self.raw
+        other.total = plus(other.pair, tie(other.moving, others))
+        index = lax.axis_index("seq")
+        both = jnp.where((index == 0) | (index == 3), self.raw, other.total)
+        self.moving = lax.ppermute(both, "seq", [(0, 1), (1, 0), (2, 3), (3, 2)])
+        other.moving = self.moving
+        return both
+
+    def hold(self, others):
+        if self.seq == 4:
+            self.moving = tie(self.moving, others)
 
     def across(self, *others):
         if self.seq == 4:
@@ -737,8 +785,8 @@
         [[two]], [[packed]], weights, wr, None, "experts_own", lambda flops: SHORT
     )
     cots = [[cot_x], [cot_y], cot_far]
-    left, dwr, outs, gins = experts_call(
-        two_far, cots, weights, wr, dwr, "experts_far", true_cost
+    (*left, dw_kept, dw_sent), dwr, outs, gins = experts_call(
+        two_far, cots, weights, wr, [dwr, dw], "experts_far", true_cost
     )
     arrived = [spread(a, bits=bits) for a, bits in zip(gins, (2, 4, 6))]
 
@@ -750,7 +798,7 @@
             )
         return lax.optimization_barrier([raw[n : n + 1] for n in range(raw.shape[0])])
 
-    first = Line(seq, finished(*grads_call(two_far, cots, left, dw, 0, 1))[0]).inwards()
+    first = Line(seq, finished(dw_kept, dw_sent)[0]).inwards()
     left, dw = tie((left, dw), first.raw)
     parts = grads_call(two_far, cots, left, dw, 1, expert_count - 1)
     ready = first.across(arrived)
@@ -779,12 +827,11 @@
     lines[2].raw, lines[3].raw = tie((lines[2].raw, lines[3].raw), grad_tok)
     lines[2].inwards()
     ready = lines[1].across(grad_tok, flying)
-    ready = lines[0].outwards(ready)
-    lines[3].inwards()
+    ready = lines[3].inwards_with(lines[0], ready)
     ready = lines[2].across(ready)
     ready = lines[1].outwards(ready)
     ready = lines[3].across(ready)
-    ready = lines[2].outwards(ready)
+    ready = lines[2].outwards(ready, lines[1].waiting())
     dense_line = Line(seq, tie(dense, ready)).inwards()
     ready = lines[3].outwards(dense_line.raw)
 
@@ -802,6 +849,7 @@
     outputs, grad_tokens = (
         jnp.concatenate([a[n] for a in home], 0).reshape(images, span, width) for n in range(2)
     )
+    lines[3].hold(dense_line.waiting())
     grads = [line.finish() for line in lines]
     dense = dense_line.finish().astype(f32)
     expert_grads = [jnp.concatenate([g[:, n] for g in grads], 0).astype(f32) for n in range(2)]

time: 460 us -> 444 us (0.965)
  waiting for transfers between devices: 175 us -> 161 us
  Pallas kernels: 148 us -> 142 us
    ppermute x5 -> x4, waiting for transfers between devices: 77 us -> 25.3 us  [outwards(): self.moving = lax.ppermute(self.total, 'seq', [(1, 0), (2, 3)])]
    ppermute x9, waiting for transfers between devices: 27 us -> 67.1 us  [exchange(): lax.ppermute(pieces[k], 'seq', [(n, n ^ k) for n in range(count)])]
    ppermute x5 -> x4, waiting for transfers between devices: 40.1 us -> 20.3 us  [inwards(): self.moving = lax.ppermute(self.raw, 'seq', [(0, 1), (3, 2)])]
    ppermute x0 -> x1, waiting for transfers between devices: none -> 17.4 us  [inwards_with(): self.moving = lax.ppermute(both, 'seq', [(0, 1), (1, 0), (2, 3), (3, 2)])]
    pallas_call x2 -> x1, Pallas kernels: 30.7 us -> 19.9 us  [grads_call(): pl.pallas_call(functools.partial(grads_kernel, plan), grid=(many,), in_sp...]
    pallas_call x2, Pallas kernels: 81.2 us -> 86.6 us  [experts_call(): pl.pallas_call(functools.partial(expert_kernel, plan), grid=(groups,), in...]
    convert_element_type x12 -> x11, other arithmetic: 10.8 us -> 14.4 us  [plus(): return sum((a.astype(f32) for a in arrays)).astype(bf16)]
    ppermute x5 -> x4, starting transfers between devices: 18.3 us -> 14.9 us  [inwards(): self.moving = lax.ppermute(self.raw, 'seq', [(0, 1), (3, 2)])]
  transfers between devices with their start and end apart: 51 -> 50, of which waited for: 20 -> 20; matrix products, arithmetic and copies ran while one was open for 8% -> 9% of each run, Pallas kernels for 18% -> 19%
where the time goes in v3:
time: 444 us; the launch traced here: 436 us
  waiting for transfers between devices  161 us (36%)
  Pallas kernels  142 us (32%)
  starting transfers between devices  65.7 us (15%)
  other arithmetic  33 us (7%)
  local copies, waits for them, and re-layouts  18 us (4%)
  between operations  15 us (3%)
    pallas_call x2, Pallas kernels, experts_call(): pl.pallas_call(functools.partial(expert_kernel, plan), grid=(groups,), in...  86.6 us
    ppermute x9, waiting for transfers between devices, exchange(): lax.ppermute(pieces[k], 'seq', [(n, n ^ k) for n in range(count)])  67.1 us
    ppermute x26, waiting for transfers between devices, flip(): return lax.ppermute(array, 'fsdp', [(n, n ^ bits) for n in range(fsdp)])  31.1 us
    ppermute x4, waiting for transfers between devices, outwards(): self.moving = lax.ppermute(self.total, 'seq', [(1, 0), (2, 3)])  25.3 us
    ppermute x26, starting transfers between devices, flip(): return lax.ppermute(array, 'fsdp', [(n, n ^ bits) for n in range(fsdp)])  22.2 us
    pallas_call x1, Pallas kernels, back(): pl.pallas_call(back_kernel, grid=(images,), in_specs=[split] * 7 + [pl.Bl...  21.2 us
    ppermute x4, waiting for transfers between devices, inwards(): self.moving = lax.ppermute(self.raw, 'seq', [(0, 1), (3, 2)])  20.3 us
    pallas_call x1, Pallas kernels, grads_call(): pl.pallas_call(functools.partial(grads_kernel, plan), grid=(many,), in_sp...  19.9 us
  transfers between devices with their start and end apart: 50, of which 20 were waited for; matrix products, arithmetic and copies ran while one was open for 9% of the time, Pallas kernels for 19%

profile of v3, /device:TPU:0, one launch (start us, length us, event | category | flops | bytes accessed | tf_op | source)
XLA Modules:
  0.0 435.6 jit_solution(18176101962445473602)
XLA Ops:
  9.4 3.0 collective-permute-start.1
  12.4 1.5 collective-permute-start
  14.7 3.6 collective-permute-start.4
  21.4 3.2 collective-permute-done.4
  24.6 10.0 %collective-permute-done.3 = bf16[128,768]{1,0:T(8,128)(2,1)S(1)} collective-permute-done((bf16[128,768]{1,0:T(8,128)(2,1)}, bf16[128,768]{1,0:T(8,128)(2,1)S(1)}, u32[]{:S(2)}, u32[]{:S(2)}) %collective-permute-start.3) | collective-permute-done | bytes 196640 | tf_op jit(solution)/shard_map/ppermute | solution.py:511
  35.7 2.5 collective-permute-start.12
  38.2 1.9 collective-permute-start.10
  41.4 4.7 %collective-permute-done.12 = bf16[144,768]{1,0:T(8,128)(2,1)S(1)} collective-permute-done((bf16[144,768]{1,0:T(8,128)(2,1)S(1)}, bf16[144,768]{1,0:T(8,128)(2,1)S(1)}, u32[]{:S(2)}, u32[]{:S(2)}) %collective-permute-start.12) | collective-permute-done | bytes 221216 | tf_op jit(solution)/shard_map/ppermute | solution.py:511
  46.0 9.1 %collective-permute-done.11 = bf16[144,768]{1,0:T(8,128)(2,1)S(1)} collective-permute-done((bf16[144,768]{1,0:T(8,128)(2,1)S(1)}, bf16[144,768]{1,0:T(8,128)(2,1)S(1)}, u32[]{:S(2)}, u32[]{:S(2)}) %collective-permute-start.11) | collective-permute-done | bytes 221216 | tf_op jit(solution)/shard_map/ppermute | solution.py:511
  56.4 2.1 collective-permute-done.13.refs_8_
  64.0 14.7 %front.1 = (f32[4,2,64,768]{3,2,1,0:T(8,128)}, bf16[4,2,64,768]{3,2,1,0:T(8,128)(2,1)}, bf16[2,256,2304]{2,1,0:T(8,128)(2,1)}, bf16[2,256,768]{2,1,0:T(8,128)(2,...) custom-call(bf16[96,3200]{1,0:T(8,128)(2,1)} %copy-done.6, ...), custom_call_target="tpu_custom_call" | custom-call | flops 1000 | bytes 1000 | tf_op jit(solution)/shard_map/front/pallas_call | solution.py:124
  78.7 2.5 collective-permute-start.19
  84.5 1.5 collective-permute-start.23
  86.1 1.5 collective-permute-start.22
  87.6 27.9 %experts_own.1 = (bf16[4,2,768,768]{3,2,1,0:T(8,128)(2,1)}, f32[8,768]{1,0:T(8,128)}, bf16[4,128,768]{2,1,0:T(8,128)(2,1)}, bf16[4,128,768]{2,1,0:T(8,128)(2,1)}) custom-call(bf16[4,128,768]{2,1,0:T(8,128)(2,1)} %bitcast.101, bf16[4,144,768]{2,1,0:T(8,128)(2,1)} %copy-done, bf16[4,384,768]{2,1,0:T(8,128)(2,1)} %refs_7_, bf16[4,384,768]{2,1,0:T(8,128)(2,1)} %copy-done.10, ...), custom_call_target="tpu_custom_call" | custom-call | flops 1000 | bytes 1000 | tf_op jit(solution)/shard_map/experts_own/pallas_call | solution.py:380
  117.4 7.9 %collective-permute-done.23.refs_6_ = bf16[2,144,768]{2,1,0:T(8,128)(2,1)S(1)} collective-permute-done((bf16[2,144,768]{2,1,0:T(8,128)(2,1)S(1)}, bf16[2,144,768]{2,1,0:T(8,128)(2,1)S(1)}, u32[]{:S(2)}, u32[]{:S(2)}) %collective-permute-start.23) | collective-permute-done | bytes 442400 | tf_op jit(solution)/shard_map/ppermute | solution.py:501
  126.1 58.7 %experts_far.1 = (bf16[1536,2304]{1,0:T(8,128)(2,1)}, bf16[1536,2304]{1,0:T(8,128)(2,1)}, bf16[1,2,384,768]{3,2,1,0:T(8,128)(2,1)}, bf16[1,2,384,768]{3,2,1,0:T(...) custom-call(bf16[4,128,768]{2,1,0:T(8,128)(2,1)} %collective-permute, ...), custom_call_target="tpu_custom_call" | custom-call | flops 72477573120 | bytes 16777216 | tf_op jit(solution)/shard_map/experts_far/pallas_call | solution.py:380
  184.9 1.6 collective-permute-start.24
  188.5 1.6 add_convert_fusion.9
  191.5 19.9 %expert_grads.1 = (bf16[3,2,384,768]{3,2,1,0:T(8,128)(2,1)}, bf16[3,2,384,768]{3,2,1,0:T(8,128)(2,1)}) custom-call(bf16[4,128,768]{2,1,0:T(8,128)(2,1)} %collective-permute-done.17.refs_0_, bf16[4,128,768]{2,1,0:T(8,128)(2,1)} %collective-permute-done.18.refs_1_, bf16[4,128,768]{2,1,0:T(8,128)(2,1)} %collective-permute-done.19.refs_2_, ...), custom_call_target="tpu_custom_call" | custom-call | flops 43486543872 | bytes 16777216 | tf_op jit(solution)/shard_map/expert_grads/pallas_call | solution.py:481
  211.4 11.8 %collective-permute-done.25 = bf16[4,128,768]{2,1,0:T(8,128)(2,1)S(1)} collective-permute-done((bf16[4,128,768]{2,1,0:T(8,128)(2,1)}, bf16[4,128,768]{2,1,0:T(8,128)(2,1)S(1)}, u32[]{:S(2)}, u32[]{:S(2)}) %collective-permute-start.25) | collective-permute-done | bytes 786464 | tf_op jit(solution)/shard_map/ppermute | solution.py:501
  226.4 2.5 collective-permute-start.29
  231.8 1.6 fusion.26
  233.5 3.0 collective-permute-start.34
  236.4 21.2 %back.1 = (bf16[2,64,768]{2,1,0:T(8,128)(2,1)}, bf16[2,64,768]{2,1,0:T(8,128)(2,1)}, bf16[2,64,768]{2,1,0:T(8,128)(2,1)}, bf16[2,64,768]{2,1,0:T(8,128)(2,1)}, bf16[768,3200]{1,0:T(8,128)(2,1)}) custom-call(bf16[4,2,64,768]{3,2,1,0:T(8,128)(2,1)} %bitcast.129, bf16[4,2,64,768]{3,2,1,0:T(8,128)(2,1)} %bitcast.130, bf16[4,2,64,768]{3,2,1,0:T(8,128)(2,1)} %bitcast.131, ...), custom_call_target="tpu_custom_call" | custom-call | flops 30198988800 | bytes 16777216 | tf_op jit(solution)/shard_map/back/pallas_call | solution.py:649
  257.6 5.0 %collective-permute-done.29 = bf16[4,128,768]{2,1,0:T(8,128)(2,1)} collective-permute-done((bf16[4,128,768]{2,1,0:T(8,128)(2,1)}, bf16[4,128,768]{2,1,0:T(8,128)(2,1)}, u32[]{:S(2)}, u32[]{:S(2)}) %collective-permute-start.29) | collective-permute-done | bytes 786464 | tf_op jit(solution)/shard_map/ppermute | solution.py:501
  262.7 3.6 collective-permute-start.35
  266.3 3.1 add_convert_fusion.7
  269.4 1.8 collective-permute-start.38
  271.7 20.3 %collective-permute-done.35 = bf16[1,2,384,768]{3,2,1,0:T(8,128)(2,1)} collective-permute-done((bf16[1,2,384,768]{3,2,1,0:T(8,128)(2,1)}, bf16[1,2,384,768]{3,2,1,0:T(8,128)(2,1)}, u32[]{:S(2)}, u32[]{:S(2)}) %collective-permute-start.35) | collective-permute-done | bytes 1179680 | tf_op jit(solution)/shard_map/ppermute | solution.py:536
  292.0 1.6 add_convert_fusion.5
  294.3 2.0 add_convert_fusion.4
  297.6 17.4 %collective-permute-done.37 = bf16[1,2,384,768]{3,2,1,0:T(8,128)(2,1)S(1)} collective-permute-done((bf16[1,2,384,768]{3,2,1,0:T(8,128)(2,1)S(1)}, bf16[1,2,384,768]{3,2,1,0:T(8,128)(2,1)S(1)}, u32[]{:S(2)}, u32[]{:S(2)}) %collective-permute-start.37) | collective-permute-done | bytes 1179680 | tf_op jit(solution)/shard_map/ppermute | solution.py:545
  316.3 7.7 %collective-permute-done.39 = bf16[1,2,384,768]{3,2,1,0:T(8,128)(2,1)S(1)} collective-permute-done((bf16[1,2,384,768]{3,2,1,0:T(8,128)(2,1)S(1)}, bf16[1,2,384,768]{3,2,1,0:T(8,128)(2,1)S(1)}, u32[]{:S(2)}, u32[]{:S(2)}) %collective-permute-start.39) | collective-permute-done | bytes 1179680 | tf_op jit(solution)/shard_map/ppermute | solution.py:563
  325.7 1.7 collective-permute-start.41
  329.0 7.0 %collective-permute-start.40 = (bf16[96,3200]{1,0:T(8,128)(2,1)}, bf16[96,3200]{1,0:T(8,128)(2,1)S(1)}, u32[]{:S(2)}, u32[]{:S(2)}) collective-permute-start(bf16[96,3200]{1,0:T(8,128)(2,1)} %reduce-scatter.2.cloned.1.call-done), channel_id=1, source_target_pairs={{0,1},{3,2},{4,5},{7,6},{8,9},{11,10},{12,13},{15,14},{16,17},{19,... | collective-permute-start | bytes 1843208 | tf_op jit(solution)/shard_map/ppermute | solution.py:536
  336.0 13.2 %collective-permute-done.47 = bf16[1,2,384,768]{3,2,1,0:T(8,128)(2,1)} collective-permute-done((bf16[1,2,384,768]{3,2,1,0:T(8,128)(2,1)S(1)}, bf16[1,2,384,768]{3,2,1,0:T(8,128)(2,1)}, u32[]{:S(2)}, u32[]{:S(2)}) %collective-permute-start.47) | collective-permute-done | bytes 1179680 | tf_op jit(solution)/shard_map/ppermute | solution.py:563
  349.2 1.4 broadcast_select_fusion.1
  351.5 3.0 add_convert_fusion.1
  354.5 1.6 collective-permute-start.48
  357.0 2.2 convert_add_fusion
  360.2 5.9 %collective-permute-start.42 = (bf16[2,2,64,768]{3,2,1,0:T(8,128)(2,1)S(1)}, bf16[2,2,64,768]{3,2,1,0:T(8,128)(2,1)S(1)}, u32[]{:S(2)}, u32[]{:S(2)}) collective-permute-start(bf16[2,2,64,768]{3,2,1,0:T(8,128)(2,1)S(1)} %pad_maximum_fusion.5), channel_id=1, source_target_pairs={{0,1},{1,0},{2,3},{3,2},{4,5},{5,4},{6,7},{7,6},{8,9},{9,8},{10,11... | collective-permute-start | bytes 1179656 | tf_op jit(solution)/shard_map/ppermute | solution.py:511
  366.8 2.0 collective-permute-start.44
  370.3 40.2 %collective-permute-done.42 = bf16[2,2,64,768]{3,2,1,0:T(8,128)(2,1)S(1)} collective-permute-done((bf16[2,2,64,768]{3,2,1,0:T(8,128)(2,1)S(1)}, bf16[2,2,64,768]{3,2,1,0:T(8,128)(2,1)S(1)}, u32[]{:S(2)}, u32[]{:S(2)}) %collective-permute-start.42) | collective-permute-done | bytes 393248 | tf_op jit(solution)/shard_map/ppermute | solution.py:511
  412.7 4.3 collective-permute-done.46
  420.2 1.9 broadcast_select_fusion
  423.4 2.6 maximum_convert_fusion.1
  426.0 2.6 maximum_convert_fusion
  (206 shorter events, 49.1 us)
Async XLA Ops:
  7.2 321.8 %reduce-scatter.2.cloned.1.call-start = ((), (), s32[]{:S(2)}) async-start(), calls=%async_computation.1 | async-start | bytes 5529600 | tf_op jit(solution)/shard_map/reduce_scatter | solution.py:826
  9.4 26.3 %collective-permute-start.1 = (bf16[96,3200]{1,0:T(8,128)(2,1)S(1)}, bf16[96,3200]{1,0:T(8,128)(2,1)S(1)}, u32[]{:S(2)}, u32[]{:S(2)}) collective-permute-start(bf16[96,3200]{1,0:T(8,128)(2,1)S(1)} %fusion.5.refs_0_), channel_id=1, source_target_pairs={{0,16},{4,20},{8,24},{12,28},{16,0},{20,4},{24,8},{28,12},{1,17},{... | collective-permute-start | bytes 1843208 | tf_op jit(solution)/shard_map/ppermute | solution.py:501
  12.4 23.2 %collective-permute-start = (bf16[96,3200]{1,0:T(8,128)(2,1)S(1)}, bf16[96,3200]{1,0:T(8,128)(2,1)S(1)}, u32[]{:S(2)}, u32[]{:S(2)}) collective-permute-start(bf16[96,3200]{1,0:T(8,128)(2,1)S(1)} %fusion.5.refs_0_), channel_id=1, source_target_pairs={{0,8},{4,12},{8,0},{12,4},{16,24},{20,28},{24,16},{28,20},{1,9},{5... | collective-permute-start | bytes 1843208 | tf_op jit(solution)/shard_map/ppermute | solution.py:501
  14.7 9.9 %collective-permute-start.4 = (bf16[128,768]{1,0:T(8,128)(2,1)}, bf16[128,768]{1,0:T(8,128)(2,1)S(1)}, u32[]{:S(2)}, u32[]{:S(2)}) collective-permute-start(bf16[128,768]{1,0:T(8,128)(2,1)} %get-tuple-element.238), channel_id=1, source_target_pairs={{0,3},{1,2},{2,1},{3,0},{4,7},{5,6},{6,5},{7,4},{8,11},{9,10},{10,... | collective-permute-start | bytes 589832 | tf_op jit(solution)/shard_map/ppermute | solution.py:511
  18.3 16.3 %collective-permute-start.3 = (bf16[128,768]{1,0:T(8,128)(2,1)}, bf16[128,768]{1,0:T(8,128)(2,1)S(1)}, u32[]{:S(2)}, u32[]{:S(2)}) collective-permute-start(bf16[128,768]{1,0:T(8,128)(2,1)} %get-tuple-element.239), channel_id=1, source_target_pairs={{0,2},{1,3},{2,0},{3,1},{4,6},{5,7},{6,4},{7,5},{8,10},{9,11},{10,... | collective-permute-start | bytes 589832 | tf_op jit(solution)/shard_map/ppermute | solution.py:511
  18.3 16.3 %collective-permute-start.2 = (bf16[128,768]{1,0:T(8,128)(2,1)S(1)}, bf16[128,768]{1,0:T(8,128)(2,1)S(1)}, u32[]{:S(2)}, u32[]{:S(2)}) collective-permute-start(bf16[128,768]{1,0:T(8,128)(2,1)S(1)} %get-tuple-element.240), channel_id=1, source_target_pairs={{0,1},{1,0},{2,3},{3,2},{4,5},{5,4},{6,7},{7,6},{8,9},{9,8},{10,11... | collective-permute-start | bytes 589832 | tf_op jit(solution)/shard_map/ppermute | solution.py:511
  35.7 10.3 %collective-permute-start.12 = (bf16[144,768]{1,0:T(8,128)(2,1)S(1)}, bf16[144,768]{1,0:T(8,128)(2,1)S(1)}, u32[]{:S(2)}, u32[]{:S(2)}) collective-permute-start(bf16[144,768]{1,0:T(8,128)(2,1)S(1)} %get-tuple-element.234), channel_id=1, source_target_pairs={{0,3},{1,2},{2,1},{3,0},{4,7},{5,6},{6,5},{7,4},{8,11},{9,10},{10,... | collective-permute-start | bytes 663560 | tf_op jit(solution)/shard_map/ppermute | solution.py:511
  38.2 16.9 %collective-permute-start.11 = (bf16[144,768]{1,0:T(8,128)(2,1)S(1)}, bf16[144,768]{1,0:T(8,128)(2,1)S(1)}, u32[]{:S(2)}, u32[]{:S(2)}) collective-permute-start(bf16[144,768]{1,0:T(8,128)(2,1)S(1)} %get-tuple-element.235), channel_id=1, source_target_pairs={{0,2},{1,3},{2,0},{3,1},{4,6},{5,7},{6,4},{7,5},{8,10},{9,11},{10,... | collective-permute-start | bytes 663560 | tf_op jit(solution)/shard_map/ppermute | solution.py:511
  38.2 16.9 %collective-permute-start.10 = (bf16[144,768]{1,0:T(8,128)(2,1)S(1)}, bf16[144,768]{1,0:T(8,128)(2,1)S(1)}, u32[]{:S(2)}, u32[]{:S(2)}) collective-permute-start(bf16[144,768]{1,0:T(8,128)(2,1)S(1)} %get-tuple-element.236), channel_id=1, source_target_pairs={{0,1},{1,0},{2,3},{3,2},{4,5},{5,4},{6,7},{7,6},{8,9},{9,8},{10,11... | collective-permute-start | bytes 663560 | tf_op jit(solution)/shard_map/ppermute | solution.py:511
  40.2 15.6 %collective-permute-start.9 = (bf16[48,3200]{1,0:T(8,128)(2,1)S(1)}, bf16[48,3200]{1,0:T(8,128)(2,1)S(1)}, u32[]{:S(2)}, u32[]{:S(2)}) collective-permute-start(bf16[48,3200]{1,0:T(8,128)(2,1)S(1)} %slice.204), channel_id=1, source_target_pairs={{0,8},{4,12},{8,0},{12,4},{16,24},{20,28},{24,16},{28,20},{1,9},{5... | collective-permute-start | bytes 921608 | tf_op jit(solution)/shard_map/ppermute | solution.py:501
  40.8 15.0 %collective-permute-start.8 = (bf16[48,3200]{1,0:T(8,128)(2,1)S(1)}, bf16[48,3200]{1,0:T(8,128)(2,1)S(1)}, u32[]{:S(2)}, u32[]{:S(2)}) collective-permute-start(bf16[48,3200]{1,0:T(8,128)(2,1)S(1)} %slice.203), channel_id=1, source_target_pairs={{0,16},{4,20},{8,24},{12,28},{16,0},{20,4},{24,8},{28,12},{1,17},{... | collective-permute-start | bytes 921608 | tf_op jit(solution)/shard_map/ppermute | solution.py:501
  46.0 10.4 %collective-permute-start.5 = (bf16[96,3200]{1,0:T(8,128)(2,1)S(1)}, bf16[96,3200]{1,0:T(8,128)(2,1)S(1)}, u32[]{:S(2)}, u32[]{:S(2)}) collective-permute-start(bf16[96,3200]{1,0:T(8,128)(2,1)S(1)} %fusion.5.refs_0_), channel_id=1, source_target_pairs={{0,4},{4,0},{8,12},{12,8},{16,20},{20,16},{24,28},{28,24},{1,5},{5... | collective-permute-start | bytes 1843208 | tf_op jit(solution)/shard_map/ppermute | solution.py:501
  55.1 3.8 collective-permute-start.6
  55.2 3.8 collective-permute-start.7
  59.0 25.5 %collective-permute-start.15 = (bf16[4,384,768]{2,1,0:T(8,128)(2,1)}, bf16[4,384,768]{2,1,0:T(8,128)(2,1)S(1)}, u32[]{:S(2)}, u32[]{:S(2)}) collective-permute-start(bf16[4,384,768]{2,1,0:T(8,128)(2,1)} %refs_7_), channel_id=1, source_target_pairs={{0,4},{4,0},{8,12},{12,8},{16,20},{20,16},{24,28},{28,24},{1,5},{5... | collective-permute-start | bytes 7077896 | tf_op jit(solution)/shard_map/ppermute | solution.py:501
  59.2 26.9 %collective-permute-start.16 = (bf16[4,384,768]{2,1,0:T(8,128)(2,1)}, bf16[4,384,768]{2,1,0:T(8,128)(2,1)}, u32[]{:S(2)}, u32[]{:S(2)}) collective-permute-start(bf16[4,384,768]{2,1,0:T(8,128)(2,1)} %refs_9_), channel_id=1, source_target_pairs={{0,4},{4,0},{8,12},{12,8},{16,20},{20,16},{24,28},{28,24},{1,5},{5... | collective-permute-start | bytes 7077896 | tf_op jit(solution)/shard_map/ppermute | solution.py:501
  59.5 21.8 %collective-permute-start.21 = (bf16[4,144,768]{2,1,0:T(8,128)(2,1)S(1)}, bf16[4,144,768]{2,1,0:T(8,128)(2,1)}, u32[]{:S(2)}, u32[]{:S(2)}) collective-permute-start(bf16[4,144,768]{2,1,0:T(8,128)(2,1)S(1)} %pad_maximum_fusion.refs_1_), channel_id=1, source_target_pairs={{0,16},{4,20},{8,24},{12,28},{16,0},{20,4},{24,8},{28,12},{1,17},{... | collective-permute-start | bytes 2654216 | tf_op jit(solution)/shard_map/ppermute | solution.py:501
  60.1 21.8 %collective-permute-start.20 = (bf16[4,144,768]{2,1,0:T(8,128)(2,1)S(1)}, bf16[4,144,768]{2,1,0:T(8,128)(2,1)}, u32[]{:S(2)}, u32[]{:S(2)}) collective-permute-start(bf16[4,144,768]{2,1,0:T(8,128)(2,1)S(1)} %pad_maximum_fusion.refs_1_), channel_id=1, source_target_pairs={{0,8},{4,12},{8,0},{12,4},{16,24},{20,28},{24,16},{28,20},{1,9},{5... | collective-permute-start | bytes 2654216 | tf_op jit(solution)/shard_map/ppermute | solution.py:501
  78.7 36.7 %collective-permute-start.19 = (bf16[4,128,768]{2,1,0:T(8,128)(2,1)}, bf16[4,128,768]{2,1,0:T(8,128)(2,1)}, u32[]{:S(2)}, u32[]{:S(2)}) collective-permute-start(bf16[4,128,768]{2,1,0:T(8,128)(2,1)} %bitcast.98), channel_id=1, source_target_pairs={{0,24},{4,28},{8,16},{12,20},{16,8},{20,12},{24,0},{28,4},{1,25},{... | collective-permute-start | bytes 2359304 | tf_op jit(solution)/shard_map/ppermute | solution.py:501
  81.3 35.1 %collective-permute-start.18 = (bf16[4,128,768]{2,1,0:T(8,128)(2,1)}, bf16[4,128,768]{2,1,0:T(8,128)(2,1)}, u32[]{:S(2)}, u32[]{:S(2)}) collective-permute-start(bf16[4,128,768]{2,1,0:T(8,128)(2,1)} %bitcast.99), channel_id=1, source_target_pairs={{0,16},{4,20},{8,24},{12,28},{16,0},{20,4},{24,8},{28,12},{1,17},{... | collective-permute-start | bytes 2359304 | tf_op jit(solution)/shard_map/ppermute | solution.py:501
  81.9 35.6 %collective-permute-start.17 = (bf16[4,128,768]{2,1,0:T(8,128)(2,1)}, bf16[4,128,768]{2,1,0:T(8,128)(2,1)}, u32[]{:S(2)}, u32[]{:S(2)}) collective-permute-start(bf16[4,128,768]{2,1,0:T(8,128)(2,1)} %bitcast.100), channel_id=1, source_target_pairs={{0,8},{4,12},{8,0},{12,4},{16,24},{20,28},{24,16},{28,20},{1,9},{5... | collective-permute-start | bytes 2359304 | tf_op jit(solution)/shard_map/ppermute | solution.py:501
  84.5 40.8 %collective-permute-start.23 = (bf16[2,144,768]{2,1,0:T(8,128)(2,1)S(1)}, bf16[2,144,768]{2,1,0:T(8,128)(2,1)S(1)}, u32[]{:S(2)}, u32[]{:S(2)}) collective-permute-start(bf16[2,144,768]{2,1,0:T(8,128)(2,1)S(1)} %slice.267), channel_id=1, source_target_pairs={{0,8},{4,12},{8,0},{12,4},{16,24},{20,28},{24,16},{28,20},{1,9},{5... | collective-permute-start | bytes 1327112 | tf_op jit(solution)/shard_map/ppermute | solution.py:501
  86.1 39.7 %collective-permute-start.22 = (bf16[2,144,768]{2,1,0:T(8,128)(2,1)S(1)}, bf16[2,144,768]{2,1,0:T(8,128)(2,1)}, u32[]{:S(2)}, u32[]{:S(2)}) collective-permute-start(bf16[2,144,768]{2,1,0:T(8,128)(2,1)S(1)} %slice.266), channel_id=1, source_target_pairs={{0,16},{4,20},{8,24},{12,28},{16,0},{20,4},{24,8},{28,12},{1,17},{... | collective-permute-start | bytes 1327112 | tf_op jit(solution)/shard_map/ppermute | solution.py:501
  184.9 3.6 collective-permute-start.30
  184.9 26.4 %collective-permute-start.24 = (bf16[4,128,768]{2,1,0:T(8,128)(2,1)}, bf16[4,128,768]{2,1,0:T(8,128)(2,1)S(1)}, u32[]{:S(2)}, u32[]{:S(2)}) collective-permute-start(bf16[4,128,768]{2,1,0:T(8,128)(2,1)} %get-tuple-element.104), channel_id=1, source_target_pairs={{0,8},{4,12},{8,0},{12,4},{16,24},{20,28},{24,16},{28,20},{1,9},{5... | collective-permute-start | bytes 2359304 | tf_op jit(solution)/shard_map/ppermute | solution.py:501
  186.5 36.7 %collective-permute-start.25 = (bf16[4,128,768]{2,1,0:T(8,128)(2,1)}, bf16[4,128,768]{2,1,0:T(8,128)(2,1)S(1)}, u32[]{:S(2)}, u32[]{:S(2)}) collective-permute-start(bf16[4,128,768]{2,1,0:T(8,128)(2,1)} %get-tuple-element.105), channel_id=1, source_target_pairs={{0,16},{4,20},{8,24},{12,28},{16,0},{20,4},{24,8},{28,12},{1,17},{... | collective-permute-start | bytes 2359304 | tf_op jit(solution)/shard_map/ppermute | solution.py:501
  187.2 36.0 %collective-permute-start.26 = (bf16[4,128,768]{2,1,0:T(8,128)(2,1)}, bf16[4,128,768]{2,1,0:T(8,128)(2,1)}, u32[]{:S(2)}, u32[]{:S(2)}) collective-permute-start(bf16[4,128,768]{2,1,0:T(8,128)(2,1)} %get-tuple-element.106), channel_id=1, source_target_pairs={{0,24},{4,28},{8,16},{12,20},{16,8},{20,12},{24,0},{28,4},{1,25},{... | collective-permute-start | bytes 2359304 | tf_op jit(solution)/shard_map/ppermute | solution.py:501
  190.1 34.0 %collective-permute-start.31 = (bf16[1,2,384,768]{3,2,1,0:T(8,128)(2,1)S(1)}, bf16[1,2,384,768]{3,2,1,0:T(8,128)(2,1)S(1)}, u32[]{:S(2)}, u32[]{:S(2)}) collective-permute-start(bf16[1,2,384,768]{3,2,1,0:T(8,128)(2,1)S(1)} %add_convert_fusion.9), channel_id=1, source_target_pairs={{0,1},{3,2},{4,5},{7,6},{8,9},{11,10},{12,13},{15,14},{16,17},{19,... | collective-permute-start | bytes 3538952 | tf_op jit(solution)/shard_map/ppermute | solution.py:536
  224.4 6.5 %collective-permute-start.32 = (bf16[3,2,384,768]{3,2,1,0:T(8,128)(2,1)}, bf16[3,2,384,768]{3,2,1,0:T(8,128)(2,1)S(1)}, u32[]{:S(2)}, u32[]{:S(2)}) collective-permute-start(bf16[3,2,384,768]{3,2,1,0:T(8,128)(2,1)} %get-tuple-element.122), channel_id=1, source_target_pairs={{0,4},{4,0},{8,12},{12,8},{16,20},{20,16},{24,28},{28,24},{1,5},{5... | collective-permute-start | bytes 10616840 | tf_op jit(solution)/shard_map/ppermute | solution.py:501
  225.4 32.2 %collective-permute-start.27 = (bf16[4,128,768]{2,1,0:T(8,128)(2,1)}, bf16[4,128,768]{2,1,0:T(8,128)(2,1)}, u32[]{:S(2)}, u32[]{:S(2)}) collective-permute-start(bf16[4,128,768]{2,1,0:T(8,128)(2,1)} %get-tuple-element.107), channel_id=1, source_target_pairs={{0,8},{4,12},{8,0},{12,4},{16,24},{20,28},{24,16},{28,20},{1,9},{5... | collective-permute-start | bytes 2359304 | tf_op jit(solution)/shard_map/ppermute | solution.py:501
  225.4 32.2 %collective-permute-start.28 = (bf16[4,128,768]{2,1,0:T(8,128)(2,1)}, bf16[4,128,768]{2,1,0:T(8,128)(2,1)}, u32[]{:S(2)}, u32[]{:S(2)}) collective-permute-start(bf16[4,128,768]{2,1,0:T(8,128)(2,1)} %get-tuple-element.108), channel_id=1, source_target_pairs={{0,16},{4,20},{8,24},{12,28},{16,0},{20,4},{24,8},{28,12},{1,17},{... | collective-permute-start | bytes 2359304 | tf_op jit(solution)/shard_map/ppermute | solution.py:501
  226.4 36.3 %collective-permute-start.29 = (bf16[4,128,768]{2,1,0:T(8,128)(2,1)}, bf16[4,128,768]{2,1,0:T(8,128)(2,1)}, u32[]{:S(2)}, u32[]{:S(2)}) collective-permute-start(bf16[4,128,768]{2,1,0:T(8,128)(2,1)} %get-tuple-element.109), channel_id=1, source_target_pairs={{0,24},{4,28},{8,16},{12,20},{16,8},{20,12},{24,0},{28,4},{1,25},{... | collective-permute-start | bytes 2359304 | tf_op jit(solution)/shard_map/ppermute | solution.py:501
  228.9 33.8 %collective-permute-start.33 = (bf16[1,2,384,768]{3,2,1,0:T(8,128)(2,1)S(1)}, bf16[1,2,384,768]{3,2,1,0:T(8,128)(2,1)S(1)}, u32[]{:S(2)}, u32[]{:S(2)}) collective-permute-start(bf16[1,2,384,768]{3,2,1,0:T(8,128)(2,1)S(1)} %add_convert_fusion.8), channel_id=1, source_target_pairs={{1,2},{2,1},{5,6},{6,5},{9,10},{10,9},{13,14},{14,13},{17,18},{18,... | collective-permute-start | bytes 3538952 | tf_op jit(solution)/shard_map/ppermute | solution.py:556
  233.5 29.2 %collective-permute-start.34 = (bf16[1,2,384,768]{3,2,1,0:T(8,128)(2,1)}, bf16[1,2,384,768]{3,2,1,0:T(8,128)(2,1)}, u32[]{:S(2)}, u32[]{:S(2)}) collective-permute-start(bf16[1,2,384,768]{3,2,1,0:T(8,128)(2,1)} %get-tuple-element.123), channel_id=1, source_target_pairs={{0,1},{3,2},{4,5},{7,6},{8,9},{11,10},{12,13},{15,14},{16,17},{19,... | collective-permute-start | bytes 3538952 | tf_op jit(solution)/shard_map/ppermute | solution.py:536
  262.7 29.3 %collective-permute-start.35 = (bf16[1,2,384,768]{3,2,1,0:T(8,128)(2,1)}, bf16[1,2,384,768]{3,2,1,0:T(8,128)(2,1)}, u32[]{:S(2)}, u32[]{:S(2)}) collective-permute-start(bf16[1,2,384,768]{3,2,1,0:T(8,128)(2,1)} %get-tuple-element.141), channel_id=1, source_target_pairs={{0,1},{3,2},{4,5},{7,6},{8,9},{11,10},{12,13},{15,14},{16,17},{19,... | collective-permute-start | bytes 3538952 | tf_op jit(solution)/shard_map/ppermute | solution.py:536
  269.4 24.9 %collective-permute-start.38 = (bf16[1,2,384,768]{3,2,1,0:T(8,128)(2,1)}, bf16[1,2,384,768]{3,2,1,0:T(8,128)(2,1)}, u32[]{:S(2)}, u32[]{:S(2)}) collective-permute-start(bf16[1,2,384,768]{3,2,1,0:T(8,128)(2,1)} %add_convert_fusion.7), channel_id=1, source_target_pairs={{1,2},{2,1},{5,6},{6,5},{9,10},{10,9},{13,14},{14,13},{17,18},{18,... | collective-permute-start | bytes 3538952 | tf_op jit(solution)/shard_map/ppermute | solution.py:556
  271.7 43.4 %collective-permute-start.37 = (bf16[1,2,384,768]{3,2,1,0:T(8,128)(2,1)S(1)}, bf16[1,2,384,768]{3,2,1,0:T(8,128)(2,1)S(1)}, u32[]{:S(2)}, u32[]{:S(2)}) collective-permute-start(bf16[1,2,384,768]{3,2,1,0:T(8,128)(2,1)S(1)} %broadcast_select_fusion.4), channel_id=1, source_target_pairs={{0,1},{1,0},{2,3},{3,2},{4,5},{5,4},{6,7},{7,6},{8,9},{9,8},{10,11... | collective-permute-start | bytes 3538952 | tf_op jit(solution)/shard_map/ppermute | solution.py:545
  293.6 22.8 %collective-permute-start.36 = (bf16[1,2,384,768]{3,2,1,0:T(8,128)(2,1)S(1)}, bf16[1,2,384,768]{3,2,1,0:T(8,128)(2,1)S(1)}, u32[]{:S(2)}, u32[]{:S(2)}) collective-permute-start(bf16[1,2,384,768]{3,2,1,0:T(8,128)(2,1)S(1)} %add_convert_fusion.5), channel_id=1, source_target_pairs={{1,2},{2,1},{5,6},{6,5},{9,10},{10,9},{13,14},{14,13},{17,18},{18,... | collective-permute-start | bytes 3538952 | tf_op jit(solution)/shard_map/ppermute | solution.py:556
  296.3 27.8 %collective-permute-start.39 = (bf16[1,2,384,768]{3,2,1,0:T(8,128)(2,1)S(1)}, bf16[1,2,384,768]{3,2,1,0:T(8,128)(2,1)S(1)}, u32[]{:S(2)}, u32[]{:S(2)}) collective-permute-start(bf16[1,2,384,768]{3,2,1,0:T(8,128)(2,1)S(1)} %add_convert_fusion.4), channel_id=1, source_target_pairs={{1,0},{2,3},{5,4},{6,7},{9,8},{10,11},{13,12},{14,15},{17,16},{18,... | collective-permute-start | bytes 3538952 | tf_op jit(solution)/shard_map/ppermute | solution.py:563
  324.4 24.8 %collective-permute-start.47 = (bf16[1,2,384,768]{3,2,1,0:T(8,128)(2,1)S(1)}, bf16[1,2,384,768]{3,2,1,0:T(8,128)(2,1)}, u32[]{:S(2)}, u32[]{:S(2)}) collective-permute-start(bf16[1,2,384,768]{3,2,1,0:T(8,128)(2,1)S(1)} %add_convert_fusion.2), channel_id=1, source_target_pairs={{1,0},{2,3},{5,4},{6,7},{9,8},{10,11},{13,12},{14,15},{17,16},{18,... | collective-permute-start | bytes 3538952 | tf_op jit(solution)/shard_map/ppermute | solution.py:563
  325.7 25.8 %collective-permute-start.41 = (bf16[1,2,384,768]{3,2,1,0:T(8,128)(2,1)}, bf16[1,2,384,768]{3,2,1,0:T(8,128)(2,1)}, u32[]{:S(2)}, u32[]{:S(2)}) collective-permute-start(bf16[1,2,384,768]{3,2,1,0:T(8,128)(2,1)} %add_convert_fusion.3), channel_id=1, source_target_pairs={{1,2},{2,1},{5,6},{6,5},{9,10},{10,9},{13,14},{14,13},{17,18},{18,... | collective-permute-start | bytes 3538952 | tf_op jit(solution)/shard_map/ppermute | solution.py:556
  329.0 27.0 %collective-permute-start.40 = (bf16[96,3200]{1,0:T(8,128)(2,1)}, bf16[96,3200]{1,0:T(8,128)(2,1)S(1)}, u32[]{:S(2)}, u32[]{:S(2)}) collective-permute-start(bf16[96,3200]{1,0:T(8,128)(2,1)} %reduce-scatter.2.cloned.1.call-done), channel_id=1, source_target_pairs={{0,1},{3,2},{4,5},{7,6},{8,9},{11,10},{12,13},{15,14},{16,17},{19,... | collective-permute-start | bytes 1843208 | tf_op jit(solution)/shard_map/ppermute | solution.py:536
  354.5 65.8 %collective-permute-start.48 = (bf16[1,2,384,768]{3,2,1,0:T(8,128)(2,1)}, bf16[1,2,384,768]{3,2,1,0:T(8,128)(2,1)}, u32[]{:S(2)}, u32[]{:S(2)}) collective-permute-start(bf16[1,2,384,768]{3,2,1,0:T(8,128)(2,1)} %add_convert_fusion.1), channel_id=1, source_target_pairs={{1,0},{2,3},{5,4},{6,7},{9,8},{10,11},{13,12},{14,15},{17,16},{18,... | collective-permute-start | bytes 3538952 | tf_op jit(solution)/shard_map/ppermute | solution.py:563
  356.2 12.6 %collective-permute-start.45 = (bf16[96,3200]{1,0:T(8,128)(2,1)S(1)}, bf16[96,3200]{1,0:T(8,128)(2,1)S(1)}, u32[]{:S(2)}, u32[]{:S(2)}) collective-permute-start(bf16[96,3200]{1,0:T(8,128)(2,1)S(1)} %add_convert_fusion.11), channel_id=1, source_target_pairs={{1,2},{2,1},{5,6},{6,5},{9,10},{10,9},{13,14},{14,13},{17,18},{18,... | collective-permute-start | bytes 1843208 | tf_op jit(solution)/shard_map/ppermute | solution.py:556
  360.2 50.2 %collective-permute-start.42 = (bf16[2,2,64,768]{3,2,1,0:T(8,128)(2,1)S(1)}, bf16[2,2,64,768]{3,2,1,0:T(8,128)(2,1)S(1)}, u32[]{:S(2)}, u32[]{:S(2)}) collective-permute-start(bf16[2,2,64,768]{3,2,1,0:T(8,128)(2,1)S(1)} %pad_maximum_fusion.5), channel_id=1, source_target_pairs={{0,1},{1,0},{2,3},{3,2},{4,5},{5,4},{6,7},{7,6},{8,9},{9,8},{10,11... | collective-permute-start | bytes 1179656 | tf_op jit(solution)/shard_map/ppermute | solution.py:511
  366.2 44.2 %collective-permute-start.43 = (bf16[2,2,64,768]{3,2,1,0:T(8,128)(2,1)S(1)}, bf16[2,2,64,768]{3,2,1,0:T(8,128)(2,1)S(1)}, u32[]{:S(2)}, u32[]{:S(2)}) collective-permute-start(bf16[2,2,64,768]{3,2,1,0:T(8,128)(2,1)S(1)} %pad_maximum_fusion.6), channel_id=1, source_target_pairs={{0,2},{1,3},{2,0},{3,1},{4,6},{5,7},{6,4},{7,5},{8,10},{9,11},{10,... | collective-permute-start | bytes 1179656 | tf_op jit(solution)/shard_map/ppermute | solution.py:511
  366.8 43.7 %collective-permute-start.44 = (bf16[2,2,64,768]{3,2,1,0:T(8,128)(2,1)S(1)}, bf16[2,2,64,768]{3,2,1,0:T(8,128)(2,1)S(1)}, u32[]{:S(2)}, u32[]{:S(2)}) collective-permute-start(bf16[2,2,64,768]{3,2,1,0:T(8,128)(2,1)S(1)} %pad_maximum_fusion.7), channel_id=1, source_target_pairs={{0,3},{1,2},{2,1},{3,0},{4,7},{5,6},{6,5},{7,4},{8,11},{9,10},{10,... | collective-permute-start | bytes 1179656 | tf_op jit(solution)/shard_map/ppermute | solution.py:511
  369.0 48.0 %collective-permute-start.46 = (bf16[96,3200]{1,0:T(8,128)(2,1)S(1)}, bf16[96,3200]{1,0:T(8,128)(2,1)S(1)}, u32[]{:S(2)}, u32[]{:S(2)}) collective-permute-start(bf16[96,3200]{1,0:T(8,128)(2,1)S(1)} %add_convert_fusion.10), channel_id=1, source_target_pairs={{1,0},{2,3},{5,4},{6,7},{9,8},{10,11},{13,12},{14,15},{17,16},{18,... | collective-permute-start | bytes 1843208 | tf_op jit(solution)/shard_map/ppermute | solution.py:563
  (41 other events, 289.7 us)
Sparse Core Ops, SparseCore 0:
  262.8 53.6 reduce-scatter.1

commit v4 on v3

--- a/solution.py
+++ b/solution.py
@@ -746,6 +746,10 @@
         from_x = from_y = full
         near, far = [(n, 0, full[n * (width // 8) : (n + 1) * (width // 8)]) for n in range(8)], []
 
+    mine = lax.dynamic_slice_in_dim(padding, seq_index * own, own, 0).reshape(own, seq, span)
+    mine = jnp.stack(relative([mine[:, b] for b in range(seq)], seq_index))
+    vis = jnp.where(mine > 0, 0.0, neg_fill).astype(f32)
+    vis = jnp.swapaxes(vis, 0, 1).reshape(own, 1, length)
     live = lax.dynamic_slice_in_dim(padding, seq_index * span, span, 1)
     kept = kept_pairs(
         routes.reshape(rows, 2), live.reshape(rows), priority.reshape(rows), expert_count, capacity
@@ -756,7 +760,7 @@
     ).astype(bf16)
     cot = cotangent * live[:, :, None].astype(bf16)
     packed = jnp.concatenate([cot.reshape(seq, own * span, width), kept], 1)
-    packed = tie(packed, tok, from_x, from_y)
+    packed = tie(packed, tok, from_x, from_y, vis, mine)
     packed = jnp.stack(exchange([picked(packed, k) for k in range(seq)]))
     late = tie([a for _, _, a in far], packed)
     far += [(r + 1, skip, spread(a, bits=1)) for (r, skip, _), a in zip(far, late)]
@@ -773,10 +777,6 @@
     win, wdn = tie((win, wdn), pieces)
     weights = [win, spread(win, bits=1), wdn, spread(wdn, bits=1)]
 
-    mine = lax.dynamic_slice_in_dim(padding, seq_index * own, own, 0).reshape(own, seq, span)
-    mine = jnp.stack(relative([mine[:, b] for b in range(seq)], seq_index))
-    vis = jnp.where(mine > 0, 0.0, neg_fill).astype(f32)
-    vis = jnp.swapaxes(vis, 0, 1).reshape(own, 1, length)
     middle, two, proj, att, prob, wall, wr, small = front(tok, pieces, offsets, vis, place)
     two = two.reshape(seq, own * span, width)
     two_far = [[spread(two, bits=bits)] for bits in (2, 4, 6)]
@@ -844,15 +844,14 @@
         combined = sum(a[k].astype(f32) for a in outs)
         home.append(jnp.stack([(alive * (middle[k] + combined)).astype(bf16), grad_tok[k]]))
     home = exchange(home)
-    ready = dense_line.outwards(ready)
-    home = relative(tie(home, ready), seq_index)
+    lines[3].hold(dense_line.outwards(ready))
+    grads = [line.finish() for line in lines]
+    expert_grads = [jnp.concatenate([g[:, n] for g in grads], 0).astype(f32) for n in range(2)]
+    home = relative(tie(home, expert_grads), seq_index)
     outputs, grad_tokens = (
         jnp.concatenate([a[n] for a in home], 0).reshape(images, span, width) for n in range(2)
     )
-    lines[3].hold(dense_line.waiting())
-    grads = [line.finish() for line in lines]
     dense = dense_line.finish().astype(f32)
-    expert_grads = [jnp.concatenate([g[:, n] for g in grads], 0).astype(f32) for n in range(2)]
     tail = dense[:, 4 * width :]
     return (
         outputs,

time: 444 us -> 436 us (0.982)
  local copies, waits for them, and re-layouts: 18 us -> 12.5 us
    ppermute x9, waiting for transfers between devices: 67.1 us -> 28.4 us  [exchange(): lax.ppermute(pieces[k], 'seq', [(n, n ^ k) for n in range(count)])]
    ppermute x4, waiting for transfers between devices: 25.3 us -> 61.7 us  [outwards(): self.moving = lax.ppermute(self.total, 'seq', [(1, 0), (2, 3)])]
  transfers between devices with their start and end apart: 50 -> 50, of which waited for: 20 -> 21; matrix products, arithmetic and copies ran while one was open for 9% -> 9% of each run, Pallas kernels for 19% -> 19%
where the time goes in v4:
time: 436 us; the launch traced here: 430 us
  waiting for transfers between devices  164 us (38%)
  Pallas kernels  142 us (33%)
  starting transfers between devices  64.3 us (15%)
  other arithmetic  31.3 us (7%)
  between operations  15 us (3%)
  local copies, waits for them, and re-layouts  12.5 us (3%)
    pallas_call x2, Pallas kernels, experts_call(): pl.pallas_call(functools.partial(expert_kernel, plan), grid=(groups,), in...  86.6 us
    ppermute x4, waiting for transfers between devices, outwards(): self.moving = lax.ppermute(self.total, 'seq', [(1, 0), (2, 3)])  61.7 us
    ppermute x26, waiting for transfers between devices, flip(): return lax.ppermute(array, 'fsdp', [(n, n ^ bits) for n in range(fsdp)])  35.2 us
    ppermute x9, waiting for transfers between devices, exchange(): lax.ppermute(pieces[k], 'seq', [(n, n ^ k) for n in range(count)])  28.4 us
    ppermute x26, starting transfers between devices, flip(): return lax.ppermute(array, 'fsdp', [(n, n ^ bits) for n in range(fsdp)])  22.3 us
    pallas_call x1, Pallas kernels, back(): pl.pallas_call(back_kernel, grid=(images,), in_specs=[split] * 7 + [pl.Bl...  21.2 us
    ppermute x4, waiting for transfers between devices, inwards(): self.moving = lax.ppermute(self.raw, 'seq', [(0, 1), (3, 2)])  20.4 us
    pallas_call x1, Pallas kernels, grads_call(): pl.pallas_call(functools.partial(grads_kernel, plan), grid=(many,), in_sp...  19.9 us
  transfers between devices with their start and end apart: 50, of which 21 were waited for; matrix products, arithmetic and copies ran while one was open for 9% of the time, Pallas kernels for 19%

profile of v4, /device:TPU:0, one launch (start us, length us, event | category | flops | bytes accessed | tf_op | source)
XLA Modules:
  0.0 429.7 jit_solution(2133320632982006050)
XLA Ops:
  9.4 3.0 collective-permute-start.1
  14.7 3.6 collective-permute-start.4
  22.7 1.9 collective-permute-done.4
  24.6 10.0 %collective-permute-done.3 = bf16[128,768]{1,0:T(8,128)(2,1)S(1)} collective-permute-done((bf16[128,768]{1,0:T(8,128)(2,1)}, bf16[128,768]{1,0:T(8,128)(2,1)S(1)}, u32[]{:S(2)}, u32[]{:S(2)}) %collective-permute-start.3) | collective-permute-done | bytes 196640 | tf_op jit(solution)/shard_map/ppermute | solution.py:511
  34.6 1.9 pad_maximum_fusion.1.refs_10_.tok_ref
  36.6 2.5 collective-permute-start.12
  39.2 1.9 collective-permute-start.10
  42.3 4.7 %collective-permute-done.12 = bf16[144,768]{1,0:T(8,128)(2,1)S(1)} collective-permute-done((bf16[144,768]{1,0:T(8,128)(2,1)S(1)}, bf16[144,768]{1,0:T(8,128)(2,1)S(1)}, u32[]{:S(2)}, u32[]{:S(2)}) %collective-permute-start.12) | collective-permute-done | bytes 221216 | tf_op jit(solution)/shard_map/ppermute | solution.py:511
  47.0 9.1 %collective-permute-done.11 = bf16[144,768]{1,0:T(8,128)(2,1)S(1)} collective-permute-done((bf16[144,768]{1,0:T(8,128)(2,1)S(1)}, bf16[144,768]{1,0:T(8,128)(2,1)S(1)}, u32[]{:S(2)}, u32[]{:S(2)}) %collective-permute-start.11) | collective-permute-done | bytes 221216 | tf_op jit(solution)/shard_map/ppermute | solution.py:511
  57.3 2.1 collective-permute-done.13.refs_8_
  61.6 14.7 %front.1 = (f32[4,2,64,768]{3,2,1,0:T(8,128)}, bf16[4,2,64,768]{3,2,1,0:T(8,128)(2,1)}, bf16[2,256,2304]{2,1,0:T(8,128)(2,1)}, bf16[2,256,768]{2,1,0:T(8,128)(2,...) custom-call(bf16[96,3200]{1,0:T(8,128)(2,1)} %copy-done.6, ...), custom_call_target="tpu_custom_call" | custom-call | flops 1000 | bytes 1000 | tf_op jit(solution)/shard_map/front/pallas_call | solution.py:124
  76.4 2.5 collective-permute-start.19
  78.9 3.4 collective-permute-done.21.refs_4_
  86.4 1.5 collective-permute-start.23
  87.9 1.6 collective-permute-start.22
  89.4 27.9 %experts_own.1 = (bf16[4,2,768,768]{3,2,1,0:T(8,128)(2,1)}, f32[8,768]{1,0:T(8,128)}, bf16[4,128,768]{2,1,0:T(8,128)(2,1)}, bf16[4,128,768]{2,1,0:T(8,128)(2,1)}) custom-call(bf16[4,128,768]{2,1,0:T(8,128)(2,1)} %bitcast.101, bf16[4,144,768]{2,1,0:T(8,128)(2,1)} %copy-done, bf16[4,384,768]{2,1,0:T(8,128)(2,1)} %refs_7_, bf16[4,384,768]{2,1,0:T(8,128)(2,1)} %copy-done.7, ...), custom_call_target="tpu_custom_call" | custom-call | flops 1000 | bytes 1000 | tf_op jit(solution)/shard_map/experts_own/pallas_call | solution.py:380
  117.4 8.5 %collective-permute-done.23.refs_6_ = bf16[2,144,768]{2,1,0:T(8,128)(2,1)S(1)} collective-permute-done((bf16[2,144,768]{2,1,0:T(8,128)(2,1)S(1)}, bf16[2,144,768]{2,1,0:T(8,128)(2,1)S(1)}, u32[]{:S(2)}, u32[]{:S(2)}) %collective-permute-start.23) | collective-permute-done | bytes 442400 | tf_op jit(solution)/shard_map/ppermute | solution.py:501
  126.7 58.7 %experts_far.1 = (bf16[1536,2304]{1,0:T(8,128)(2,1)}, bf16[1536,2304]{1,0:T(8,128)(2,1)}, bf16[1,2,384,768]{3,2,1,0:T(8,128)(2,1)}, bf16[1,2,384,768]{3,2,1,0:T(...) custom-call(bf16[4,128,768]{2,1,0:T(8,128)(2,1)} %collective-permute, ...), custom_call_target="tpu_custom_call" | custom-call | flops 72477573120 | bytes 16777216 | tf_op jit(solution)/shard_map/experts_far/pallas_call | solution.py:380
  187.4 1.6 collective-permute-start.26
  189.1 1.6 add_convert_fusion.9
  192.0 19.9 %expert_grads.1 = (bf16[3,2,384,768]{3,2,1,0:T(8,128)(2,1)}, bf16[3,2,384,768]{3,2,1,0:T(8,128)(2,1)}) custom-call(bf16[4,128,768]{2,1,0:T(8,128)(2,1)} %collective-permute-done.17.refs_0_, bf16[4,128,768]{2,1,0:T(8,128)(2,1)} %collective-permute-done.18.refs_1_, bf16[4,128,768]{2,1,0:T(8,128)(2,1)} %collective-permute-done.19.refs_2_, ...), custom_call_target="tpu_custom_call" | custom-call | flops 43486543872 | bytes 16777216 | tf_op jit(solution)/shard_map/expert_grads/pallas_call | solution.py:481
  212.0 11.4 %collective-permute-done.26 = bf16[4,128,768]{2,1,0:T(8,128)(2,1)} collective-permute-done((bf16[4,128,768]{2,1,0:T(8,128)(2,1)}, bf16[4,128,768]{2,1,0:T(8,128)(2,1)}, u32[]{:S(2)}, u32[]{:S(2)}) %collective-permute-start.26) | collective-permute-done | bytes 786464 | tf_op jit(solution)/shard_map/ppermute | solution.py:501
  224.7 1.8 collective-permute-start.27
  231.1 1.6 fusion.26
  232.8 3.0 collective-permute-start.34
  235.7 21.2 %back.1 = (bf16[2,64,768]{2,1,0:T(8,128)(2,1)}, bf16[2,64,768]{2,1,0:T(8,128)(2,1)}, bf16[2,64,768]{2,1,0:T(8,128)(2,1)}, bf16[2,64,768]{2,1,0:T(8,128)(2,1)}, bf16[768,3200]{1,0:T(8,128)(2,1)}) custom-call(bf16[4,2,64,768]{3,2,1,0:T(8,128)(2,1)} %bitcast.128, bf16[4,2,64,768]{3,2,1,0:T(8,128)(2,1)} %bitcast.129, bf16[4,2,64,768]{3,2,1,0:T(8,128)(2,1)} %bitcast.130, ...), custom_call_target="tpu_custom_call" | custom-call | flops 30198988800 | bytes 16777216 | tf_op jit(solution)/shard_map/back/pallas_call | solution.py:649
  256.9 6.4 %collective-permute-done.28 = bf16[4,128,768]{2,1,0:T(8,128)(2,1)} collective-permute-done((bf16[4,128,768]{2,1,0:T(8,128)(2,1)}, bf16[4,128,768]{2,1,0:T(8,128)(2,1)}, u32[]{:S(2)}, u32[]{:S(2)}) %collective-permute-start.28) | collective-permute-done | bytes 786464 | tf_op jit(solution)/shard_map/ppermute | solution.py:501
  263.4 2.3 collective-permute-start.35
  265.7 3.0 add_convert_fusion.7
  268.7 1.8 collective-permute-start.38
  271.0 20.4 %collective-permute-done.35 = bf16[1,2,384,768]{3,2,1,0:T(8,128)(2,1)} collective-permute-done((bf16[1,2,384,768]{3,2,1,0:T(8,128)(2,1)}, bf16[1,2,384,768]{3,2,1,0:T(8,128)(2,1)}, u32[]{:S(2)}, u32[]{:S(2)}) %collective-permute-start.35) | collective-permute-done | bytes 1179680 | tf_op jit(solution)/shard_map/ppermute | solution.py:536
  291.4 1.6 add_convert_fusion.5
  293.8 2.0 add_convert_fusion.4
  297.0 18.0 %collective-permute-done.37 = bf16[1,2,384,768]{3,2,1,0:T(8,128)(2,1)S(1)} collective-permute-done((bf16[1,2,384,768]{3,2,1,0:T(8,128)(2,1)S(1)}, bf16[1,2,384,768]{3,2,1,0:T(8,128)(2,1)S(1)}, u32[]{:S(2)}, u32[]{:S(2)}) %collective-permute-start.37) | collective-permute-done | bytes 1179680 | tf_op jit(solution)/shard_map/ppermute | solution.py:545
  316.4 8.1 %collective-permute-done.39 = bf16[1,2,384,768]{3,2,1,0:T(8,128)(2,1)S(1)} collective-permute-done((bf16[1,2,384,768]{3,2,1,0:T(8,128)(2,1)S(1)}, bf16[1,2,384,768]{3,2,1,0:T(8,128)(2,1)S(1)}, u32[]{:S(2)}, u32[]{:S(2)}) %collective-permute-start.39) | collective-permute-done | bytes 1179680 | tf_op jit(solution)/shard_map/ppermute | solution.py:563
  326.8 1.7 collective-permute-start.41
  329.1 6.9 %collective-permute-start.40 = (bf16[96,3200]{1,0:T(8,128)(2,1)}, bf16[96,3200]{1,0:T(8,128)(2,1)S(1)}, u32[]{:S(2)}, u32[]{:S(2)}) collective-permute-start(bf16[96,3200]{1,0:T(8,128)(2,1)} %reduce-scatter.2.cloned.1.call-done), channel_id=1, source_target_pairs={{0,1},{3,2},{4,5},{7,6},{8,9},{11,10},{12,13},{15,14},{16,17},{19,... | collective-permute-start | bytes 1843208 | tf_op jit(solution)/shard_map/ppermute | solution.py:536
  336.1 15.6 %collective-permute-done.45 = bf16[1,2,384,768]{3,2,1,0:T(8,128)(2,1)} collective-permute-done((bf16[1,2,384,768]{3,2,1,0:T(8,128)(2,1)S(1)}, bf16[1,2,384,768]{3,2,1,0:T(8,128)(2,1)}, u32[]{:S(2)}, u32[]{:S(2)}) %collective-permute-start.45) | collective-permute-done | bytes 1179680 | tf_op jit(solution)/shard_map/ppermute | solution.py:563
  353.1 2.0 add_convert_fusion.1
  355.1 1.6 collective-permute-start.46
  357.6 2.2 convert_add_fusion
  360.8 5.7 %collective-permute-start.42 = (bf16[2,2,64,768]{3,2,1,0:T(8,128)(2,1)S(1)}, bf16[2,2,64,768]{3,2,1,0:T(8,128)(2,1)S(1)}, u32[]{:S(2)}, u32[]{:S(2)}) collective-permute-start(bf16[2,2,64,768]{3,2,1,0:T(8,128)(2,1)S(1)} %pad_maximum_fusion.5), channel_id=1, source_target_pairs={{0,1},{1,0},{2,3},{3,2},{4,5},{5,4},{6,7},{7,6},{8,9},{9,8},{10,11... | collective-permute-start | bytes 1179656 | tf_op jit(solution)/shard_map/ppermute | solution.py:511
  367.2 1.9 collective-permute-start.44
  370.8 32.8 %collective-permute-done.46 = bf16[1,2,384,768]{3,2,1,0:T(8,128)(2,1)S(1)} collective-permute-done((bf16[1,2,384,768]{3,2,1,0:T(8,128)(2,1)S(1)}, bf16[1,2,384,768]{3,2,1,0:T(8,128)(2,1)S(1)}, u32[]{:S(2)}, u32[]{:S(2)}) %collective-permute-start.46) | collective-permute-done | bytes 1179680 | tf_op jit(solution)/shard_map/ppermute | solution.py:563
  404.1 2.6 maximum_convert_fusion.1
  406.7 2.6 maximum_convert_fusion
  409.3 2.8 collective-permute-done.42
  414.3 5.2 %collective-permute-done.48 = bf16[96,3200]{1,0:T(8,128)(2,1)S(1)} collective-permute-done((bf16[96,3200]{1,0:T(8,128)(2,1)S(1)}, bf16[96,3200]{1,0:T(8,128)(2,1)S(1)}, u32[]{:S(2)}, u32[]{:S(2)}) %collective-permute-start.48) | collective-permute-done | bytes 614432 | tf_op jit(solution)/shard_map/ppermute | solution.py:563
  (204 shorter events, 46.0 us)
Async XLA Ops:
  7.2 321.9 %reduce-scatter.2.cloned.1.call-start = ((), (), s32[]{:S(2)}) async-start(), calls=%async_computation.1 | async-start | bytes 5529600 | tf_op jit(solution)/shard_map/reduce_scatter | solution.py:826
  9.4 27.2 %collective-permute-start.1 = (bf16[96,3200]{1,0:T(8,128)(2,1)S(1)}, bf16[96,3200]{1,0:T(8,128)(2,1)S(1)}, u32[]{:S(2)}, u32[]{:S(2)}) collective-permute-start(bf16[96,3200]{1,0:T(8,128)(2,1)S(1)} %fusion.5.refs_0_), channel_id=1, source_target_pairs={{0,16},{4,20},{8,24},{12,28},{16,0},{20,4},{24,8},{28,12},{1,17},{... | collective-permute-start | bytes 1843208 | tf_op jit(solution)/shard_map/ppermute | solution.py:501
  12.4 24.1 %collective-permute-start = (bf16[96,3200]{1,0:T(8,128)(2,1)S(1)}, bf16[96,3200]{1,0:T(8,128)(2,1)S(1)}, u32[]{:S(2)}, u32[]{:S(2)}) collective-permute-start(bf16[96,3200]{1,0:T(8,128)(2,1)S(1)} %fusion.5.refs_0_), channel_id=1, source_target_pairs={{0,8},{4,12},{8,0},{12,4},{16,24},{20,28},{24,16},{28,20},{1,9},{5... | collective-permute-start | bytes 1843208 | tf_op jit(solution)/shard_map/ppermute | solution.py:501
  14.7 9.9 %collective-permute-start.4 = (bf16[128,768]{1,0:T(8,128)(2,1)}, bf16[128,768]{1,0:T(8,128)(2,1)S(1)}, u32[]{:S(2)}, u32[]{:S(2)}) collective-permute-start(bf16[128,768]{1,0:T(8,128)(2,1)} %get-tuple-element.240), channel_id=1, source_target_pairs={{0,3},{1,2},{2,1},{3,0},{4,7},{5,6},{6,5},{7,4},{8,11},{9,10},{10,... | collective-permute-start | bytes 589832 | tf_op jit(solution)/shard_map/ppermute | solution.py:511
  18.3 16.3 %collective-permute-start.3 = (bf16[128,768]{1,0:T(8,128)(2,1)}, bf16[128,768]{1,0:T(8,128)(2,1)S(1)}, u32[]{:S(2)}, u32[]{:S(2)}) collective-permute-start(bf16[128,768]{1,0:T(8,128)(2,1)} %get-tuple-element.241), channel_id=1, source_target_pairs={{0,2},{1,3},{2,0},{3,1},{4,6},{5,7},{6,4},{7,5},{8,10},{9,11},{10,... | collective-permute-start | bytes 589832 | tf_op jit(solution)/shard_map/ppermute | solution.py:511
  18.3 16.3 %collective-permute-start.2 = (bf16[128,768]{1,0:T(8,128)(2,1)S(1)}, bf16[128,768]{1,0:T(8,128)(2,1)}, u32[]{:S(2)}, u32[]{:S(2)}) collective-permute-start(bf16[128,768]{1,0:T(8,128)(2,1)S(1)} %get-tuple-element.242), channel_id=1, source_target_pairs={{0,1},{1,0},{2,3},{3,2},{4,5},{5,4},{6,7},{7,6},{8,9},{9,8},{10,11... | collective-permute-start | bytes 589832 | tf_op jit(solution)/shard_map/ppermute | solution.py:511
  36.6 10.3 %collective-permute-start.12 = (bf16[144,768]{1,0:T(8,128)(2,1)S(1)}, bf16[144,768]{1,0:T(8,128)(2,1)S(1)}, u32[]{:S(2)}, u32[]{:S(2)}) collective-permute-start(bf16[144,768]{1,0:T(8,128)(2,1)S(1)} %get-tuple-element.236), channel_id=1, source_target_pairs={{0,3},{1,2},{2,1},{3,0},{4,7},{5,6},{6,5},{7,4},{8,11},{9,10},{10,... | collective-permute-start | bytes 663560 | tf_op jit(solution)/shard_map/ppermute | solution.py:511
  39.2 16.9 %collective-permute-start.11 = (bf16[144,768]{1,0:T(8,128)(2,1)S(1)}, bf16[144,768]{1,0:T(8,128)(2,1)S(1)}, u32[]{:S(2)}, u32[]{:S(2)}) collective-permute-start(bf16[144,768]{1,0:T(8,128)(2,1)S(1)} %get-tuple-element.237), channel_id=1, source_target_pairs={{0,2},{1,3},{2,0},{3,1},{4,6},{5,7},{6,4},{7,5},{8,10},{9,11},{10,... | collective-permute-start | bytes 663560 | tf_op jit(solution)/shard_map/ppermute | solution.py:511
  39.2 16.9 %collective-permute-start.10 = (bf16[144,768]{1,0:T(8,128)(2,1)S(1)}, bf16[144,768]{1,0:T(8,128)(2,1)S(1)}, u32[]{:S(2)}, u32[]{:S(2)}) collective-permute-start(bf16[144,768]{1,0:T(8,128)(2,1)S(1)} %get-tuple-element.238), channel_id=1, source_target_pairs={{0,1},{1,0},{2,3},{3,2},{4,5},{5,4},{6,7},{7,6},{8,9},{9,8},{10,11... | collective-permute-start | bytes 663560 | tf_op jit(solution)/shard_map/ppermute | solution.py:511
  41.1 15.6 %collective-permute-start.9 = (bf16[48,3200]{1,0:T(8,128)(2,1)S(1)}, bf16[48,3200]{1,0:T(8,128)(2,1)S(1)}, u32[]{:S(2)}, u32[]{:S(2)}) collective-permute-start(bf16[48,3200]{1,0:T(8,128)(2,1)S(1)} %slice.204), channel_id=1, source_target_pairs={{0,8},{4,12},{8,0},{12,4},{16,24},{20,28},{24,16},{28,20},{1,9},{5... | collective-permute-start | bytes 921608 | tf_op jit(solution)/shard_map/ppermute | solution.py:501
  41.7 15.0 %collective-permute-start.8 = (bf16[48,3200]{1,0:T(8,128)(2,1)S(1)}, bf16[48,3200]{1,0:T(8,128)(2,1)S(1)}, u32[]{:S(2)}, u32[]{:S(2)}) collective-permute-start(bf16[48,3200]{1,0:T(8,128)(2,1)S(1)} %slice.203), channel_id=1, source_target_pairs={{0,16},{4,20},{8,24},{12,28},{16,0},{20,4},{24,8},{28,12},{1,17},{... | collective-permute-start | bytes 921608 | tf_op jit(solution)/shard_map/ppermute | solution.py:501
  47.0 10.4 %collective-permute-start.5 = (bf16[96,3200]{1,0:T(8,128)(2,1)S(1)}, bf16[96,3200]{1,0:T(8,128)(2,1)S(1)}, u32[]{:S(2)}, u32[]{:S(2)}) collective-permute-start(bf16[96,3200]{1,0:T(8,128)(2,1)S(1)} %fusion.5.refs_0_), channel_id=1, source_target_pairs={{0,4},{4,0},{8,12},{12,8},{16,20},{20,16},{24,28},{28,24},{1,5},{5... | collective-permute-start | bytes 1843208 | tf_op jit(solution)/shard_map/ppermute | solution.py:501
  56.1 3.8 collective-permute-start.6
  56.1 3.8 collective-permute-start.7
  59.9 26.4 %collective-permute-start.15 = (bf16[4,384,768]{2,1,0:T(8,128)(2,1)}, bf16[4,384,768]{2,1,0:T(8,128)(2,1)S(1)}, u32[]{:S(2)}, u32[]{:S(2)}) collective-permute-start(bf16[4,384,768]{2,1,0:T(8,128)(2,1)} %refs_7_), channel_id=1, source_target_pairs={{0,4},{4,0},{8,12},{12,8},{16,20},{20,16},{24,28},{28,24},{1,5},{5... | collective-permute-start | bytes 7077896 | tf_op jit(solution)/shard_map/ppermute | solution.py:501
  60.1 27.8 %collective-permute-start.16 = (bf16[4,384,768]{2,1,0:T(8,128)(2,1)}, bf16[4,384,768]{2,1,0:T(8,128)(2,1)}, u32[]{:S(2)}, u32[]{:S(2)}) collective-permute-start(bf16[4,384,768]{2,1,0:T(8,128)(2,1)} %refs_9_), channel_id=1, source_target_pairs={{0,4},{4,0},{8,12},{12,8},{16,20},{20,16},{24,28},{28,24},{1,5},{5... | collective-permute-start | bytes 7077896 | tf_op jit(solution)/shard_map/ppermute | solution.py:501
  60.5 21.8 %collective-permute-start.21 = (bf16[4,144,768]{2,1,0:T(8,128)(2,1)S(1)}, bf16[4,144,768]{2,1,0:T(8,128)(2,1)}, u32[]{:S(2)}, u32[]{:S(2)}) collective-permute-start(bf16[4,144,768]{2,1,0:T(8,128)(2,1)S(1)} %pad_maximum_fusion.refs_1_), channel_id=1, source_target_pairs={{0,16},{4,20},{8,24},{12,28},{16,0},{20,4},{24,8},{28,12},{1,17},{... | collective-permute-start | bytes 2654216 | tf_op jit(solution)/shard_map/ppermute | solution.py:501
  61.0 22.7 %collective-permute-start.20 = (bf16[4,144,768]{2,1,0:T(8,128)(2,1)S(1)}, bf16[4,144,768]{2,1,0:T(8,128)(2,1)}, u32[]{:S(2)}, u32[]{:S(2)}) collective-permute-start(bf16[4,144,768]{2,1,0:T(8,128)(2,1)S(1)} %pad_maximum_fusion.refs_1_), channel_id=1, source_target_pairs={{0,8},{4,12},{8,0},{12,4},{16,24},{20,28},{24,16},{28,20},{1,9},{5... | collective-permute-start | bytes 2654216 | tf_op jit(solution)/shard_map/ppermute | solution.py:501
  76.4 40.9 %collective-permute-start.19 = (bf16[4,128,768]{2,1,0:T(8,128)(2,1)}, bf16[4,128,768]{2,1,0:T(8,128)(2,1)}, u32[]{:S(2)}, u32[]{:S(2)}) collective-permute-start(bf16[4,128,768]{2,1,0:T(8,128)(2,1)} %bitcast.98), channel_id=1, source_target_pairs={{0,24},{4,28},{8,16},{12,20},{16,8},{20,12},{24,0},{28,4},{1,25},{... | collective-permute-start | bytes 2359304 | tf_op jit(solution)/shard_map/ppermute | solution.py:501
  82.3 35.1 %collective-permute-start.18 = (bf16[4,128,768]{2,1,0:T(8,128)(2,1)}, bf16[4,128,768]{2,1,0:T(8,128)(2,1)}, u32[]{:S(2)}, u32[]{:S(2)}) collective-permute-start(bf16[4,128,768]{2,1,0:T(8,128)(2,1)} %bitcast.99), channel_id=1, source_target_pairs={{0,16},{4,20},{8,24},{12,28},{16,0},{20,4},{24,8},{28,12},{1,17},{... | collective-permute-start | bytes 2359304 | tf_op jit(solution)/shard_map/ppermute | solution.py:501
  83.7 33.7 %collective-permute-start.17 = (bf16[4,128,768]{2,1,0:T(8,128)(2,1)}, bf16[4,128,768]{2,1,0:T(8,128)(2,1)}, u32[]{:S(2)}, u32[]{:S(2)}) collective-permute-start(bf16[4,128,768]{2,1,0:T(8,128)(2,1)} %bitcast.100), channel_id=1, source_target_pairs={{0,8},{4,12},{8,0},{12,4},{16,24},{20,28},{24,16},{28,20},{1,9},{5... | collective-permute-start | bytes 2359304 | tf_op jit(solution)/shard_map/ppermute | solution.py:501
  86.4 39.5 %collective-permute-start.23 = (bf16[2,144,768]{2,1,0:T(8,128)(2,1)S(1)}, bf16[2,144,768]{2,1,0:T(8,128)(2,1)S(1)}, u32[]{:S(2)}, u32[]{:S(2)}) collective-permute-start(bf16[2,144,768]{2,1,0:T(8,128)(2,1)S(1)} %slice.267), channel_id=1, source_target_pairs={{0,8},{4,12},{8,0},{12,4},{16,24},{20,28},{24,16},{28,20},{1,9},{5... | collective-permute-start | bytes 1327112 | tf_op jit(solution)/shard_map/ppermute | solution.py:501
  87.9 38.7 %collective-permute-start.22 = (bf16[2,144,768]{2,1,0:T(8,128)(2,1)S(1)}, bf16[2,144,768]{2,1,0:T(8,128)(2,1)}, u32[]{:S(2)}, u32[]{:S(2)}) collective-permute-start(bf16[2,144,768]{2,1,0:T(8,128)(2,1)S(1)} %slice.266), channel_id=1, source_target_pairs={{0,16},{4,20},{8,24},{12,28},{16,0},{20,4},{24,8},{28,12},{1,17},{... | collective-permute-start | bytes 1327112 | tf_op jit(solution)/shard_map/ppermute | solution.py:501
  185.4 3.6 collective-permute-start.30
  185.5 26.4 %collective-permute-start.24 = (bf16[4,128,768]{2,1,0:T(8,128)(2,1)}, bf16[4,128,768]{2,1,0:T(8,128)(2,1)S(1)}, u32[]{:S(2)}, u32[]{:S(2)}) collective-permute-start(bf16[4,128,768]{2,1,0:T(8,128)(2,1)} %get-tuple-element.104), channel_id=1, source_target_pairs={{0,8},{4,12},{8,0},{12,4},{16,24},{20,28},{24,16},{28,20},{1,9},{5... | collective-permute-start | bytes 2359304 | tf_op jit(solution)/shard_map/ppermute | solution.py:501
  186.1 25.8 %collective-permute-start.25 = (bf16[4,128,768]{2,1,0:T(8,128)(2,1)}, bf16[4,128,768]{2,1,0:T(8,128)(2,1)S(1)}, u32[]{:S(2)}, u32[]{:S(2)}) collective-permute-start(bf16[4,128,768]{2,1,0:T(8,128)(2,1)} %get-tuple-element.105), channel_id=1, source_target_pairs={{0,16},{4,20},{8,24},{12,28},{16,0},{20,4},{24,8},{28,12},{1,17},{... | collective-permute-start | bytes 2359304 | tf_op jit(solution)/shard_map/ppermute | solution.py:501
  187.4 36.0 %collective-permute-start.26 = (bf16[4,128,768]{2,1,0:T(8,128)(2,1)}, bf16[4,128,768]{2,1,0:T(8,128)(2,1)}, u32[]{:S(2)}, u32[]{:S(2)}) collective-permute-start(bf16[4,128,768]{2,1,0:T(8,128)(2,1)} %get-tuple-element.106), channel_id=1, source_target_pairs={{0,24},{4,28},{8,16},{12,20},{16,8},{20,12},{24,0},{28,4},{1,25},{... | collective-permute-start | bytes 2359304 | tf_op jit(solution)/shard_map/ppermute | solution.py:501
  190.7 32.7 %collective-permute-start.31 = (bf16[1,2,384,768]{3,2,1,0:T(8,128)(2,1)S(1)}, bf16[1,2,384,768]{3,2,1,0:T(8,128)(2,1)S(1)}, u32[]{:S(2)}, u32[]{:S(2)}) collective-permute-start(bf16[1,2,384,768]{3,2,1,0:T(8,128)(2,1)S(1)} %add_convert_fusion.9), channel_id=1, source_target_pairs={{0,1},{3,2},{4,5},{7,6},{8,9},{11,10},{12,13},{15,14},{16,17},{19,... | collective-permute-start | bytes 3538952 | tf_op jit(solution)/shard_map/ppermute | solution.py:536
  223.7 6.5 %collective-permute-start.32 = (bf16[3,2,384,768]{3,2,1,0:T(8,128)(2,1)}, bf16[3,2,384,768]{3,2,1,0:T(8,128)(2,1)S(1)}, u32[]{:S(2)}, u32[]{:S(2)}) collective-permute-start(bf16[3,2,384,768]{3,2,1,0:T(8,128)(2,1)} %get-tuple-element.122), channel_id=1, source_target_pairs={{0,4},{4,0},{8,12},{12,8},{16,20},{20,16},{24,28},{28,24},{1,5},{5... | collective-permute-start | bytes 10616840 | tf_op jit(solution)/shard_map/ppermute | solution.py:501
  224.7 32.2 %collective-permute-start.27 = (bf16[4,128,768]{2,1,0:T(8,128)(2,1)}, bf16[4,128,768]{2,1,0:T(8,128)(2,1)}, u32[]{:S(2)}, u32[]{:S(2)}) collective-permute-start(bf16[4,128,768]{2,1,0:T(8,128)(2,1)} %get-tuple-element.107), channel_id=1, source_target_pairs={{0,8},{4,12},{8,0},{12,4},{16,24},{20,28},{24,16},{28,20},{1,9},{5... | collective-permute-start | bytes 2359304 | tf_op jit(solution)/shard_map/ppermute | solution.py:501
  226.5 36.8 %collective-permute-start.28 = (bf16[4,128,768]{2,1,0:T(8,128)(2,1)}, bf16[4,128,768]{2,1,0:T(8,128)(2,1)}, u32[]{:S(2)}, u32[]{:S(2)}) collective-permute-start(bf16[4,128,768]{2,1,0:T(8,128)(2,1)} %get-tuple-element.108), channel_id=1, source_target_pairs={{0,16},{4,20},{8,24},{12,28},{16,0},{20,4},{24,8},{28,12},{1,17},{... | collective-permute-start | bytes 2359304 | tf_op jit(solution)/shard_map/ppermute | solution.py:501
  227.8 35.5 %collective-permute-start.29 = (bf16[4,128,768]{2,1,0:T(8,128)(2,1)}, bf16[4,128,768]{2,1,0:T(8,128)(2,1)}, u32[]{:S(2)}, u32[]{:S(2)}) collective-permute-start(bf16[4,128,768]{2,1,0:T(8,128)(2,1)} %get-tuple-element.109), channel_id=1, source_target_pairs={{0,24},{4,28},{8,16},{12,20},{16,8},{20,12},{24,0},{28,4},{1,25},{... | collective-permute-start | bytes 2359304 | tf_op jit(solution)/shard_map/ppermute | solution.py:501
  228.2 35.1 %collective-permute-start.33 = (bf16[1,2,384,768]{3,2,1,0:T(8,128)(2,1)S(1)}, bf16[1,2,384,768]{3,2,1,0:T(8,128)(2,1)S(1)}, u32[]{:S(2)}, u32[]{:S(2)}) collective-permute-start(bf16[1,2,384,768]{3,2,1,0:T(8,128)(2,1)S(1)} %add_convert_fusion.8), channel_id=1, source_target_pairs={{1,2},{2,1},{5,6},{6,5},{9,10},{10,9},{13,14},{14,13},{17,18},{18,... | collective-permute-start | bytes 3538952 | tf_op jit(solution)/shard_map/ppermute | solution.py:556
  232.8 30.6 %collective-permute-start.34 = (bf16[1,2,384,768]{3,2,1,0:T(8,128)(2,1)}, bf16[1,2,384,768]{3,2,1,0:T(8,128)(2,1)}, u32[]{:S(2)}, u32[]{:S(2)}) collective-permute-start(bf16[1,2,384,768]{3,2,1,0:T(8,128)(2,1)} %get-tuple-element.123), channel_id=1, source_target_pairs={{0,1},{3,2},{4,5},{7,6},{8,9},{11,10},{12,13},{15,14},{16,17},{19,... | collective-permute-start | bytes 3538952 | tf_op jit(solution)/shard_map/ppermute | solution.py:536
  263.4 28.0 %collective-permute-start.35 = (bf16[1,2,384,768]{3,2,1,0:T(8,128)(2,1)}, bf16[1,2,384,768]{3,2,1,0:T(8,128)(2,1)}, u32[]{:S(2)}, u32[]{:S(2)}) collective-permute-start(bf16[1,2,384,768]{3,2,1,0:T(8,128)(2,1)} %get-tuple-element.141), channel_id=1, source_target_pairs={{0,1},{3,2},{4,5},{7,6},{8,9},{11,10},{12,13},{15,14},{16,17},{19,... | collective-permute-start | bytes 3538952 | tf_op jit(solution)/shard_map/ppermute | solution.py:536
  268.7 25.0 %collective-permute-start.38 = (bf16[1,2,384,768]{3,2,1,0:T(8,128)(2,1)}, bf16[1,2,384,768]{3,2,1,0:T(8,128)(2,1)}, u32[]{:S(2)}, u32[]{:S(2)}) collective-permute-start(bf16[1,2,384,768]{3,2,1,0:T(8,128)(2,1)} %add_convert_fusion.7), channel_id=1, source_target_pairs={{1,2},{2,1},{5,6},{6,5},{9,10},{10,9},{13,14},{14,13},{17,18},{18,... | collective-permute-start | bytes 3538952 | tf_op jit(solution)/shard_map/ppermute | solution.py:556
  270.9 44.1 %collective-permute-start.37 = (bf16[1,2,384,768]{3,2,1,0:T(8,128)(2,1)S(1)}, bf16[1,2,384,768]{3,2,1,0:T(8,128)(2,1)S(1)}, u32[]{:S(2)}, u32[]{:S(2)}) collective-permute-start(bf16[1,2,384,768]{3,2,1,0:T(8,128)(2,1)S(1)} %broadcast_select_fusion.4), channel_id=1, source_target_pairs={{0,1},{1,0},{2,3},{3,2},{4,5},{5,4},{6,7},{7,6},{8,9},{9,8},{10,11... | collective-permute-start | bytes 3538952 | tf_op jit(solution)/shard_map/ppermute | solution.py:545
  293.0 23.4 %collective-permute-start.36 = (bf16[1,2,384,768]{3,2,1,0:T(8,128)(2,1)S(1)}, bf16[1,2,384,768]{3,2,1,0:T(8,128)(2,1)S(1)}, u32[]{:S(2)}, u32[]{:S(2)}) collective-permute-start(bf16[1,2,384,768]{3,2,1,0:T(8,128)(2,1)S(1)} %add_convert_fusion.5), channel_id=1, source_target_pairs={{1,2},{2,1},{5,6},{6,5},{9,10},{10,9},{13,14},{14,13},{17,18},{18,... | collective-permute-start | bytes 3538952 | tf_op jit(solution)/shard_map/ppermute | solution.py:556
  295.7 28.8 %collective-permute-start.39 = (bf16[1,2,384,768]{3,2,1,0:T(8,128)(2,1)S(1)}, bf16[1,2,384,768]{3,2,1,0:T(8,128)(2,1)S(1)}, u32[]{:S(2)}, u32[]{:S(2)}) collective-permute-start(bf16[1,2,384,768]{3,2,1,0:T(8,128)(2,1)S(1)} %add_convert_fusion.4), channel_id=1, source_target_pairs={{1,0},{2,3},{5,4},{6,7},{9,8},{10,11},{13,12},{14,15},{17,16},{18,... | collective-permute-start | bytes 3538952 | tf_op jit(solution)/shard_map/ppermute | solution.py:563
  325.5 26.1 %collective-permute-start.45 = (bf16[1,2,384,768]{3,2,1,0:T(8,128)(2,1)S(1)}, bf16[1,2,384,768]{3,2,1,0:T(8,128)(2,1)}, u32[]{:S(2)}, u32[]{:S(2)}) collective-permute-start(bf16[1,2,384,768]{3,2,1,0:T(8,128)(2,1)S(1)} %add_convert_fusion.2), channel_id=1, source_target_pairs={{1,0},{2,3},{5,4},{6,7},{9,8},{10,11},{13,12},{14,15},{17,16},{18,... | collective-permute-start | bytes 3538952 | tf_op jit(solution)/shard_map/ppermute | solution.py:563
  326.8 26.3 %collective-permute-start.41 = (bf16[1,2,384,768]{3,2,1,0:T(8,128)(2,1)}, bf16[1,2,384,768]{3,2,1,0:T(8,128)(2,1)}, u32[]{:S(2)}, u32[]{:S(2)}) collective-permute-start(bf16[1,2,384,768]{3,2,1,0:T(8,128)(2,1)} %add_convert_fusion.3), channel_id=1, source_target_pairs={{1,2},{2,1},{5,6},{6,5},{9,10},{10,9},{13,14},{14,13},{17,18},{18,... | collective-permute-start | bytes 3538952 | tf_op jit(solution)/shard_map/ppermute | solution.py:556
  329.1 27.6 %collective-permute-start.40 = (bf16[96,3200]{1,0:T(8,128)(2,1)}, bf16[96,3200]{1,0:T(8,128)(2,1)S(1)}, u32[]{:S(2)}, u32[]{:S(2)}) collective-permute-start(bf16[96,3200]{1,0:T(8,128)(2,1)} %reduce-scatter.2.cloned.1.call-done), channel_id=1, source_target_pairs={{0,1},{3,2},{4,5},{7,6},{8,9},{11,10},{12,13},{15,14},{16,17},{19,... | collective-permute-start | bytes 1843208 | tf_op jit(solution)/shard_map/ppermute | solution.py:536
  355.1 48.6 %collective-permute-start.46 = (bf16[1,2,384,768]{3,2,1,0:T(8,128)(2,1)S(1)}, bf16[1,2,384,768]{3,2,1,0:T(8,128)(2,1)S(1)}, u32[]{:S(2)}, u32[]{:S(2)}) collective-permute-start(bf16[1,2,384,768]{3,2,1,0:T(8,128)(2,1)S(1)} %add_convert_fusion.1), channel_id=1, source_target_pairs={{1,0},{2,3},{5,4},{6,7},{9,8},{10,11},{13,12},{14,15},{17,16},{18,... | collective-permute-start | bytes 3538952 | tf_op jit(solution)/shard_map/ppermute | solution.py:563
  356.9 12.3 %collective-permute-start.47 = (bf16[96,3200]{1,0:T(8,128)(2,1)S(1)}, bf16[96,3200]{1,0:T(8,128)(2,1)S(1)}, u32[]{:S(2)}, u32[]{:S(2)}) collective-permute-start(bf16[96,3200]{1,0:T(8,128)(2,1)S(1)} %add_convert_fusion.11), channel_id=1, source_target_pairs={{1,2},{2,1},{5,6},{6,5},{9,10},{10,9},{13,14},{14,13},{17,18},{18,... | collective-permute-start | bytes 1843208 | tf_op jit(solution)/shard_map/ppermute | solution.py:556
  360.8 51.3 %collective-permute-start.42 = (bf16[2,2,64,768]{3,2,1,0:T(8,128)(2,1)S(1)}, bf16[2,2,64,768]{3,2,1,0:T(8,128)(2,1)S(1)}, u32[]{:S(2)}, u32[]{:S(2)}) collective-permute-start(bf16[2,2,64,768]{3,2,1,0:T(8,128)(2,1)S(1)} %pad_maximum_fusion.5), channel_id=1, source_target_pairs={{0,1},{1,0},{2,3},{3,2},{4,5},{5,4},{6,7},{7,6},{8,9},{9,8},{10,11... | collective-permute-start | bytes 1179656 | tf_op jit(solution)/shard_map/ppermute | solution.py:511
  366.6 45.5 %collective-permute-start.43 = (bf16[2,2,64,768]{3,2,1,0:T(8,128)(2,1)S(1)}, bf16[2,2,64,768]{3,2,1,0:T(8,128)(2,1)S(1)}, u32[]{:S(2)}, u32[]{:S(2)}) collective-permute-start(bf16[2,2,64,768]{3,2,1,0:T(8,128)(2,1)S(1)} %pad_maximum_fusion.6), channel_id=1, source_target_pairs={{0,2},{1,3},{2,0},{3,1},{4,6},{5,7},{6,4},{7,5},{8,10},{9,11},{10,... | collective-permute-start | bytes 1179656 | tf_op jit(solution)/shard_map/ppermute | solution.py:511
  367.2 44.9 %collective-permute-start.44 = (bf16[2,2,64,768]{3,2,1,0:T(8,128)(2,1)S(1)}, bf16[2,2,64,768]{3,2,1,0:T(8,128)(2,1)S(1)}, u32[]{:S(2)}, u32[]{:S(2)}) collective-permute-start(bf16[2,2,64,768]{3,2,1,0:T(8,128)(2,1)S(1)} %pad_maximum_fusion.7), channel_id=1, source_target_pairs={{0,3},{1,2},{2,1},{3,0},{4,7},{5,6},{6,5},{7,4},{8,11},{9,10},{10,... | collective-permute-start | bytes 1179656 | tf_op jit(solution)/shard_map/ppermute | solution.py:511
  369.4 50.1 %collective-permute-start.48 = (bf16[96,3200]{1,0:T(8,128)(2,1)S(1)}, bf16[96,3200]{1,0:T(8,128)(2,1)S(1)}, u32[]{:S(2)}, u32[]{:S(2)}) collective-permute-start(bf16[96,3200]{1,0:T(8,128)(2,1)S(1)} %add_convert_fusion.10), channel_id=1, source_target_pairs={{1,0},{2,3},{5,4},{6,7},{9,8},{10,11},{13,12},{14,15},{17,16},{18,... | collective-permute-start | bytes 1843208 | tf_op jit(solution)/shard_map/ppermute | solution.py:563
  (39 other events, 320.3 us)
Sparse Core Ops, SparseCore 0:
  263.5 53.2 reduce-scatter.1

commit v5 on v4

--- a/solution.py
+++ b/solution.py
@@ -826,8 +826,8 @@
     dense = lax.psum_scatter(dense, "fsdp", scatter_dimension=0, tiled=True)
     lines[2].raw, lines[3].raw = tie((lines[2].raw, lines[3].raw), grad_tok)
     lines[2].inwards()
-    ready = lines[1].across(grad_tok, flying)
-    ready = lines[3].inwards_with(lines[0], ready)
+    ready = lines[1].across(grad_tok, flying[1:])
+    ready = lines[3].inwards_with(lines[0], ready, flying)
     ready = lines[2].across(ready)
     ready = lines[1].outwards(ready)
     ready = lines[3].across(ready)

time: 436 us -> 436 us (level)
  no operation moved by 1% of the time
where the time goes in v5:
time: 436 us; the launch traced here: 430 us
  waiting for transfers between devices  164 us (38%)
  Pallas kernels  142 us (33%)
  starting transfers between devices  64.3 us (15%)
  other arithmetic  31.3 us (7%)
  between operations  15 us (3%)
  local copies, waits for them, and re-layouts  12.5 us (3%)
    pallas_call x2, Pallas kernels, experts_call(): pl.pallas_call(functools.partial(expert_kernel, plan), grid=(groups,), in...  86.6 us
    ppermute x4, waiting for transfers between devices, outwards(): self.moving = lax.ppermute(self.total, 'seq', [(1, 0), (2, 3)])  61.7 us
    ppermute x26, waiting for transfers between devices, flip(): return lax.ppermute(array, 'fsdp', [(n, n ^ bits) for n in range(fsdp)])  35.2 us
    ppermute x9, waiting for transfers between devices, exchange(): lax.ppermute(pieces[k], 'seq', [(n, n ^ k) for n in range(count)])  28.4 us
    ppermute x26, starting transfers between devices, flip(): return lax.ppermute(array, 'fsdp', [(n, n ^ bits) for n in range(fsdp)])  22.3 us
    pallas_call x1, Pallas kernels, back(): pl.pallas_call(back_kernel, grid=(images,), in_specs=[split] * 7 + [pl.Bl...  21.2 us
    ppermute x4, waiting for transfers between devices, inwards(): self.moving = lax.ppermute(self.raw, 'seq', [(0, 1), (3, 2)])  20.4 us
    pallas_call x1, Pallas kernels, grads_call(): pl.pallas_call(functools.partial(grads_kernel, plan), grid=(many,), in_sp...  19.9 us
  transfers between devices with their start and end apart: 50, of which 21 were waited for; matrix products, arithmetic and copies ran while one was open for 9% of the time, Pallas kernels for 19%

profile of v5, /device:TPU:0, one launch (start us, length us, event | category | flops | bytes accessed | tf_op | source)
XLA Modules:
  0.0 429.7 jit_solution(2133320632982006050)
XLA Ops:
  9.4 3.0 collective-permute-start.1
  14.7 3.6 collective-permute-start.4
  22.7 1.9 collective-permute-done.4
  24.6 10.0 %collective-permute-done.3 = bf16[128,768]{1,0:T(8,128)(2,1)S(1)} collective-permute-done((bf16[128,768]{1,0:T(8,128)(2,1)}, bf16[128,768]{1,0:T(8,128)(2,1)S(1)}, u32[]{:S(2)}, u32[]{:S(2)}) %collective-permute-start.3) | collective-permute-done | bytes 196640 | tf_op jit(solution)/shard_map/ppermute | solution.py:511
  34.6 1.9 pad_maximum_fusion.1.refs_10_.tok_ref
  36.6 2.5 collective-permute-start.12
  39.2 1.9 collective-permute-start.10
  42.3 4.7 %collective-permute-done.12 = bf16[144,768]{1,0:T(8,128)(2,1)S(1)} collective-permute-done((bf16[144,768]{1,0:T(8,128)(2,1)S(1)}, bf16[144,768]{1,0:T(8,128)(2,1)S(1)}, u32[]{:S(2)}, u32[]{:S(2)}) %collective-permute-start.12) | collective-permute-done | bytes 221216 | tf_op jit(solution)/shard_map/ppermute | solution.py:511
  47.0 9.1 %collective-permute-done.11 = bf16[144,768]{1,0:T(8,128)(2,1)S(1)} collective-permute-done((bf16[144,768]{1,0:T(8,128)(2,1)S(1)}, bf16[144,768]{1,0:T(8,128)(2,1)S(1)}, u32[]{:S(2)}, u32[]{:S(2)}) %collective-permute-start.11) | collective-permute-done | bytes 221216 | tf_op jit(solution)/shard_map/ppermute | solution.py:511
  57.3 2.1 collective-permute-done.13.refs_8_
  61.6 14.7 %front.1 = (f32[4,2,64,768]{3,2,1,0:T(8,128)}, bf16[4,2,64,768]{3,2,1,0:T(8,128)(2,1)}, bf16[2,256,2304]{2,1,0:T(8,128)(2,1)}, bf16[2,256,768]{2,1,0:T(8,128)(2,...) custom-call(bf16[96,3200]{1,0:T(8,128)(2,1)} %copy-done.6, ...), custom_call_target="tpu_custom_call" | custom-call | flops 1000 | bytes 1000 | tf_op jit(solution)/shard_map/front/pallas_call | solution.py:124
  76.4 2.5 collective-permute-start.19
  78.9 3.4 collective-permute-done.21.refs_4_
  86.4 1.5 collective-permute-start.23
  87.9 1.6 collective-permute-start.22
  89.4 27.9 %experts_own.1 = (bf16[4,2,768,768]{3,2,1,0:T(8,128)(2,1)}, f32[8,768]{1,0:T(8,128)}, bf16[4,128,768]{2,1,0:T(8,128)(2,1)}, bf16[4,128,768]{2,1,0:T(8,128)(2,1)}) custom-call(bf16[4,128,768]{2,1,0:T(8,128)(2,1)} %bitcast.101, bf16[4,144,768]{2,1,0:T(8,128)(2,1)} %copy-done, bf16[4,384,768]{2,1,0:T(8,128)(2,1)} %refs_7_, bf16[4,384,768]{2,1,0:T(8,128)(2,1)} %copy-done.7, ...), custom_call_target="tpu_custom_call" | custom-call | flops 1000 | bytes 1000 | tf_op jit(solution)/shard_map/experts_own/pallas_call | solution.py:380
  117.4 8.5 %collective-permute-done.23.refs_6_ = bf16[2,144,768]{2,1,0:T(8,128)(2,1)S(1)} collective-permute-done((bf16[2,144,768]{2,1,0:T(8,128)(2,1)S(1)}, bf16[2,144,768]{2,1,0:T(8,128)(2,1)S(1)}, u32[]{:S(2)}, u32[]{:S(2)}) %collective-permute-start.23) | collective-permute-done | bytes 442400 | tf_op jit(solution)/shard_map/ppermute | solution.py:501
  126.7 58.7 %experts_far.1 = (bf16[1536,2304]{1,0:T(8,128)(2,1)}, bf16[1536,2304]{1,0:T(8,128)(2,1)}, bf16[1,2,384,768]{3,2,1,0:T(8,128)(2,1)}, bf16[1,2,384,768]{3,2,1,0:T(...) custom-call(bf16[4,128,768]{2,1,0:T(8,128)(2,1)} %collective-permute, ...), custom_call_target="tpu_custom_call" | custom-call | flops 72477573120 | bytes 16777216 | tf_op jit(solution)/shard_map/experts_far/pallas_call | solution.py:380
  187.4 1.6 collective-permute-start.26
  189.1 1.6 add_convert_fusion.9
  192.0 19.9 %expert_grads.1 = (bf16[3,2,384,768]{3,2,1,0:T(8,128)(2,1)}, bf16[3,2,384,768]{3,2,1,0:T(8,128)(2,1)}) custom-call(bf16[4,128,768]{2,1,0:T(8,128)(2,1)} %collective-permute-done.17.refs_0_, bf16[4,128,768]{2,1,0:T(8,128)(2,1)} %collective-permute-done.18.refs_1_, bf16[4,128,768]{2,1,0:T(8,128)(2,1)} %collective-permute-done.19.refs_2_, ...), custom_call_target="tpu_custom_call" | custom-call | flops 43486543872 | bytes 16777216 | tf_op jit(solution)/shard_map/expert_grads/pallas_call | solution.py:481
  212.0 11.4 %collective-permute-done.26 = bf16[4,128,768]{2,1,0:T(8,128)(2,1)} collective-permute-done((bf16[4,128,768]{2,1,0:T(8,128)(2,1)}, bf16[4,128,768]{2,1,0:T(8,128)(2,1)}, u32[]{:S(2)}, u32[]{:S(2)}) %collective-permute-start.26) | collective-permute-done | bytes 786464 | tf_op jit(solution)/shard_map/ppermute | solution.py:501
  224.7 1.8 collective-permute-start.27
  231.1 1.6 fusion.26
  232.8 3.0 collective-permute-start.34
  235.7 21.2 %back.1 = (bf16[2,64,768]{2,1,0:T(8,128)(2,1)}, bf16[2,64,768]{2,1,0:T(8,128)(2,1)}, bf16[2,64,768]{2,1,0:T(8,128)(2,1)}, bf16[2,64,768]{2,1,0:T(8,128)(2,1)}, bf16[768,3200]{1,0:T(8,128)(2,1)}) custom-call(bf16[4,2,64,768]{3,2,1,0:T(8,128)(2,1)} %bitcast.128, bf16[4,2,64,768]{3,2,1,0:T(8,128)(2,1)} %bitcast.129, bf16[4,2,64,768]{3,2,1,0:T(8,128)(2,1)} %bitcast.130, ...), custom_call_target="tpu_custom_call" | custom-call | flops 30198988800 | bytes 16777216 | tf_op jit(solution)/shard_map/back/pallas_call | solution.py:649
  256.9 6.4 %collective-permute-done.28 = bf16[4,128,768]{2,1,0:T(8,128)(2,1)} collective-permute-done((bf16[4,128,768]{2,1,0:T(8,128)(2,1)}, bf16[4,128,768]{2,1,0:T(8,128)(2,1)}, u32[]{:S(2)}, u32[]{:S(2)}) %collective-permute-start.28) | collective-permute-done | bytes 786464 | tf_op jit(solution)/shard_map/ppermute | solution.py:501
  263.4 2.3 collective-permute-start.35
  265.7 3.0 add_convert_fusion.7
  268.7 1.8 collective-permute-start.38
  271.0 20.4 %collective-permute-done.35 = bf16[1,2,384,768]{3,2,1,0:T(8,128)(2,1)} collective-permute-done((bf16[1,2,384,768]{3,2,1,0:T(8,128)(2,1)}, bf16[1,2,384,768]{3,2,1,0:T(8,128)(2,1)}, u32[]{:S(2)}, u32[]{:S(2)}) %collective-permute-start.35) | collective-permute-done | bytes 1179680 | tf_op jit(solution)/shard_map/ppermute | solution.py:536
  291.4 1.6 add_convert_fusion.5
  293.8 2.0 add_convert_fusion.4
  297.0 18.0 %collective-permute-done.37 = bf16[1,2,384,768]{3,2,1,0:T(8,128)(2,1)S(1)} collective-permute-done((bf16[1,2,384,768]{3,2,1,0:T(8,128)(2,1)S(1)}, bf16[1,2,384,768]{3,2,1,0:T(8,128)(2,1)S(1)}, u32[]{:S(2)}, u32[]{:S(2)}) %collective-permute-start.37) | collective-permute-done | bytes 1179680 | tf_op jit(solution)/shard_map/ppermute | solution.py:545
  316.4 8.1 %collective-permute-done.39 = bf16[1,2,384,768]{3,2,1,0:T(8,128)(2,1)S(1)} collective-permute-done((bf16[1,2,384,768]{3,2,1,0:T(8,128)(2,1)S(1)}, bf16[1,2,384,768]{3,2,1,0:T(8,128)(2,1)S(1)}, u32[]{:S(2)}, u32[]{:S(2)}) %collective-permute-start.39) | collective-permute-done | bytes 1179680 | tf_op jit(solution)/shard_map/ppermute | solution.py:563
  326.8 1.7 collective-permute-start.41
  329.1 6.9 %collective-permute-start.40 = (bf16[96,3200]{1,0:T(8,128)(2,1)}, bf16[96,3200]{1,0:T(8,128)(2,1)S(1)}, u32[]{:S(2)}, u32[]{:S(2)}) collective-permute-start(bf16[96,3200]{1,0:T(8,128)(2,1)} %reduce-scatter.2.cloned.1.call-done), channel_id=1, source_target_pairs={{0,1},{3,2},{4,5},{7,6},{8,9},{11,10},{12,13},{15,14},{16,17},{19,... | collective-permute-start | bytes 1843208 | tf_op jit(solution)/shard_map/ppermute | solution.py:536
  336.1 15.6 %collective-permute-done.45 = bf16[1,2,384,768]{3,2,1,0:T(8,128)(2,1)} collective-permute-done((bf16[1,2,384,768]{3,2,1,0:T(8,128)(2,1)S(1)}, bf16[1,2,384,768]{3,2,1,0:T(8,128)(2,1)}, u32[]{:S(2)}, u32[]{:S(2)}) %collective-permute-start.45) | collective-permute-done | bytes 1179680 | tf_op jit(solution)/shard_map/ppermute | solution.py:563
  353.1 2.0 add_convert_fusion.1
  355.1 1.6 collective-permute-start.46
  357.6 2.2 convert_add_fusion
  360.8 5.7 %collective-permute-start.42 = (bf16[2,2,64,768]{3,2,1,0:T(8,128)(2,1)S(1)}, bf16[2,2,64,768]{3,2,1,0:T(8,128)(2,1)S(1)}, u32[]{:S(2)}, u32[]{:S(2)}) collective-permute-start(bf16[2,2,64,768]{3,2,1,0:T(8,128)(2,1)S(1)} %pad_maximum_fusion.5), channel_id=1, source_target_pairs={{0,1},{1,0},{2,3},{3,2},{4,5},{5,4},{6,7},{7,6},{8,9},{9,8},{10,11... | collective-permute-start | bytes 1179656 | tf_op jit(solution)/shard_map/ppermute | solution.py:511
  367.2 1.9 collective-permute-start.44
  370.8 32.8 %collective-permute-done.46 = bf16[1,2,384,768]{3,2,1,0:T(8,128)(2,1)S(1)} collective-permute-done((bf16[1,2,384,768]{3,2,1,0:T(8,128)(2,1)S(1)}, bf16[1,2,384,768]{3,2,1,0:T(8,128)(2,1)S(1)}, u32[]{:S(2)}, u32[]{:S(2)}) %collective-permute-start.46) | collective-permute-done | bytes 1179680 | tf_op jit(solution)/shard_map/ppermute | solution.py:563
  404.1 2.6 maximum_convert_fusion.1
  406.7 2.6 maximum_convert_fusion
  409.3 2.8 collective-permute-done.42
  414.3 5.2 %collective-permute-done.48 = bf16[96,3200]{1,0:T(8,128)(2,1)S(1)} collective-permute-done((bf16[96,3200]{1,0:T(8,128)(2,1)S(1)}, bf16[96,3200]{1,0:T(8,128)(2,1)S(1)}, u32[]{:S(2)}, u32[]{:S(2)}) %collective-permute-start.48) | collective-permute-done | bytes 614432 | tf_op jit(solution)/shard_map/ppermute | solution.py:563
  (204 shorter events, 46.0 us)
Async XLA Ops:
  7.2 321.9 %reduce-scatter.2.cloned.1.call-start = ((), (), s32[]{:S(2)}) async-start(), calls=%async_computation.1 | async-start | bytes 5529600 | tf_op jit(solution)/shard_map/reduce_scatter | solution.py:826
  9.4 27.2 %collective-permute-start.1 = (bf16[96,3200]{1,0:T(8,128)(2,1)S(1)}, bf16[96,3200]{1,0:T(8,128)(2,1)S(1)}, u32[]{:S(2)}, u32[]{:S(2)}) collective-permute-start(bf16[96,3200]{1,0:T(8,128)(2,1)S(1)} %fusion.5.refs_0_), channel_id=1, source_target_pairs={{0,16},{4,20},{8,24},{12,28},{16,0},{20,4},{24,8},{28,12},{1,17},{... | collective-permute-start | bytes 1843208 | tf_op jit(solution)/shard_map/ppermute | solution.py:501
  12.4 24.1 %collective-permute-start = (bf16[96,3200]{1,0:T(8,128)(2,1)S(1)}, bf16[96,3200]{1,0:T(8,128)(2,1)S(1)}, u32[]{:S(2)}, u32[]{:S(2)}) collective-permute-start(bf16[96,3200]{1,0:T(8,128)(2,1)S(1)} %fusion.5.refs_0_), channel_id=1, source_target_pairs={{0,8},{4,12},{8,0},{12,4},{16,24},{20,28},{24,16},{28,20},{1,9},{5... | collective-permute-start | bytes 1843208 | tf_op jit(solution)/shard_map/ppermute | solution.py:501
  14.7 9.9 %collective-permute-start.4 = (bf16[128,768]{1,0:T(8,128)(2,1)}, bf16[128,768]{1,0:T(8,128)(2,1)S(1)}, u32[]{:S(2)}, u32[]{:S(2)}) collective-permute-start(bf16[128,768]{1,0:T(8,128)(2,1)} %get-tuple-element.240), channel_id=1, source_target_pairs={{0,3},{1,2},{2,1},{3,0},{4,7},{5,6},{6,5},{7,4},{8,11},{9,10},{10,... | collective-permute-start | bytes 589832 | tf_op jit(solution)/shard_map/ppermute | solution.py:511
  18.3 16.3 %collective-permute-start.3 = (bf16[128,768]{1,0:T(8,128)(2,1)}, bf16[128,768]{1,0:T(8,128)(2,1)S(1)}, u32[]{:S(2)}, u32[]{:S(2)}) collective-permute-start(bf16[128,768]{1,0:T(8,128)(2,1)} %get-tuple-element.241), channel_id=1, source_target_pairs={{0,2},{1,3},{2,0},{3,1},{4,6},{5,7},{6,4},{7,5},{8,10},{9,11},{10,... | collective-permute-start | bytes 589832 | tf_op jit(solution)/shard_map/ppermute | solution.py:511
  18.3 16.3 %collective-permute-start.2 = (bf16[128,768]{1,0:T(8,128)(2,1)S(1)}, bf16[128,768]{1,0:T(8,128)(2,1)}, u32[]{:S(2)}, u32[]{:S(2)}) collective-permute-start(bf16[128,768]{1,0:T(8,128)(2,1)S(1)} %get-tuple-element.242), channel_id=1, source_target_pairs={{0,1},{1,0},{2,3},{3,2},{4,5},{5,4},{6,7},{7,6},{8,9},{9,8},{10,11... | collective-permute-start | bytes 589832 | tf_op jit(solution)/shard_map/ppermute | solution.py:511
  36.6 10.3 %collective-permute-start.12 = (bf16[144,768]{1,0:T(8,128)(2,1)S(1)}, bf16[144,768]{1,0:T(8,128)(2,1)S(1)}, u32[]{:S(2)}, u32[]{:S(2)}) collective-permute-start(bf16[144,768]{1,0:T(8,128)(2,1)S(1)} %get-tuple-element.236), channel_id=1, source_target_pairs={{0,3},{1,2},{2,1},{3,0},{4,7},{5,6},{6,5},{7,4},{8,11},{9,10},{10,... | collective-permute-start | bytes 663560 | tf_op jit(solution)/shard_map/ppermute | solution.py:511
  39.2 16.9 %collective-permute-start.11 = (bf16[144,768]{1,0:T(8,128)(2,1)S(1)}, bf16[144,768]{1,0:T(8,128)(2,1)S(1)}, u32[]{:S(2)}, u32[]{:S(2)}) collective-permute-start(bf16[144,768]{1,0:T(8,128)(2,1)S(1)} %get-tuple-element.237), channel_id=1, source_target_pairs={{0,2},{1,3},{2,0},{3,1},{4,6},{5,7},{6,4},{7,5},{8,10},{9,11},{10,... | collective-permute-start | bytes 663560 | tf_op jit(solution)/shard_map/ppermute | solution.py:511
  39.2 16.9 %collective-permute-start.10 = (bf16[144,768]{1,0:T(8,128)(2,1)S(1)}, bf16[144,768]{1,0:T(8,128)(2,1)S(1)}, u32[]{:S(2)}, u32[]{:S(2)}) collective-permute-start(bf16[144,768]{1,0:T(8,128)(2,1)S(1)} %get-tuple-element.238), channel_id=1, source_target_pairs={{0,1},{1,0},{2,3},{3,2},{4,5},{5,4},{6,7},{7,6},{8,9},{9,8},{10,11... | collective-permute-start | bytes 663560 | tf_op jit(solution)/shard_map/ppermute | solution.py:511
  41.1 15.6 %collective-permute-start.9 = (bf16[48,3200]{1,0:T(8,128)(2,1)S(1)}, bf16[48,3200]{1,0:T(8,128)(2,1)S(1)}, u32[]{:S(2)}, u32[]{:S(2)}) collective-permute-start(bf16[48,3200]{1,0:T(8,128)(2,1)S(1)} %slice.204), channel_id=1, source_target_pairs={{0,8},{4,12},{8,0},{12,4},{16,24},{20,28},{24,16},{28,20},{1,9},{5... | collective-permute-start | bytes 921608 | tf_op jit(solution)/shard_map/ppermute | solution.py:501
  41.7 15.0 %collective-permute-start.8 = (bf16[48,3200]{1,0:T(8,128)(2,1)S(1)}, bf16[48,3200]{1,0:T(8,128)(2,1)S(1)}, u32[]{:S(2)}, u32[]{:S(2)}) collective-permute-start(bf16[48,3200]{1,0:T(8,128)(2,1)S(1)} %slice.203), channel_id=1, source_target_pairs={{0,16},{4,20},{8,24},{12,28},{16,0},{20,4},{24,8},{28,12},{1,17},{... | collective-permute-start | bytes 921608 | tf_op jit(solution)/shard_map/ppermute | solution.py:501
  47.0 10.4 %collective-permute-start.5 = (bf16[96,3200]{1,0:T(8,128)(2,1)S(1)}, bf16[96,3200]{1,0:T(8,128)(2,1)S(1)}, u32[]{:S(2)}, u32[]{:S(2)}) collective-permute-start(bf16[96,3200]{1,0:T(8,128)(2,1)S(1)} %fusion.5.refs_0_), channel_id=1, source_target_pairs={{0,4},{4,0},{8,12},{12,8},{16,20},{20,16},{24,28},{28,24},{1,5},{5... | collective-permute-start | bytes 1843208 | tf_op jit(solution)/shard_map/ppermute | solution.py:501
  56.1 3.8 collective-permute-start.6
  56.1 3.8 collective-permute-start.7
  59.9 26.4 %collective-permute-start.15 = (bf16[4,384,768]{2,1,0:T(8,128)(2,1)}, bf16[4,384,768]{2,1,0:T(8,128)(2,1)S(1)}, u32[]{:S(2)}, u32[]{:S(2)}) collective-permute-start(bf16[4,384,768]{2,1,0:T(8,128)(2,1)} %refs_7_), channel_id=1, source_target_pairs={{0,4},{4,0},{8,12},{12,8},{16,20},{20,16},{24,28},{28,24},{1,5},{5... | collective-permute-start | bytes 7077896 | tf_op jit(solution)/shard_map/ppermute | solution.py:501
  60.1 27.8 %collective-permute-start.16 = (bf16[4,384,768]{2,1,0:T(8,128)(2,1)}, bf16[4,384,768]{2,1,0:T(8,128)(2,1)}, u32[]{:S(2)}, u32[]{:S(2)}) collective-permute-start(bf16[4,384,768]{2,1,0:T(8,128)(2,1)} %refs_9_), channel_id=1, source_target_pairs={{0,4},{4,0},{8,12},{12,8},{16,20},{20,16},{24,28},{28,24},{1,5},{5... | collective-permute-start | bytes 7077896 | tf_op jit(solution)/shard_map/ppermute | solution.py:501
  60.5 21.8 %collective-permute-start.21 = (bf16[4,144,768]{2,1,0:T(8,128)(2,1)S(1)}, bf16[4,144,768]{2,1,0:T(8,128)(2,1)}, u32[]{:S(2)}, u32[]{:S(2)}) collective-permute-start(bf16[4,144,768]{2,1,0:T(8,128)(2,1)S(1)} %pad_maximum_fusion.refs_1_), channel_id=1, source_target_pairs={{0,16},{4,20},{8,24},{12,28},{16,0},{20,4},{24,8},{28,12},{1,17},{... | collective-permute-start | bytes 2654216 | tf_op jit(solution)/shard_map/ppermute | solution.py:501
  61.0 22.7 %collective-permute-start.20 = (bf16[4,144,768]{2,1,0:T(8,128)(2,1)S(1)}, bf16[4,144,768]{2,1,0:T(8,128)(2,1)}, u32[]{:S(2)}, u32[]{:S(2)}) collective-permute-start(bf16[4,144,768]{2,1,0:T(8,128)(2,1)S(1)} %pad_maximum_fusion.refs_1_), channel_id=1, source_target_pairs={{0,8},{4,12},{8,0},{12,4},{16,24},{20,28},{24,16},{28,20},{1,9},{5... | collective-permute-start | bytes 2654216 | tf_op jit(solution)/shard_map/ppermute | solution.py:501
  76.4 40.9 %collective-permute-start.19 = (bf16[4,128,768]{2,1,0:T(8,128)(2,1)}, bf16[4,128,768]{2,1,0:T(8,128)(2,1)}, u32[]{:S(2)}, u32[]{:S(2)}) collective-permute-start(bf16[4,128,768]{2,1,0:T(8,128)(2,1)} %bitcast.98), channel_id=1, source_target_pairs={{0,24},{4,28},{8,16},{12,20},{16,8},{20,12},{24,0},{28,4},{1,25},{... | collective-permute-start | bytes 2359304 | tf_op jit(solution)/shard_map/ppermute | solution.py:501
  82.3 35.1 %collective-permute-start.18 = (bf16[4,128,768]{2,1,0:T(8,128)(2,1)}, bf16[4,128,768]{2,1,0:T(8,128)(2,1)}, u32[]{:S(2)}, u32[]{:S(2)}) collective-permute-start(bf16[4,128,768]{2,1,0:T(8,128)(2,1)} %bitcast.99), channel_id=1, source_target_pairs={{0,16},{4,20},{8,24},{12,28},{16,0},{20,4},{24,8},{28,12},{1,17},{... | collective-permute-start | bytes 2359304 | tf_op jit(solution)/shard_map/ppermute | solution.py:501
  83.7 33.7 %collective-permute-start.17 = (bf16[4,128,768]{2,1,0:T(8,128)(2,1)}, bf16[4,128,768]{2,1,0:T(8,128)(2,1)}, u32[]{:S(2)}, u32[]{:S(2)}) collective-permute-start(bf16[4,128,768]{2,1,0:T(8,128)(2,1)} %bitcast.100), channel_id=1, source_target_pairs={{0,8},{4,12},{8,0},{12,4},{16,24},{20,28},{24,16},{28,20},{1,9},{5... | collective-permute-start | bytes 2359304 | tf_op jit(solution)/shard_map/ppermute | solution.py:501
  86.4 39.5 %collective-permute-start.23 = (bf16[2,144,768]{2,1,0:T(8,128)(2,1)S(1)}, bf16[2,144,768]{2,1,0:T(8,128)(2,1)S(1)}, u32[]{:S(2)}, u32[]{:S(2)}) collective-permute-start(bf16[2,144,768]{2,1,0:T(8,128)(2,1)S(1)} %slice.267), channel_id=1, source_target_pairs={{0,8},{4,12},{8,0},{12,4},{16,24},{20,28},{24,16},{28,20},{1,9},{5... | collective-permute-start | bytes 1327112 | tf_op jit(solution)/shard_map/ppermute | solution.py:501
  87.9 38.7 %collective-permute-start.22 = (bf16[2,144,768]{2,1,0:T(8,128)(2,1)S(1)}, bf16[2,144,768]{2,1,0:T(8,128)(2,1)}, u32[]{:S(2)}, u32[]{:S(2)}) collective-permute-start(bf16[2,144,768]{2,1,0:T(8,128)(2,1)S(1)} %slice.266), channel_id=1, source_target_pairs={{0,16},{4,20},{8,24},{12,28},{16,0},{20,4},{24,8},{28,12},{1,17},{... | collective-permute-start | bytes 1327112 | tf_op jit(solution)/shard_map/ppermute | solution.py:501
  185.4 3.6 collective-permute-start.30
  185.5 26.4 %collective-permute-start.24 = (bf16[4,128,768]{2,1,0:T(8,128)(2,1)}, bf16[4,128,768]{2,1,0:T(8,128)(2,1)S(1)}, u32[]{:S(2)}, u32[]{:S(2)}) collective-permute-start(bf16[4,128,768]{2,1,0:T(8,128)(2,1)} %get-tuple-element.104), channel_id=1, source_target_pairs={{0,8},{4,12},{8,0},{12,4},{16,24},{20,28},{24,16},{28,20},{1,9},{5... | collective-permute-start | bytes 2359304 | tf_op jit(solution)/shard_map/ppermute | solution.py:501
  186.1 25.8 %collective-permute-start.25 = (bf16[4,128,768]{2,1,0:T(8,128)(2,1)}, bf16[4,128,768]{2,1,0:T(8,128)(2,1)S(1)}, u32[]{:S(2)}, u32[]{:S(2)}) collective-permute-start(bf16[4,128,768]{2,1,0:T(8,128)(2,1)} %get-tuple-element.105), channel_id=1, source_target_pairs={{0,16},{4,20},{8,24},{12,28},{16,0},{20,4},{24,8},{28,12},{1,17},{... | collective-permute-start | bytes 2359304 | tf_op jit(solution)/shard_map/ppermute | solution.py:501
  187.4 36.0 %collective-permute-start.26 = (bf16[4,128,768]{2,1,0:T(8,128)(2,1)}, bf16[4,128,768]{2,1,0:T(8,128)(2,1)}, u32[]{:S(2)}, u32[]{:S(2)}) collective-permute-start(bf16[4,128,768]{2,1,0:T(8,128)(2,1)} %get-tuple-element.106), channel_id=1, source_target_pairs={{0,24},{4,28},{8,16},{12,20},{16,8},{20,12},{24,0},{28,4},{1,25},{... | collective-permute-start | bytes 2359304 | tf_op jit(solution)/shard_map/ppermute | solution.py:501
  190.7 32.7 %collective-permute-start.31 = (bf16[1,2,384,768]{3,2,1,0:T(8,128)(2,1)S(1)}, bf16[1,2,384,768]{3,2,1,0:T(8,128)(2,1)S(1)}, u32[]{:S(2)}, u32[]{:S(2)}) collective-permute-start(bf16[1,2,384,768]{3,2,1,0:T(8,128)(2,1)S(1)} %add_convert_fusion.9), channel_id=1, source_target_pairs={{0,1},{3,2},{4,5},{7,6},{8,9},{11,10},{12,13},{15,14},{16,17},{19,... | collective-permute-start | bytes 3538952 | tf_op jit(solution)/shard_map/ppermute | solution.py:536
  223.7 6.5 %collective-permute-start.32 = (bf16[3,2,384,768]{3,2,1,0:T(8,128)(2,1)}, bf16[3,2,384,768]{3,2,1,0:T(8,128)(2,1)S(1)}, u32[]{:S(2)}, u32[]{:S(2)}) collective-permute-start(bf16[3,2,384,768]{3,2,1,0:T(8,128)(2,1)} %get-tuple-element.122), channel_id=1, source_target_pairs={{0,4},{4,0},{8,12},{12,8},{16,20},{20,16},{24,28},{28,24},{1,5},{5... | collective-permute-start | bytes 10616840 | tf_op jit(solution)/shard_map/ppermute | solution.py:501
  224.7 32.2 %collective-permute-start.27 = (bf16[4,128,768]{2,1,0:T(8,128)(2,1)}, bf16[4,128,768]{2,1,0:T(8,128)(2,1)}, u32[]{:S(2)}, u32[]{:S(2)}) collective-permute-start(bf16[4,128,768]{2,1,0:T(8,128)(2,1)} %get-tuple-element.107), channel_id=1, source_target_pairs={{0,8},{4,12},{8,0},{12,4},{16,24},{20,28},{24,16},{28,20},{1,9},{5... | collective-permute-start | bytes 2359304 | tf_op jit(solution)/shard_map/ppermute | solution.py:501
  226.5 36.8 %collective-permute-start.28 = (bf16[4,128,768]{2,1,0:T(8,128)(2,1)}, bf16[4,128,768]{2,1,0:T(8,128)(2,1)}, u32[]{:S(2)}, u32[]{:S(2)}) collective-permute-start(bf16[4,128,768]{2,1,0:T(8,128)(2,1)} %get-tuple-element.108), channel_id=1, source_target_pairs={{0,16},{4,20},{8,24},{12,28},{16,0},{20,4},{24,8},{28,12},{1,17},{... | collective-permute-start | bytes 2359304 | tf_op jit(solution)/shard_map/ppermute | solution.py:501
  227.8 35.5 %collective-permute-start.29 = (bf16[4,128,768]{2,1,0:T(8,128)(2,1)}, bf16[4,128,768]{2,1,0:T(8,128)(2,1)}, u32[]{:S(2)}, u32[]{:S(2)}) collective-permute-start(bf16[4,128,768]{2,1,0:T(8,128)(2,1)} %get-tuple-element.109), channel_id=1, source_target_pairs={{0,24},{4,28},{8,16},{12,20},{16,8},{20,12},{24,0},{28,4},{1,25},{... | collective-permute-start | bytes 2359304 | tf_op jit(solution)/shard_map/ppermute | solution.py:501
  228.2 35.1 %collective-permute-start.33 = (bf16[1,2,384,768]{3,2,1,0:T(8,128)(2,1)S(1)}, bf16[1,2,384,768]{3,2,1,0:T(8,128)(2,1)S(1)}, u32[]{:S(2)}, u32[]{:S(2)}) collective-permute-start(bf16[1,2,384,768]{3,2,1,0:T(8,128)(2,1)S(1)} %add_convert_fusion.8), channel_id=1, source_target_pairs={{1,2},{2,1},{5,6},{6,5},{9,10},{10,9},{13,14},{14,13},{17,18},{18,... | collective-permute-start | bytes 3538952 | tf_op jit(solution)/shard_map/ppermute | solution.py:556
  232.8 30.6 %collective-permute-start.34 = (bf16[1,2,384,768]{3,2,1,0:T(8,128)(2,1)}, bf16[1,2,384,768]{3,2,1,0:T(8,128)(2,1)}, u32[]{:S(2)}, u32[]{:S(2)}) collective-permute-start(bf16[1,2,384,768]{3,2,1,0:T(8,128)(2,1)} %get-tuple-element.123), channel_id=1, source_target_pairs={{0,1},{3,2},{4,5},{7,6},{8,9},{11,10},{12,13},{15,14},{16,17},{19,... | collective-permute-start | bytes 3538952 | tf_op jit(solution)/shard_map/ppermute | solution.py:536
  263.4 28.0 %collective-permute-start.35 = (bf16[1,2,384,768]{3,2,1,0:T(8,128)(2,1)}, bf16[1,2,384,768]{3,2,1,0:T(8,128)(2,1)}, u32[]{:S(2)}, u32[]{:S(2)}) collective-permute-start(bf16[1,2,384,768]{3,2,1,0:T(8,128)(2,1)} %get-tuple-element.141), channel_id=1, source_target_pairs={{0,1},{3,2},{4,5},{7,6},{8,9},{11,10},{12,13},{15,14},{16,17},{19,... | collective-permute-start | bytes 3538952 | tf_op jit(solution)/shard_map/ppermute | solution.py:536
  268.7 25.0 %collective-permute-start.38 = (bf16[1,2,384,768]{3,2,1,0:T(8,128)(2,1)}, bf16[1,2,384,768]{3,2,1,0:T(8,128)(2,1)}, u32[]{:S(2)}, u32[]{:S(2)}) collective-permute-start(bf16[1,2,384,768]{3,2,1,0:T(8,128)(2,1)} %add_convert_fusion.7), channel_id=1, source_target_pairs={{1,2},{2,1},{5,6},{6,5},{9,10},{10,9},{13,14},{14,13},{17,18},{18,... | collective-permute-start | bytes 3538952 | tf_op jit(solution)/shard_map/ppermute | solution.py:556
  270.9 44.1 %collective-permute-start.37 = (bf16[1,2,384,768]{3,2,1,0:T(8,128)(2,1)S(1)}, bf16[1,2,384,768]{3,2,1,0:T(8,128)(2,1)S(1)}, u32[]{:S(2)}, u32[]{:S(2)}) collective-permute-start(bf16[1,2,384,768]{3,2,1,0:T(8,128)(2,1)S(1)} %broadcast_select_fusion.4), channel_id=1, source_target_pairs={{0,1},{1,0},{2,3},{3,2},{4,5},{5,4},{6,7},{7,6},{8,9},{9,8},{10,11... | collective-permute-start | bytes 3538952 | tf_op jit(solution)/shard_map/ppermute | solution.py:545
  293.0 23.4 %collective-permute-start.36 = (bf16[1,2,384,768]{3,2,1,0:T(8,128)(2,1)S(1)}, bf16[1,2,384,768]{3,2,1,0:T(8,128)(2,1)S(1)}, u32[]{:S(2)}, u32[]{:S(2)}) collective-permute-start(bf16[1,2,384,768]{3,2,1,0:T(8,128)(2,1)S(1)} %add_convert_fusion.5), channel_id=1, source_target_pairs={{1,2},{2,1},{5,6},{6,5},{9,10},{10,9},{13,14},{14,13},{17,18},{18,... | collective-permute-start | bytes 3538952 | tf_op jit(solution)/shard_map/ppermute | solution.py:556
  295.7 28.8 %collective-permute-start.39 = (bf16[1,2,384,768]{3,2,1,0:T(8,128)(2,1)S(1)}, bf16[1,2,384,768]{3,2,1,0:T(8,128)(2,1)S(1)}, u32[]{:S(2)}, u32[]{:S(2)}) collective-permute-start(bf16[1,2,384,768]{3,2,1,0:T(8,128)(2,1)S(1)} %add_convert_fusion.4), channel_id=1, source_target_pairs={{1,0},{2,3},{5,4},{6,7},{9,8},{10,11},{13,12},{14,15},{17,16},{18,... | collective-permute-start | bytes 3538952 | tf_op jit(solution)/shard_map/ppermute | solution.py:563
  325.5 26.1 %collective-permute-start.45 = (bf16[1,2,384,768]{3,2,1,0:T(8,128)(2,1)S(1)}, bf16[1,2,384,768]{3,2,1,0:T(8,128)(2,1)}, u32[]{:S(2)}, u32[]{:S(2)}) collective-permute-start(bf16[1,2,384,768]{3,2,1,0:T(8,128)(2,1)S(1)} %add_convert_fusion.2), channel_id=1, source_target_pairs={{1,0},{2,3},{5,4},{6,7},{9,8},{10,11},{13,12},{14,15},{17,16},{18,... | collective-permute-start | bytes 3538952 | tf_op jit(solution)/shard_map/ppermute | solution.py:563
  326.8 26.3 %collective-permute-start.41 = (bf16[1,2,384,768]{3,2,1,0:T(8,128)(2,1)}, bf16[1,2,384,768]{3,2,1,0:T(8,128)(2,1)}, u32[]{:S(2)}, u32[]{:S(2)}) collective-permute-start(bf16[1,2,384,768]{3,2,1,0:T(8,128)(2,1)} %add_convert_fusion.3), channel_id=1, source_target_pairs={{1,2},{2,1},{5,6},{6,5},{9,10},{10,9},{13,14},{14,13},{17,18},{18,... | collective-permute-start | bytes 3538952 | tf_op jit(solution)/shard_map/ppermute | solution.py:556
  329.1 27.6 %collective-permute-start.40 = (bf16[96,3200]{1,0:T(8,128)(2,1)}, bf16[96,3200]{1,0:T(8,128)(2,1)S(1)}, u32[]{:S(2)}, u32[]{:S(2)}) collective-permute-start(bf16[96,3200]{1,0:T(8,128)(2,1)} %reduce-scatter.2.cloned.1.call-done), channel_id=1, source_target_pairs={{0,1},{3,2},{4,5},{7,6},{8,9},{11,10},{12,13},{15,14},{16,17},{19,... | collective-permute-start | bytes 1843208 | tf_op jit(solution)/shard_map/ppermute | solution.py:536
  355.1 48.6 %collective-permute-start.46 = (bf16[1,2,384,768]{3,2,1,0:T(8,128)(2,1)S(1)}, bf16[1,2,384,768]{3,2,1,0:T(8,128)(2,1)S(1)}, u32[]{:S(2)}, u32[]{:S(2)}) collective-permute-start(bf16[1,2,384,768]{3,2,1,0:T(8,128)(2,1)S(1)} %add_convert_fusion.1), channel_id=1, source_target_pairs={{1,0},{2,3},{5,4},{6,7},{9,8},{10,11},{13,12},{14,15},{17,16},{18,... | collective-permute-start | bytes 3538952 | tf_op jit(solution)/shard_map/ppermute | solution.py:563
  356.9 12.3 %collective-permute-start.47 = (bf16[96,3200]{1,0:T(8,128)(2,1)S(1)}, bf16[96,3200]{1,0:T(8,128)(2,1)S(1)}, u32[]{:S(2)}, u32[]{:S(2)}) collective-permute-start(bf16[96,3200]{1,0:T(8,128)(2,1)S(1)} %add_convert_fusion.11), channel_id=1, source_target_pairs={{1,2},{2,1},{5,6},{6,5},{9,10},{10,9},{13,14},{14,13},{17,18},{18,... | collective-permute-start | bytes 1843208 | tf_op jit(solution)/shard_map/ppermute | solution.py:556
  360.8 51.3 %collective-permute-start.42 = (bf16[2,2,64,768]{3,2,1,0:T(8,128)(2,1)S(1)}, bf16[2,2,64,768]{3,2,1,0:T(8,128)(2,1)S(1)}, u32[]{:S(2)}, u32[]{:S(2)}) collective-permute-start(bf16[2,2,64,768]{3,2,1,0:T(8,128)(2,1)S(1)} %pad_maximum_fusion.5), channel_id=1, source_target_pairs={{0,1},{1,0},{2,3},{3,2},{4,5},{5,4},{6,7},{7,6},{8,9},{9,8},{10,11... | collective-permute-start | bytes 1179656 | tf_op jit(solution)/shard_map/ppermute | solution.py:511
  366.6 45.5 %collective-permute-start.43 = (bf16[2,2,64,768]{3,2,1,0:T(8,128)(2,1)S(1)}, bf16[2,2,64,768]{3,2,1,0:T(8,128)(2,1)S(1)}, u32[]{:S(2)}, u32[]{:S(2)}) collective-permute-start(bf16[2,2,64,768]{3,2,1,0:T(8,128)(2,1)S(1)} %pad_maximum_fusion.6), channel_id=1, source_target_pairs={{0,2},{1,3},{2,0},{3,1},{4,6},{5,7},{6,4},{7,5},{8,10},{9,11},{10,... | collective-permute-start | bytes 1179656 | tf_op jit(solution)/shard_map/ppermute | solution.py:511
  367.2 44.9 %collective-permute-start.44 = (bf16[2,2,64,768]{3,2,1,0:T(8,128)(2,1)S(1)}, bf16[2,2,64,768]{3,2,1,0:T(8,128)(2,1)S(1)}, u32[]{:S(2)}, u32[]{:S(2)}) collective-permute-start(bf16[2,2,64,768]{3,2,1,0:T(8,128)(2,1)S(1)} %pad_maximum_fusion.7), channel_id=1, source_target_pairs={{0,3},{1,2},{2,1},{3,0},{4,7},{5,6},{6,5},{7,4},{8,11},{9,10},{10,... | collective-permute-start | bytes 1179656 | tf_op jit(solution)/shard_map/ppermute | solution.py:511
  369.4 50.1 %collective-permute-start.48 = (bf16[96,3200]{1,0:T(8,128)(2,1)S(1)}, bf16[96,3200]{1,0:T(8,128)(2,1)S(1)}, u32[]{:S(2)}, u32[]{:S(2)}) collective-permute-start(bf16[96,3200]{1,0:T(8,128)(2,1)S(1)} %add_convert_fusion.10), channel_id=1, source_target_pairs={{1,0},{2,3},{5,4},{6,7},{9,8},{10,11},{13,12},{14,15},{17,16},{18,... | collective-permute-start | bytes 1843208 | tf_op jit(solution)/shard_map/ppermute | solution.py:563
  (39 other events, 320.3 us)
Sparse Core Ops, SparseCore 0:
  263.5 53.2 reduce-scatter.1

commit v6 on v5

--- a/solution.py
+++ b/solution.py
@@ -822,7 +822,7 @@
         dwr,
     )
     flying = (outs, lines[0].waiting(), lines[1].waiting())
-    dense = tie(dense, flying)
+    dense = tie(dense, flying[1:])
     dense = lax.psum_scatter(dense, "fsdp", scatter_dimension=0, tiled=True)
     lines[2].raw, lines[3].raw = tie((lines[2].raw, lines[3].raw), grad_tok)
     lines[2].inwards()

time: 436 us -> 473 us (1.085)
  waiting for transfers between devices: 164 us -> 196 us
  starting transfers between devices: 64.3 us -> 69.2 us
    ppermute x26, waiting for transfers between devices: 35.2 us -> 67.1 us  [flip(): return lax.ppermute(array, 'fsdp', [(n, n ^ bits) for n in range(fsdp)])]
    ppermute x4, waiting for transfers between devices: 20.4 us -> 3.88 us  [inwards(): self.moving = lax.ppermute(self.raw, 'seq', [(0, 1), (3, 2)])]
    ppermute x4, waiting for transfers between devices: 61.7 us -> 74.8 us  [outwards(): self.moving = lax.ppermute(self.total, 'seq', [(1, 0), (2, 3)])]
  transfers between devices with their start and end apart: 50 -> 50, of which waited for: 21 -> 23; matrix products, arithmetic and copies ran while one was open for 9% -> 8% of each run, Pallas kernels for 19% -> 18%
where the time goes in v6:
time: 473 us; the launch traced here: 466 us
  waiting for transfers between devices  196 us (41%)
  Pallas kernels  142 us (30%)
  starting transfers between devices  69.2 us (15%)
  other arithmetic  31.3 us (7%)
  between operations  15 us (3%)
  local copies, waits for them, and re-layouts  12.5 us (3%)
    pallas_call x2, Pallas kernels, experts_call(): pl.pallas_call(functools.partial(expert_kernel, plan), grid=(groups,), in...  86.6 us
    ppermute x4, waiting for transfers between devices, outwards(): self.moving = lax.ppermute(self.total, 'seq', [(1, 0), (2, 3)])  74.8 us
    ppermute x26, waiting for transfers between devices, flip(): return lax.ppermute(array, 'fsdp', [(n, n ^ bits) for n in range(fsdp)])  67.1 us
    ppermute x9, waiting for transfers between devices, exchange(): lax.ppermute(pieces[k], 'seq', [(n, n ^ k) for n in range(count)])  28.4 us
    ppermute x26, starting transfers between devices, flip(): return lax.ppermute(array, 'fsdp', [(n, n ^ bits) for n in range(fsdp)])  22.3 us
    ppermute x1, waiting for transfers between devices, inwards_with(): self.moving = lax.ppermute(both, 'seq', [(0, 1), (1, 0), (2, 3), (3, 2)])  21.3 us
    pallas_call x1, Pallas kernels, back(): pl.pallas_call(back_kernel, grid=(images,), in_specs=[split] * 7 + [pl.Bl...  21.2 us
    pallas_call x1, Pallas kernels, grads_call(): pl.pallas_call(functools.partial(grads_kernel, plan), grid=(many,), in_sp...  19.9 us
  transfers between devices with their start and end apart: 50, of which 23 were waited for; matrix products, arithmetic and copies ran while one was open for 8% of the time, Pallas kernels for 18%

profile of v6, /device:TPU:0, one launch (start us, length us, event | category | flops | bytes accessed | tf_op | source)
XLA Modules:
  0.0 466.4 jit_solution(996062770298765063)
XLA Ops:
  9.4 3.0 collective-permute-start.1
  14.7 3.6 collective-permute-start.4
  22.7 1.9 collective-permute-done.4
  24.6 10.0 %collective-permute-done.3 = bf16[128,768]{1,0:T(8,128)(2,1)S(1)} collective-permute-done((bf16[128,768]{1,0:T(8,128)(2,1)}, bf16[128,768]{1,0:T(8,128)(2,1)S(1)}, u32[]{:S(2)}, u32[]{:S(2)}) %collective-permute-start.3) | collective-permute-done | bytes 196640 | tf_op jit(solution)/shard_map/ppermute | solution.py:511
  34.6 1.9 pad_maximum_fusion.1.refs_10_.tok_ref
  36.6 2.5 collective-permute-start.12
  39.2 1.9 collective-permute-start.10
  42.3 4.7 %collective-permute-done.12 = bf16[144,768]{1,0:T(8,128)(2,1)S(1)} collective-permute-done((bf16[144,768]{1,0:T(8,128)(2,1)S(1)}, bf16[144,768]{1,0:T(8,128)(2,1)S(1)}, u32[]{:S(2)}, u32[]{:S(2)}) %collective-permute-start.12) | collective-permute-done | bytes 221216 | tf_op jit(solution)/shard_map/ppermute | solution.py:511
  47.0 9.1 %collective-permute-done.11 = bf16[144,768]{1,0:T(8,128)(2,1)S(1)} collective-permute-done((bf16[144,768]{1,0:T(8,128)(2,1)S(1)}, bf16[144,768]{1,0:T(8,128)(2,1)S(1)}, u32[]{:S(2)}, u32[]{:S(2)}) %collective-permute-start.11) | collective-permute-done | bytes 221216 | tf_op jit(solution)/shard_map/ppermute | solution.py:511
  57.3 2.1 collective-permute-done.13.refs_8_
  61.6 14.7 %front.1 = (f32[4,2,64,768]{3,2,1,0:T(8,128)}, bf16[4,2,64,768]{3,2,1,0:T(8,128)(2,1)}, bf16[2,256,2304]{2,1,0:T(8,128)(2,1)}, bf16[2,256,768]{2,1,0:T(8,128)(2,...) custom-call(bf16[96,3200]{1,0:T(8,128)(2,1)} %copy-done.6, ...), custom_call_target="tpu_custom_call" | custom-call | flops 1000 | bytes 1000 | tf_op jit(solution)/shard_map/front/pallas_call | solution.py:124
  76.4 2.5 collective-permute-start.19
  78.9 3.4 collective-permute-done.21.refs_4_
  89.4 27.9 %experts_own.1 = (bf16[4,2,768,768]{3,2,1,0:T(8,128)(2,1)}, f32[8,768]{1,0:T(8,128)}, bf16[4,128,768]{2,1,0:T(8,128)(2,1)}, bf16[4,128,768]{2,1,0:T(8,128)(2,1)}) custom-call(bf16[4,128,768]{2,1,0:T(8,128)(2,1)} %bitcast.101, bf16[4,144,768]{2,1,0:T(8,128)(2,1)} %copy-done, bf16[4,384,768]{2,1,0:T(8,128)(2,1)} %refs_7_, bf16[4,384,768]{2,1,0:T(8,128)(2,1)} %copy-done.7, ...), custom_call_target="tpu_custom_call" | custom-call | flops 1000 | bytes 1000 | tf_op jit(solution)/shard_map/experts_own/pallas_call | solution.py:380
  117.4 8.5 %collective-permute-done.23.refs_6_ = bf16[2,144,768]{2,1,0:T(8,128)(2,1)S(1)} collective-permute-done((bf16[2,144,768]{2,1,0:T(8,128)(2,1)S(1)}, bf16[2,144,768]{2,1,0:T(8,128)(2,1)S(1)}, u32[]{:S(2)}, u32[]{:S(2)}) %collective-permute-start.23) | collective-permute-done | bytes 442400 | tf_op jit(solution)/shard_map/ppermute | solution.py:501
  126.7 58.7 %experts_far.1 = (bf16[1536,2304]{1,0:T(8,128)(2,1)}, bf16[1536,2304]{1,0:T(8,128)(2,1)}, bf16[1,2,384,768]{3,2,1,0:T(8,128)(2,1)}, bf16[1,2,384,768]{3,2,1,0:T(...) custom-call(bf16[4,128,768]{2,1,0:T(8,128)(2,1)} %collective-permute, ...), custom_call_target="tpu_custom_call" | custom-call | flops 72477573120 | bytes 16777216 | tf_op jit(solution)/shard_map/experts_far/pallas_call | solution.py:380
  187.4 1.6 collective-permute-start.26
  189.0 1.6 add_convert_fusion.9
  192.0 19.9 %expert_grads.1 = (bf16[3,2,384,768]{3,2,1,0:T(8,128)(2,1)}, bf16[3,2,384,768]{3,2,1,0:T(8,128)(2,1)}) custom-call(bf16[4,128,768]{2,1,0:T(8,128)(2,1)} %collective-permute-done.17.refs_0_, bf16[4,128,768]{2,1,0:T(8,128)(2,1)} %collective-permute-done.18.refs_1_, bf16[4,128,768]{2,1,0:T(8,128)(2,1)} %collective-permute-done.19.refs_2_, ...), custom_call_target="tpu_custom_call" | custom-call | flops 43486543872 | bytes 16777216 | tf_op jit(solution)/shard_map/expert_grads/pallas_call | solution.py:481
  211.9 11.4 %collective-permute-done.26 = bf16[4,128,768]{2,1,0:T(8,128)(2,1)} collective-permute-done((bf16[4,128,768]{2,1,0:T(8,128)(2,1)}, bf16[4,128,768]{2,1,0:T(8,128)(2,1)}, u32[]{:S(2)}, u32[]{:S(2)}) %collective-permute-start.26) | collective-permute-done | bytes 786464 | tf_op jit(solution)/shard_map/ppermute | solution.py:501
  225.5 4.6 collective-permute-done.32
  231.1 1.6 fusion.26
  232.7 2.3 collective-permute-start.34
  235.0 21.2 %back.1 = (bf16[2,64,768]{2,1,0:T(8,128)(2,1)}, bf16[2,64,768]{2,1,0:T(8,128)(2,1)}, bf16[2,64,768]{2,1,0:T(8,128)(2,1)}, bf16[2,64,768]{2,1,0:T(8,128)(2,1)}, bf16[768,3200]{1,0:T(8,128)(2,1)}) custom-call(bf16[4,2,64,768]{3,2,1,0:T(8,128)(2,1)} %bitcast.128, bf16[4,2,64,768]{3,2,1,0:T(8,128)(2,1)} %bitcast.129, bf16[4,2,64,768]{3,2,1,0:T(8,128)(2,1)} %bitcast.130, ...), custom_call_target="tpu_custom_call" | custom-call | flops 30198988800 | bytes 16777216 | tf_op jit(solution)/shard_map/back/pallas_call | solution.py:649
  256.3 3.9 collective-permute-done.34
  260.2 1.8 collective-permute-start.27
  263.3 5.5 %collective-permute-start.35 = (bf16[1,2,384,768]{3,2,1,0:T(8,128)(2,1)}, bf16[1,2,384,768]{3,2,1,0:T(8,128)(2,1)}, u32[]{:S(2)}, u32[]{:S(2)}) collective-permute-start(bf16[1,2,384,768]{3,2,1,0:T(8,128)(2,1)} %get-tuple-element.141), channel_id=1, source_target_pairs={{0,1},{3,2},{4,5},{7,6},{8,9},{11,10},{12,13},{15,14},{16,17},{19,... | collective-permute-start | bytes 3538952 | tf_op jit(solution)/shard_map/ppermute | solution.py:536
  269.2 3.2 add_convert_fusion.7
  272.3 1.7 collective-permute-start.38
  274.0 7.0 %collective-permute-done.27 = bf16[4,128,768]{2,1,0:T(8,128)(2,1)} collective-permute-done((bf16[4,128,768]{2,1,0:T(8,128)(2,1)}, bf16[4,128,768]{2,1,0:T(8,128)(2,1)}, u32[]{:S(2)}, u32[]{:S(2)}) %collective-permute-start.27) | collective-permute-done | bytes 786464 | tf_op jit(solution)/shard_map/ppermute | solution.py:501
  281.0 10.1 %collective-permute-done.28 = bf16[4,128,768]{2,1,0:T(8,128)(2,1)} collective-permute-done((bf16[4,128,768]{2,1,0:T(8,128)(2,1)}, bf16[4,128,768]{2,1,0:T(8,128)(2,1)}, u32[]{:S(2)}, u32[]{:S(2)}) %collective-permute-start.28) | collective-permute-done | bytes 786464 | tf_op jit(solution)/shard_map/ppermute | solution.py:501
  291.1 17.8 %collective-permute-done.29 = bf16[4,128,768]{2,1,0:T(8,128)(2,1)} collective-permute-done((bf16[4,128,768]{2,1,0:T(8,128)(2,1)}, bf16[4,128,768]{2,1,0:T(8,128)(2,1)}, u32[]{:S(2)}, u32[]{:S(2)}) %collective-permute-start.29) | collective-permute-done | bytes 786464 | tf_op jit(solution)/shard_map/ppermute | solution.py:501
  309.4 3.4 collective-permute-start.37
  312.8 1.6 add_convert_fusion.5
  315.1 1.9 add_convert_fusion.4
  318.3 21.3 %collective-permute-done.37 = bf16[1,2,384,768]{3,2,1,0:T(8,128)(2,1)S(1)} collective-permute-done((bf16[1,2,384,768]{3,2,1,0:T(8,128)(2,1)S(1)}, bf16[1,2,384,768]{3,2,1,0:T(8,128)(2,1)S(1)}, u32[]{:S(2)}, u32[]{:S(2)}) %collective-permute-start.37) | collective-permute-done | bytes 1179680 | tf_op jit(solution)/shard_map/ppermute | solution.py:545
  341.0 20.1 %collective-permute-done.39 = bf16[1,2,384,768]{3,2,1,0:T(8,128)(2,1)S(1)} collective-permute-done((bf16[1,2,384,768]{3,2,1,0:T(8,128)(2,1)S(1)}, bf16[1,2,384,768]{3,2,1,0:T(8,128)(2,1)S(1)}, u32[]{:S(2)}, u32[]{:S(2)}) %collective-permute-start.39) | collective-permute-done | bytes 1179680 | tf_op jit(solution)/shard_map/ppermute | solution.py:563
  363.4 1.8 collective-permute-start.41
  365.8 6.4 %collective-permute-start.40 = (bf16[96,3200]{1,0:T(8,128)(2,1)}, bf16[96,3200]{1,0:T(8,128)(2,1)S(1)}, u32[]{:S(2)}, u32[]{:S(2)}) collective-permute-start(bf16[96,3200]{1,0:T(8,128)(2,1)} %reduce-scatter.2.cloned.1.call-done), channel_id=1, source_target_pairs={{0,1},{3,2},{4,5},{7,6},{8,9},{11,10},{12,13},{15,14},{16,17},{19,... | collective-permute-start | bytes 1843208 | tf_op jit(solution)/shard_map/ppermute | solution.py:536
  372.2 16.1 %collective-permute-done.45 = bf16[1,2,384,768]{3,2,1,0:T(8,128)(2,1)} collective-permute-done((bf16[1,2,384,768]{3,2,1,0:T(8,128)(2,1)S(1)}, bf16[1,2,384,768]{3,2,1,0:T(8,128)(2,1)}, u32[]{:S(2)}, u32[]{:S(2)}) %collective-permute-start.45) | collective-permute-done | bytes 1179680 | tf_op jit(solution)/shard_map/ppermute | solution.py:563
  389.7 2.0 add_convert_fusion.1
  394.1 2.2 convert_add_fusion
  397.3 5.2 %collective-permute-start.42 = (bf16[2,2,64,768]{3,2,1,0:T(8,128)(2,1)S(1)}, bf16[2,2,64,768]{3,2,1,0:T(8,128)(2,1)S(1)}, u32[]{:S(2)}, u32[]{:S(2)}) collective-permute-start(bf16[2,2,64,768]{3,2,1,0:T(8,128)(2,1)S(1)} %pad_maximum_fusion.5), channel_id=1, source_target_pairs={{0,1},{1,0},{2,3},{3,2},{4,5},{5,4},{6,7},{7,6},{8,9},{9,8},{10,11... | collective-permute-start | bytes 1179656 | tf_op jit(solution)/shard_map/ppermute | solution.py:511
  406.8 33.4 %collective-permute-done.46 = bf16[1,2,384,768]{3,2,1,0:T(8,128)(2,1)S(1)} collective-permute-done((bf16[1,2,384,768]{3,2,1,0:T(8,128)(2,1)S(1)}, bf16[1,2,384,768]{3,2,1,0:T(8,128)(2,1)S(1)}, u32[]{:S(2)}, u32[]{:S(2)}) %collective-permute-start.46) | collective-permute-done | bytes 1179680 | tf_op jit(solution)/shard_map/ppermute | solution.py:563
  440.7 2.6 maximum_convert_fusion.1
  443.3 2.6 maximum_convert_fusion
  445.9 2.8 collective-permute-done.42
  450.9 5.2 %collective-permute-done.48 = bf16[96,3200]{1,0:T(8,128)(2,1)S(1)} collective-permute-done((bf16[96,3200]{1,0:T(8,128)(2,1)S(1)}, bf16[96,3200]{1,0:T(8,128)(2,1)S(1)}, u32[]{:S(2)}, u32[]{:S(2)}) %collective-permute-start.48) | collective-permute-done | bytes 614432 | tf_op jit(solution)/shard_map/ppermute | solution.py:563
  (204 shorter events, 51.3 us)
Async XLA Ops:
  7.2 358.6 %reduce-scatter.2.cloned.1.call-start = ((), (), s32[]{:S(2)}) async-start(), calls=%async_computation.1 | async-start | bytes 5529600 | tf_op jit(solution)/shard_map/reduce_scatter | solution.py:826
  9.4 27.2 %collective-permute-start.1 = (bf16[96,3200]{1,0:T(8,128)(2,1)S(1)}, bf16[96,3200]{1,0:T(8,128)(2,1)S(1)}, u32[]{:S(2)}, u32[]{:S(2)}) collective-permute-start(bf16[96,3200]{1,0:T(8,128)(2,1)S(1)} %fusion.5.refs_0_), channel_id=1, source_target_pairs={{0,16},{4,20},{8,24},{12,28},{16,0},{20,4},{24,8},{28,12},{1,17},{... | collective-permute-start | bytes 1843208 | tf_op jit(solution)/shard_map/ppermute | solution.py:501
  12.4 24.1 %collective-permute-start = (bf16[96,3200]{1,0:T(8,128)(2,1)S(1)}, bf16[96,3200]{1,0:T(8,128)(2,1)S(1)}, u32[]{:S(2)}, u32[]{:S(2)}) collective-permute-start(bf16[96,3200]{1,0:T(8,128)(2,1)S(1)} %fusion.5.refs_0_), channel_id=1, source_target_pairs={{0,8},{4,12},{8,0},{12,4},{16,24},{20,28},{24,16},{28,20},{1,9},{5... | collective-permute-start | bytes 1843208 | tf_op jit(solution)/shard_map/ppermute | solution.py:501
  14.7 9.9 %collective-permute-start.4 = (bf16[128,768]{1,0:T(8,128)(2,1)}, bf16[128,768]{1,0:T(8,128)(2,1)S(1)}, u32[]{:S(2)}, u32[]{:S(2)}) collective-permute-start(bf16[128,768]{1,0:T(8,128)(2,1)} %get-tuple-element.240), channel_id=1, source_target_pairs={{0,3},{1,2},{2,1},{3,0},{4,7},{5,6},{6,5},{7,4},{8,11},{9,10},{10,... | collective-permute-start | bytes 589832 | tf_op jit(solution)/shard_map/ppermute | solution.py:511
  18.3 16.3 %collective-permute-start.3 = (bf16[128,768]{1,0:T(8,128)(2,1)}, bf16[128,768]{1,0:T(8,128)(2,1)S(1)}, u32[]{:S(2)}, u32[]{:S(2)}) collective-permute-start(bf16[128,768]{1,0:T(8,128)(2,1)} %get-tuple-element.241), channel_id=1, source_target_pairs={{0,2},{1,3},{2,0},{3,1},{4,6},{5,7},{6,4},{7,5},{8,10},{9,11},{10,... | collective-permute-start | bytes 589832 | tf_op jit(solution)/shard_map/ppermute | solution.py:511
  18.3 16.3 %collective-permute-start.2 = (bf16[128,768]{1,0:T(8,128)(2,1)S(1)}, bf16[128,768]{1,0:T(8,128)(2,1)}, u32[]{:S(2)}, u32[]{:S(2)}) collective-permute-start(bf16[128,768]{1,0:T(8,128)(2,1)S(1)} %get-tuple-element.242), channel_id=1, source_target_pairs={{0,1},{1,0},{2,3},{3,2},{4,5},{5,4},{6,7},{7,6},{8,9},{9,8},{10,11... | collective-permute-start | bytes 589832 | tf_op jit(solution)/shard_map/ppermute | solution.py:511
  36.6 10.3 %collective-permute-start.12 = (bf16[144,768]{1,0:T(8,128)(2,1)S(1)}, bf16[144,768]{1,0:T(8,128)(2,1)S(1)}, u32[]{:S(2)}, u32[]{:S(2)}) collective-permute-start(bf16[144,768]{1,0:T(8,128)(2,1)S(1)} %get-tuple-element.236), channel_id=1, source_target_pairs={{0,3},{1,2},{2,1},{3,0},{4,7},{5,6},{6,5},{7,4},{8,11},{9,10},{10,... | collective-permute-start | bytes 663560 | tf_op jit(solution)/shard_map/ppermute | solution.py:511
  39.2 16.9 %collective-permute-start.11 = (bf16[144,768]{1,0:T(8,128)(2,1)S(1)}, bf16[144,768]{1,0:T(8,128)(2,1)S(1)}, u32[]{:S(2)}, u32[]{:S(2)}) collective-permute-start(bf16[144,768]{1,0:T(8,128)(2,1)S(1)} %get-tuple-element.237), channel_id=1, source_target_pairs={{0,2},{1,3},{2,0},{3,1},{4,6},{5,7},{6,4},{7,5},{8,10},{9,11},{10,... | collective-permute-start | bytes 663560 | tf_op jit(solution)/shard_map/ppermute | solution.py:511
  39.2 16.9 %collective-permute-start.10 = (bf16[144,768]{1,0:T(8,128)(2,1)S(1)}, bf16[144,768]{1,0:T(8,128)(2,1)S(1)}, u32[]{:S(2)}, u32[]{:S(2)}) collective-permute-start(bf16[144,768]{1,0:T(8,128)(2,1)S(1)} %get-tuple-element.238), channel_id=1, source_target_pairs={{0,1},{1,0},{2,3},{3,2},{4,5},{5,4},{6,7},{7,6},{8,9},{9,8},{10,11... | collective-permute-start | bytes 663560 | tf_op jit(solution)/shard_map/ppermute | solution.py:511
  41.1 15.6 %collective-permute-start.9 = (bf16[48,3200]{1,0:T(8,128)(2,1)S(1)}, bf16[48,3200]{1,0:T(8,128)(2,1)S(1)}, u32[]{:S(2)}, u32[]{:S(2)}) collective-permute-start(bf16[48,3200]{1,0:T(8,128)(2,1)S(1)} %slice.204), channel_id=1, source_target_pairs={{0,8},{4,12},{8,0},{12,4},{16,24},{20,28},{24,16},{28,20},{1,9},{5... | collective-permute-start | bytes 921608 | tf_op jit(solution)/shard_map/ppermute | solution.py:501
  41.7 15.0 %collective-permute-start.8 = (bf16[48,3200]{1,0:T(8,128)(2,1)S(1)}, bf16[48,3200]{1,0:T(8,128)(2,1)S(1)}, u32[]{:S(2)}, u32[]{:S(2)}) collective-permute-start(bf16[48,3200]{1,0:T(8,128)(2,1)S(1)} %slice.203), channel_id=1, source_target_pairs={{0,16},{4,20},{8,24},{12,28},{16,0},{20,4},{24,8},{28,12},{1,17},{... | collective-permute-start | bytes 921608 | tf_op jit(solution)/shard_map/ppermute | solution.py:501
  47.0 10.4 %collective-permute-start.5 = (bf16[96,3200]{1,0:T(8,128)(2,1)S(1)}, bf16[96,3200]{1,0:T(8,128)(2,1)S(1)}, u32[]{:S(2)}, u32[]{:S(2)}) collective-permute-start(bf16[96,3200]{1,0:T(8,128)(2,1)S(1)} %fusion.5.refs_0_), channel_id=1, source_target_pairs={{0,4},{4,0},{8,12},{12,8},{16,20},{20,16},{24,28},{28,24},{1,5},{5... | collective-permute-start | bytes 1843208 | tf_op jit(solution)/shard_map/ppermute | solution.py:501
  56.1 3.8 collective-permute-start.6
  56.1 3.8 collective-permute-start.7
  59.9 26.4 %collective-permute-start.15 = (bf16[4,384,768]{2,1,0:T(8,128)(2,1)}, bf16[4,384,768]{2,1,0:T(8,128)(2,1)S(1)}, u32[]{:S(2)}, u32[]{:S(2)}) collective-permute-start(bf16[4,384,768]{2,1,0:T(8,128)(2,1)} %refs_7_), channel_id=1, source_target_pairs={{0,4},{4,0},{8,12},{12,8},{16,20},{20,16},{24,28},{28,24},{1,5},{5... | collective-permute-start | bytes 7077896 | tf_op jit(solution)/shard_map/ppermute | solution.py:501
  60.1 27.8 %collective-permute-start.16 = (bf16[4,384,768]{2,1,0:T(8,128)(2,1)}, bf16[4,384,768]{2,1,0:T(8,128)(2,1)}, u32[]{:S(2)}, u32[]{:S(2)}) collective-permute-start(bf16[4,384,768]{2,1,0:T(8,128)(2,1)} %refs_9_), channel_id=1, source_target_pairs={{0,4},{4,0},{8,12},{12,8},{16,20},{20,16},{24,28},{28,24},{1,5},{5... | collective-permute-start | bytes 7077896 | tf_op jit(solution)/shard_map/ppermute | solution.py:501
  60.5 21.8 %collective-permute-start.21 = (bf16[4,144,768]{2,1,0:T(8,128)(2,1)S(1)}, bf16[4,144,768]{2,1,0:T(8,128)(2,1)}, u32[]{:S(2)}, u32[]{:S(2)}) collective-permute-start(bf16[4,144,768]{2,1,0:T(8,128)(2,1)S(1)} %pad_maximum_fusion.refs_1_), channel_id=1, source_target_pairs={{0,16},{4,20},{8,24},{12,28},{16,0},{20,4},{24,8},{28,12},{1,17},{... | collective-permute-start | bytes 2654216 | tf_op jit(solution)/shard_map/ppermute | solution.py:501
  61.0 22.7 %collective-permute-start.20 = (bf16[4,144,768]{2,1,0:T(8,128)(2,1)S(1)}, bf16[4,144,768]{2,1,0:T(8,128)(2,1)}, u32[]{:S(2)}, u32[]{:S(2)}) collective-permute-start(bf16[4,144,768]{2,1,0:T(8,128)(2,1)S(1)} %pad_maximum_fusion.refs_1_), channel_id=1, source_target_pairs={{0,8},{4,12},{8,0},{12,4},{16,24},{20,28},{24,16},{28,20},{1,9},{5... | collective-permute-start | bytes 2654216 | tf_op jit(solution)/shard_map/ppermute | solution.py:501
  76.4 41.0 %collective-permute-start.19 = (bf16[4,128,768]{2,1,0:T(8,128)(2,1)}, bf16[4,128,768]{2,1,0:T(8,128)(2,1)}, u32[]{:S(2)}, u32[]{:S(2)}) collective-permute-start(bf16[4,128,768]{2,1,0:T(8,128)(2,1)} %bitcast.98), channel_id=1, source_target_pairs={{0,24},{4,28},{8,16},{12,20},{16,8},{20,12},{24,0},{28,4},{1,25},{... | collective-permute-start | bytes 2359304 | tf_op jit(solution)/shard_map/ppermute | solution.py:501
  82.3 35.1 %collective-permute-start.18 = (bf16[4,128,768]{2,1,0:T(8,128)(2,1)}, bf16[4,128,768]{2,1,0:T(8,128)(2,1)}, u32[]{:S(2)}, u32[]{:S(2)}) collective-permute-start(bf16[4,128,768]{2,1,0:T(8,128)(2,1)} %bitcast.99), channel_id=1, source_target_pairs={{0,16},{4,20},{8,24},{12,28},{16,0},{20,4},{24,8},{28,12},{1,17},{... | collective-permute-start | bytes 2359304 | tf_op jit(solution)/shard_map/ppermute | solution.py:501
  83.7 33.7 %collective-permute-start.17 = (bf16[4,128,768]{2,1,0:T(8,128)(2,1)}, bf16[4,128,768]{2,1,0:T(8,128)(2,1)}, u32[]{:S(2)}, u32[]{:S(2)}) collective-permute-start(bf16[4,128,768]{2,1,0:T(8,128)(2,1)} %bitcast.100), channel_id=1, source_target_pairs={{0,8},{4,12},{8,0},{12,4},{16,24},{20,28},{24,16},{28,20},{1,9},{5... | collective-permute-start | bytes 2359304 | tf_op jit(solution)/shard_map/ppermute | solution.py:501
  86.4 39.5 %collective-permute-start.23 = (bf16[2,144,768]{2,1,0:T(8,128)(2,1)S(1)}, bf16[2,144,768]{2,1,0:T(8,128)(2,1)S(1)}, u32[]{:S(2)}, u32[]{:S(2)}) collective-permute-start(bf16[2,144,768]{2,1,0:T(8,128)(2,1)S(1)} %slice.267), channel_id=1, source_target_pairs={{0,8},{4,12},{8,0},{12,4},{16,24},{20,28},{24,16},{28,20},{1,9},{5... | collective-permute-start | bytes 1327112 | tf_op jit(solution)/shard_map/ppermute | solution.py:501
  87.9 38.7 %collective-permute-start.22 = (bf16[2,144,768]{2,1,0:T(8,128)(2,1)S(1)}, bf16[2,144,768]{2,1,0:T(8,128)(2,1)}, u32[]{:S(2)}, u32[]{:S(2)}) collective-permute-start(bf16[2,144,768]{2,1,0:T(8,128)(2,1)S(1)} %slice.266), channel_id=1, source_target_pairs={{0,16},{4,20},{8,24},{12,28},{16,0},{20,4},{24,8},{28,12},{1,17},{... | collective-permute-start | bytes 1327112 | tf_op jit(solution)/shard_map/ppermute | solution.py:501
  185.4 3.6 collective-permute-start.30
  185.5 26.4 %collective-permute-start.24 = (bf16[4,128,768]{2,1,0:T(8,128)(2,1)}, bf16[4,128,768]{2,1,0:T(8,128)(2,1)S(1)}, u32[]{:S(2)}, u32[]{:S(2)}) collective-permute-start(bf16[4,128,768]{2,1,0:T(8,128)(2,1)} %get-tuple-element.104), channel_id=1, source_target_pairs={{0,8},{4,12},{8,0},{12,4},{16,24},{20,28},{24,16},{28,20},{1,9},{5... | collective-permute-start | bytes 2359304 | tf_op jit(solution)/shard_map/ppermute | solution.py:501
  186.1 25.8 %collective-permute-start.25 = (bf16[4,128,768]{2,1,0:T(8,128)(2,1)}, bf16[4,128,768]{2,1,0:T(8,128)(2,1)S(1)}, u32[]{:S(2)}, u32[]{:S(2)}) collective-permute-start(bf16[4,128,768]{2,1,0:T(8,128)(2,1)} %get-tuple-element.105), channel_id=1, source_target_pairs={{0,16},{4,20},{8,24},{12,28},{16,0},{20,4},{24,8},{28,12},{1,17},{... | collective-permute-start | bytes 2359304 | tf_op jit(solution)/shard_map/ppermute | solution.py:501
  187.4 36.0 %collective-permute-start.26 = (bf16[4,128,768]{2,1,0:T(8,128)(2,1)}, bf16[4,128,768]{2,1,0:T(8,128)(2,1)}, u32[]{:S(2)}, u32[]{:S(2)}) collective-permute-start(bf16[4,128,768]{2,1,0:T(8,128)(2,1)} %get-tuple-element.106), channel_id=1, source_target_pairs={{0,24},{4,28},{8,16},{12,20},{16,8},{20,12},{24,0},{28,4},{1,25},{... | collective-permute-start | bytes 2359304 | tf_op jit(solution)/shard_map/ppermute | solution.py:501
  190.6 32.7 %collective-permute-start.31 = (bf16[1,2,384,768]{3,2,1,0:T(8,128)(2,1)S(1)}, bf16[1,2,384,768]{3,2,1,0:T(8,128)(2,1)S(1)}, u32[]{:S(2)}, u32[]{:S(2)}) collective-permute-start(bf16[1,2,384,768]{3,2,1,0:T(8,128)(2,1)S(1)} %add_convert_fusion.9), channel_id=1, source_target_pairs={{0,1},{3,2},{4,5},{7,6},{8,9},{11,10},{12,13},{15,14},{16,17},{19,... | collective-permute-start | bytes 3538952 | tf_op jit(solution)/shard_map/ppermute | solution.py:536
  223.7 6.5 %collective-permute-start.32 = (bf16[3,2,384,768]{3,2,1,0:T(8,128)(2,1)}, bf16[3,2,384,768]{3,2,1,0:T(8,128)(2,1)S(1)}, u32[]{:S(2)}, u32[]{:S(2)}) collective-permute-start(bf16[3,2,384,768]{3,2,1,0:T(8,128)(2,1)} %get-tuple-element.122), channel_id=1, source_target_pairs={{0,4},{4,0},{8,12},{12,8},{16,20},{20,16},{24,28},{28,24},{1,5},{5... | collective-permute-start | bytes 10616840 | tf_op jit(solution)/shard_map/ppermute | solution.py:501
  224.7 31.6 %collective-permute-start.33 = (bf16[1,2,384,768]{3,2,1,0:T(8,128)(2,1)S(1)}, bf16[1,2,384,768]{3,2,1,0:T(8,128)(2,1)S(1)}, u32[]{:S(2)}, u32[]{:S(2)}) collective-permute-start(bf16[1,2,384,768]{3,2,1,0:T(8,128)(2,1)S(1)} %add_convert_fusion.8), channel_id=1, source_target_pairs={{1,2},{2,1},{5,6},{6,5},{9,10},{10,9},{13,14},{14,13},{17,18},{18,... | collective-permute-start | bytes 3538952 | tf_op jit(solution)/shard_map/ppermute | solution.py:556
  232.7 27.4 %collective-permute-start.34 = (bf16[1,2,384,768]{3,2,1,0:T(8,128)(2,1)}, bf16[1,2,384,768]{3,2,1,0:T(8,128)(2,1)}, u32[]{:S(2)}, u32[]{:S(2)}) collective-permute-start(bf16[1,2,384,768]{3,2,1,0:T(8,128)(2,1)} %get-tuple-element.123), channel_id=1, source_target_pairs={{0,1},{3,2},{4,5},{7,6},{8,9},{11,10},{12,13},{15,14},{16,17},{19,... | collective-permute-start | bytes 3538952 | tf_op jit(solution)/shard_map/ppermute | solution.py:536
  260.2 20.8 %collective-permute-start.27 = (bf16[4,128,768]{2,1,0:T(8,128)(2,1)}, bf16[4,128,768]{2,1,0:T(8,128)(2,1)}, u32[]{:S(2)}, u32[]{:S(2)}) collective-permute-start(bf16[4,128,768]{2,1,0:T(8,128)(2,1)} %get-tuple-element.107), channel_id=1, source_target_pairs={{0,8},{4,12},{8,0},{12,4},{16,24},{20,28},{24,16},{28,20},{1,9},{5... | collective-permute-start | bytes 2359304 | tf_op jit(solution)/shard_map/ppermute | solution.py:501
  262.0 29.1 %collective-permute-start.28 = (bf16[4,128,768]{2,1,0:T(8,128)(2,1)}, bf16[4,128,768]{2,1,0:T(8,128)(2,1)}, u32[]{:S(2)}, u32[]{:S(2)}) collective-permute-start(bf16[4,128,768]{2,1,0:T(8,128)(2,1)} %get-tuple-element.108), channel_id=1, source_target_pairs={{0,16},{4,20},{8,24},{12,28},{16,0},{20,4},{24,8},{28,12},{1,17},{... | collective-permute-start | bytes 2359304 | tf_op jit(solution)/shard_map/ppermute | solution.py:501
  263.3 49.5 %collective-permute-start.35 = (bf16[1,2,384,768]{3,2,1,0:T(8,128)(2,1)}, bf16[1,2,384,768]{3,2,1,0:T(8,128)(2,1)}, u32[]{:S(2)}, u32[]{:S(2)}) collective-permute-start(bf16[1,2,384,768]{3,2,1,0:T(8,128)(2,1)} %get-tuple-element.141), channel_id=1, source_target_pairs={{0,1},{3,2},{4,5},{7,6},{8,9},{11,10},{12,13},{15,14},{16,17},{19,... | collective-permute-start | bytes 3538952 | tf_op jit(solution)/shard_map/ppermute | solution.py:536
  268.8 40.2 %collective-permute-start.29 = (bf16[4,128,768]{2,1,0:T(8,128)(2,1)}, bf16[4,128,768]{2,1,0:T(8,128)(2,1)}, u32[]{:S(2)}, u32[]{:S(2)}) collective-permute-start(bf16[4,128,768]{2,1,0:T(8,128)(2,1)} %get-tuple-element.109), channel_id=1, source_target_pairs={{0,24},{4,28},{8,16},{12,20},{16,8},{20,12},{24,0},{28,4},{1,25},{... | collective-permute-start | bytes 2359304 | tf_op jit(solution)/shard_map/ppermute | solution.py:501
  272.3 42.8 %collective-permute-start.38 = (bf16[1,2,384,768]{3,2,1,0:T(8,128)(2,1)}, bf16[1,2,384,768]{3,2,1,0:T(8,128)(2,1)}, u32[]{:S(2)}, u32[]{:S(2)}) collective-permute-start(bf16[1,2,384,768]{3,2,1,0:T(8,128)(2,1)} %add_convert_fusion.7), channel_id=1, source_target_pairs={{1,2},{2,1},{5,6},{6,5},{9,10},{10,9},{13,14},{14,13},{17,18},{18,... | collective-permute-start | bytes 3538952 | tf_op jit(solution)/shard_map/ppermute | solution.py:556
  309.4 30.3 %collective-permute-start.37 = (bf16[1,2,384,768]{3,2,1,0:T(8,128)(2,1)S(1)}, bf16[1,2,384,768]{3,2,1,0:T(8,128)(2,1)S(1)}, u32[]{:S(2)}, u32[]{:S(2)}) collective-permute-start(bf16[1,2,384,768]{3,2,1,0:T(8,128)(2,1)S(1)} %broadcast_select_fusion.4), channel_id=1, source_target_pairs={{0,1},{1,0},{2,3},{3,2},{4,5},{5,4},{6,7},{7,6},{8,9},{9,8},{10,11... | collective-permute-start | bytes 3538952 | tf_op jit(solution)/shard_map/ppermute | solution.py:545
  314.4 26.6 %collective-permute-start.36 = (bf16[1,2,384,768]{3,2,1,0:T(8,128)(2,1)S(1)}, bf16[1,2,384,768]{3,2,1,0:T(8,128)(2,1)S(1)}, u32[]{:S(2)}, u32[]{:S(2)}) collective-permute-start(bf16[1,2,384,768]{3,2,1,0:T(8,128)(2,1)S(1)} %add_convert_fusion.5), channel_id=1, source_target_pairs={{1,2},{2,1},{5,6},{6,5},{9,10},{10,9},{13,14},{14,13},{17,18},{18,... | collective-permute-start | bytes 3538952 | tf_op jit(solution)/shard_map/ppermute | solution.py:556
  317.0 44.1 %collective-permute-start.39 = (bf16[1,2,384,768]{3,2,1,0:T(8,128)(2,1)S(1)}, bf16[1,2,384,768]{3,2,1,0:T(8,128)(2,1)S(1)}, u32[]{:S(2)}, u32[]{:S(2)}) collective-permute-start(bf16[1,2,384,768]{3,2,1,0:T(8,128)(2,1)S(1)} %add_convert_fusion.4), channel_id=1, source_target_pairs={{1,0},{2,3},{5,4},{6,7},{9,8},{10,11},{13,12},{14,15},{17,16},{18,... | collective-permute-start | bytes 3538952 | tf_op jit(solution)/shard_map/ppermute | solution.py:563
  362.1 26.1 %collective-permute-start.45 = (bf16[1,2,384,768]{3,2,1,0:T(8,128)(2,1)S(1)}, bf16[1,2,384,768]{3,2,1,0:T(8,128)(2,1)}, u32[]{:S(2)}, u32[]{:S(2)}) collective-permute-start(bf16[1,2,384,768]{3,2,1,0:T(8,128)(2,1)S(1)} %add_convert_fusion.2), channel_id=1, source_target_pairs={{1,0},{2,3},{5,4},{6,7},{9,8},{10,11},{13,12},{14,15},{17,16},{18,... | collective-permute-start | bytes 3538952 | tf_op jit(solution)/shard_map/ppermute | solution.py:563
  363.4 26.3 %collective-permute-start.41 = (bf16[1,2,384,768]{3,2,1,0:T(8,128)(2,1)}, bf16[1,2,384,768]{3,2,1,0:T(8,128)(2,1)}, u32[]{:S(2)}, u32[]{:S(2)}) collective-permute-start(bf16[1,2,384,768]{3,2,1,0:T(8,128)(2,1)} %add_convert_fusion.3), channel_id=1, source_target_pairs={{1,2},{2,1},{5,6},{6,5},{9,10},{10,9},{13,14},{14,13},{17,18},{18,... | collective-permute-start | bytes 3538952 | tf_op jit(solution)/shard_map/ppermute | solution.py:556
  365.8 27.4 %collective-permute-start.40 = (bf16[96,3200]{1,0:T(8,128)(2,1)}, bf16[96,3200]{1,0:T(8,128)(2,1)S(1)}, u32[]{:S(2)}, u32[]{:S(2)}) collective-permute-start(bf16[96,3200]{1,0:T(8,128)(2,1)} %reduce-scatter.2.cloned.1.call-done), channel_id=1, source_target_pairs={{0,1},{3,2},{4,5},{7,6},{8,9},{11,10},{12,13},{15,14},{16,17},{19,... | collective-permute-start | bytes 1843208 | tf_op jit(solution)/shard_map/ppermute | solution.py:536
  391.7 48.5 %collective-permute-start.46 = (bf16[1,2,384,768]{3,2,1,0:T(8,128)(2,1)S(1)}, bf16[1,2,384,768]{3,2,1,0:T(8,128)(2,1)S(1)}, u32[]{:S(2)}, u32[]{:S(2)}) collective-permute-start(bf16[1,2,384,768]{3,2,1,0:T(8,128)(2,1)S(1)} %add_convert_fusion.1), channel_id=1, source_target_pairs={{1,0},{2,3},{5,4},{6,7},{9,8},{10,11},{13,12},{14,15},{17,16},{18,... | collective-permute-start | bytes 3538952 | tf_op jit(solution)/shard_map/ppermute | solution.py:563
  393.3 11.9 %collective-permute-start.47 = (bf16[96,3200]{1,0:T(8,128)(2,1)S(1)}, bf16[96,3200]{1,0:T(8,128)(2,1)S(1)}, u32[]{:S(2)}, u32[]{:S(2)}) collective-permute-start(bf16[96,3200]{1,0:T(8,128)(2,1)S(1)} %add_convert_fusion.11), channel_id=1, source_target_pairs={{1,2},{2,1},{5,6},{6,5},{9,10},{10,9},{13,14},{14,13},{17,18},{18,... | collective-permute-start | bytes 1843208 | tf_op jit(solution)/shard_map/ppermute | solution.py:556
  397.3 51.4 %collective-permute-start.42 = (bf16[2,2,64,768]{3,2,1,0:T(8,128)(2,1)S(1)}, bf16[2,2,64,768]{3,2,1,0:T(8,128)(2,1)S(1)}, u32[]{:S(2)}, u32[]{:S(2)}) collective-permute-start(bf16[2,2,64,768]{3,2,1,0:T(8,128)(2,1)S(1)} %pad_maximum_fusion.5), channel_id=1, source_target_pairs={{0,1},{1,0},{2,3},{3,2},{4,5},{5,4},{6,7},{7,6},{8,9},{9,8},{10,11... | collective-permute-start | bytes 1179656 | tf_op jit(solution)/shard_map/ppermute | solution.py:511
  402.5 46.2 %collective-permute-start.43 = (bf16[2,2,64,768]{3,2,1,0:T(8,128)(2,1)S(1)}, bf16[2,2,64,768]{3,2,1,0:T(8,128)(2,1)S(1)}, u32[]{:S(2)}, u32[]{:S(2)}) collective-permute-start(bf16[2,2,64,768]{3,2,1,0:T(8,128)(2,1)S(1)} %pad_maximum_fusion.6), channel_id=1, source_target_pairs={{0,2},{1,3},{2,0},{3,1},{4,6},{5,7},{6,4},{7,5},{8,10},{9,11},{10,... | collective-permute-start | bytes 1179656 | tf_op jit(solution)/shard_map/ppermute | solution.py:511
  403.7 45.0 %collective-permute-start.44 = (bf16[2,2,64,768]{3,2,1,0:T(8,128)(2,1)S(1)}, bf16[2,2,64,768]{3,2,1,0:T(8,128)(2,1)S(1)}, u32[]{:S(2)}, u32[]{:S(2)}) collective-permute-start(bf16[2,2,64,768]{3,2,1,0:T(8,128)(2,1)S(1)} %pad_maximum_fusion.7), channel_id=1, source_target_pairs={{0,3},{1,2},{2,1},{3,0},{4,7},{5,6},{6,5},{7,4},{8,11},{9,10},{10,... | collective-permute-start | bytes 1179656 | tf_op jit(solution)/shard_map/ppermute | solution.py:511
  405.4 50.8 %collective-permute-start.48 = (bf16[96,3200]{1,0:T(8,128)(2,1)S(1)}, bf16[96,3200]{1,0:T(8,128)(2,1)S(1)}, u32[]{:S(2)}, u32[]{:S(2)}) collective-permute-start(bf16[96,3200]{1,0:T(8,128)(2,1)S(1)} %add_convert_fusion.10), channel_id=1, source_target_pairs={{1,0},{2,3},{5,4},{6,7},{9,8},{10,11},{13,12},{14,15},{17,16},{18,... | collective-permute-start | bytes 1843208 | tf_op jit(solution)/shard_map/ppermute | solution.py:563
  (39 other events, 377.1 us)
Sparse Core Ops, SparseCore 0:
  260.3 66.8 reduce-scatter.1
